TPU v7x, 32 devices: a whole 2x2x4 slice. The times are simulated.
32 devices in a mesh: group: 2 (over y), freq: 4 (over z), shot: 2 (over x), half: 2 (over core).
Axes of the slice: x: 2, y: 2, z: 4, core: 2. Of those that a mesh axis runs over, the one named last changes fastest.
Arguments:
- records: bfloat16 [8, 64, 128, 512], P(('group', 'shot'), 'half', 'freq'), parts along dimension 0, may hold values from -6 to 6
- source_pattern: bfloat16 [8, 64, 128], P(('group', 'shot'), 'half'), parts along dimension 0, may hold values from -6 to 6
- wavelet: float32 [256, 2], replicated, may hold values from -6 to 6
- filters: bfloat16 [2, 2, 13, 13, 256], replicated, may hold values from -0.3125 to 0.3125
- vel_table: float32 [64], replicated, may hold values from 0 to 1
- vel_index: int32 [4, 64, 128], P('group', 'half'), parts along dimension 0, may hold values from 0 to 63
- freq_plan: int32 [4, 6], replicated, may hold values from 0 to 255, as said below
- counts: int32 [4], replicated, may hold values from 1 to 6, 12 in all
Outputs:
- image: float32 [2, 32, 4, 128], P('half', 'freq', 'group'), parts along dimension 2
There are 2 independent parts, one for each index of `group`. A program takes and returns all parts, laid end to end along the dimension named above; an argument that names none is the same for every part. Nothing has to cross between parts.
Inputs may be any that keep to these rules, and one draw needn't show every extreme that they name: `freq_plan`: entries are distinct bins; 0 and 255 both appear. `counts`: they sum to 12; the largest is exactly 6.
All inputs are finite; a program needn't handle non-finite values.
Results may differ from a plain program's by a relative error of at most 0.0069.
Values may be sent and summed in bfloat16 or wider, within the bound.
No kernel may reach another device: no remote copies, remote signals or barrier semaphores. Data moves between devices by JAX's collectives and lax.ppermute only.
A program may use at most 64 MiB of HBM per device.

v0:
```python
import functools
import math

import jax
import jax.numpy as jnp
from jax import lax
from jax.sharding import PartitionSpec as P

SHOT_DEV = 2
NT = 512
FPD = 3
DEPTH = 2
TAPS = 13
NREF = 2


def padded_2(block, sides, width):
    for axis, dim in sides:
        count = lax.axis_size(axis)
        forward = [(i, i + 1) for i in range(count - 1)]
        backward = [(target, source) for source, target in forward]
        low = lax.ppermute(
            lax.slice_in_dim(block, block.shape[dim] - width, None, axis=dim), axis, forward
        )
        high = lax.ppermute(lax.slice_in_dim(block, 0, width, axis=dim), axis, backward)
        block = jnp.concatenate([low, block, high], axis=dim)
    return block


def slot_bins(freq_plan, counts, groups):
    run_ends = jnp.cumsum(counts)
    starts = run_ends - counts
    holders = jnp.arange(groups, dtype=jnp.int32)
    width_cap = freq_plan.shape[1]
    wanted = jnp.arange(groups * FPD, dtype=jnp.int32).reshape(groups, FPD)
    holder = jnp.sum((run_ends[None, None, :] <= wanted[:, :, None]).astype(jnp.int32), axis=-1)
    chosen = holder[:, :, None] == holders[None, None, :]
    first_slot = jnp.sum(jnp.where(chosen, starts[None, None, :], 0), axis=-1)
    offset = wanted - first_slot
    places = jnp.arange(width_cap, dtype=jnp.int32)
    picked = chosen[:, :, :, None] & (offset[:, :, None, None] == places[None, None, None, :])
    bin_ids = jnp.sum(jnp.where(picked, freq_plan[None, None, :, :], 0), axis=(2, 3))
    in_use = jnp.ones(bin_ids.shape, jnp.float32)
    return (bin_ids, in_use)


def product(left, right):
    return jnp.einsum("fnyk,kj->fnyj", left, right, preferred_element_type=jnp.float32)


def advance(inputs, blend_now, shifts):
    padded, filter_taps = inputs
    half_taps = TAPS // 2
    row_count = padded.shape[3] - 2 * half_taps
    col_count = padded.shape[4]
    band_mat = jnp.einsum(
        "rcyk,kab->cyarb", filter_taps, shifts, preferred_element_type=jnp.bfloat16
    )
    band_mat = band_mat.reshape(2, TAPS * col_count, NREF * col_count)
    stacked = jnp.concatenate(
        [padded[:, :, :, row_shift : row_shift + row_count, :] for row_shift in range(TAPS)],
        axis=-1,
    )
    real_part = stacked[:, :, 0]
    imag_part = stacked[:, :, 1]
    out_real = product(real_part, band_mat[0]) - product(imag_part, band_mat[1])
    out_imag = product(real_part, band_mat[1]) + product(imag_part, band_mat[0])
    split_shape = out_real.shape[:3] + (NREF, col_count)
    out_real = out_real.reshape(split_shape)
    out_imag = out_imag.reshape(split_shape)
    new_real = out_real[..., 0, :] + blend_now * (out_real[..., 1, :] - out_real[..., 0, :])
    new_imag = out_imag[..., 0, :] + blend_now * (out_imag[..., 1, :] - out_imag[..., 0, :])
    updated = jnp.stack([new_real, new_imag], axis=2).astype(jnp.bfloat16)
    as_float = updated.astype(jnp.float32)
    image_slot = jnp.sum(
        as_float[0, :, 0] * as_float[1, :, 0] + as_float[0, :, 1] * as_float[1, :, 1], axis=0
    )
    return (updated, image_slot)


def body(records, source_pattern, wavelet, filters, vel_table, vel_index, freq_plan, counts):
    groups = lax.axis_size("freq")
    freq_index = lax.axis_index("freq")
    half_taps = TAPS // 2
    bin_ids, in_use = slot_bins(freq_plan, counts, groups)
    slot_count = bin_ids.shape[1]
    sample = jnp.arange(NT, dtype=jnp.int32)
    phases = bin_ids[None, :, :] * sample[:, None, None] % NT
    angles = phases.astype(jnp.float32) * (2.0 * math.pi / NT)
    dft_scale = in_use[None] * (1.0 / math.sqrt(NT))
    dft_table = jnp.stack(
        [jnp.cos(angles) * dft_scale, -jnp.sin(angles) * dft_scale], axis=-1
    ).astype(jnp.bfloat16)
    spectra = jnp.einsum(
        "tdsc,nyxt->dsncyx", dft_table, records, preferred_element_type=jnp.float32
    )
    spectra = lax.all_to_all(
        spectra.astype(jnp.bfloat16), "freq", split_axis=0, concat_axis=5, tiled=True
    )
    receiver = spectra[0]
    own_pick = (jnp.arange(groups, dtype=jnp.int32) == freq_index)[:, None]
    own_bins = jnp.sum(jnp.where(own_pick, bin_ids, 0), axis=0)
    bin_total = filters.shape[-1]
    bin_hot = (own_bins[:, None] == jnp.arange(bin_total, dtype=jnp.int32)[None, :]).astype(
        jnp.float32
    )
    wavelet_bins = jnp.dot(bin_hot, wavelet, precision=lax.Precision.HIGHEST)
    filter_taps = jnp.einsum(
        "kb,sb->sk",
        filters.reshape(-1, bin_total),
        bin_hot.astype(jnp.bfloat16),
        preferred_element_type=jnp.float32,
    )
    filter_taps = filter_taps.astype(jnp.bfloat16).reshape((slot_count,) + filters.shape[:-1])
    pattern = source_pattern.astype(jnp.float32)
    source = (pattern[None, :, None] * wavelet_bins[:, None, :, None, None]).astype(jnp.bfloat16)
    fields = jnp.stack([source, receiver], axis=1)
    class_hot = (
        jnp.arange(vel_table.shape[0], dtype=jnp.int32)[:, None] == vel_index.reshape(1, -1)
    ).astype(jnp.float32)
    blends = jnp.dot(vel_table[None, :], class_hot, precision=lax.Precision.HIGHEST).reshape(
        vel_index.shape
    )
    col_count = fields.shape[-1]
    tap_axis = jnp.arange(TAPS, dtype=jnp.int32)
    columns = jnp.arange(col_count, dtype=jnp.int32)
    shifts = (
        columns[None, :, None] - columns[None, None, :] + half_taps == tap_axis[:, None, None]
    ).astype(jnp.bfloat16)
    images = []
    for depth_step in range(DEPTH):
        padded = padded_2(fields, (("half", 4),), half_taps)
        stepper = functools.partial(advance, blend_now=blends[depth_step], shifts=shifts)
        fields, slot_images = lax.map(stepper, (padded, filter_taps))
        images.append(jnp.sum(slot_images, axis=0))
    image_scale = 1.0 / math.sqrt(FPD * groups * SHOT_DEV * lax.axis_size("shot"))
    partial_value = jnp.stack(images, axis=1) * image_scale
    share_part = lax.psum_scatter(partial_value, "freq", scatter_dimension=0, tiled=True)
    summed = lax.psum(share_part, "shot")
    return summed.reshape((1, partial_value.shape[0] // groups) + partial_value.shape[1:])


def solution(mesh):
    return jax.shard_map(
        body,
        mesh=mesh,
        in_specs=(
            P(("group", "shot"), "half", "freq", None),
            P(("group", "shot"), "half", None),
            P(),
            P(),
            P(),
            P("group", "half", None),
            P(),
            P(),
        ),
        out_specs=P("half", "freq", "group", None),
        check_vma=False,
    )
```

profile of v0, /device:TPU:0, one launch (start us, length us, event | category | flops | bytes accessed | tf_op | source)
XLA Modules:
  0.0 173.7 jit_solution(3777272798241651773)
XLA Ops:
  3.8 1.6 fusion.40
  6.5 6.3 %all-to-all-start = ((bf16[4,2,6144]{2,1,0:T(2,128)(2,1)}), bf16[4,2,6144]{2,1,0:T(2,128)(2,1)S(1)}, u32[]{:S(2)}, u32[]{:S(2)}) async-start(bf16[4,2,6144]{2,1,0:T(2,128)(2,1)} %reshape.411), calls=%async_computation | async-start | bytes 196608 | tf_op jit(solution)/shard_map/all_to_all | solution.py:97
  14.4 4.2 %all-to-all-done = bf16[4,2,6144]{2,1,0:T(2,128)(2,1)S(1)} async-done(((bf16[4,2,6144]{2,1,0:T(2,128)(2,1)}), bf16[4,2,6144]{2,1,0:T(2,128)(2,1)S(1)}, u32[]{:S(2)}, u32[]{:S(2)}) %all-to-all-start) | async-done | bytes 98336 | tf_op jit(solution)/shard_map/all_to_all | solution.py:97
  20.8 3.2 %collective-permute-start = (bf16[3,2,2,2,6,128]{5,4,3,2,0,1:T(8,128)(2,1)S(1)}, bf16[3,2,2,2,6,128]{5,4,3,2,0,1:T(8,128)(2,1)S(1)}, u32[]{:S(2)}, u32[]{:S(2)}) collective-permute-start(bf16[3,2,2,2,6,128]{5,4,3,2,0,1:T(8,128)(2,1)S(1)} %get-tuple-element.170), channel_id=1, source_target_pairs={{0,1},{2,3},{4,5},{6,7},{8,9},{10,11},{12,13},{14,15},{16,17},{18,... | collective-permute-start | bytes 110600 | tf_op jit(solution)/shard_map/ppermute | solution.py:22
  25.5 59.6 %while.24 = (s32[]{:T(128)}, bf16[3,2,2,2,32,128]{5,4,2,1,3,0:T(8,128)(2,1)}, f32[3,32,128]{2,1,0:T(8,128)S(1)}, bf16[3,2,2,2,44,128]{5,4,3,2,0,1:T(8,128)(2,1)}...) while((s32[]{:T(128)}, ...), condition=%wide.region_7.8_spmd.clone, body=%wide.region_5.7_spmd.clone.sunk | while | flops 459206656 | bytes 28516516 | solution.py:134
  27.5 1.8 %copy.109 = bf16[1,13,128,2,128]{4,3,2,1,0:T(2,128)(2,1)} copy(bf16[1,13,128,2,128]{4,1,2,0,3:T(8,128)(2,1)S(1)} %get-tuple-element.266) | data formatting | bytes 1703936 | tf_op jit(solution)/shard_map/while/body/eval_jaxpr/slice | solution.py:66
  29.4 2.5 %reshape.421 = bf16[1664,256,1,1]{1,0,2,3:T(8,128)(2,1)S(1)} reshape(bf16[1,13,128,2,128]{4,3,2,1,0:T(2,128)(2,1)} %copy.109) | data formatting | bytes 1703936 | tf_op jit(solution)/shard_map/while/body/eval_jaxpr/squeeze | solution.py:66
  34.6 1.9 %copy.110 = bf16[1,13,128,2,128]{4,3,2,1,0:T(2,128)(2,1)} copy(bf16[1,13,128,2,128]{4,1,2,0,3:T(8,128)(2,1)S(1)} %copy-done.1) | data formatting | bytes 1703936 | tf_op jit(solution)/shard_map/while/body/eval_jaxpr/slice | solution.py:66
  36.5 3.3 %reshape.422 = bf16[1664,256,1,1]{1,0,2,3:T(8,128)(2,1)} reshape(bf16[1,13,128,2,128]{4,3,2,1,0:T(2,128)(2,1)} %copy.110) | data formatting | bytes 1703936 | tf_op jit(solution)/shard_map/while/body/eval_jaxpr/squeeze | solution.py:66
  39.8 1.6 convolution_subtract_fusion.4
  41.6 1.6 fusion.97
  47.4 1.8 %copy.109 = bf16[1,13,128,2,128]{4,3,2,1,0:T(2,128)(2,1)} copy(bf16[1,13,128,2,128]{4,1,2,0,3:T(8,128)(2,1)S(1)} %get-tuple-element.266) | data formatting | bytes 1703936 | tf_op jit(solution)/shard_map/while/body/eval_jaxpr/slice | solution.py:66
  49.2 2.5 %reshape.421 = bf16[1664,256,1,1]{1,0,2,3:T(8,128)(2,1)S(1)} reshape(bf16[1,13,128,2,128]{4,3,2,1,0:T(2,128)(2,1)} %copy.109) | data formatting | bytes 1703936 | tf_op jit(solution)/shard_map/while/body/eval_jaxpr/squeeze | solution.py:66
  54.5 1.9 %copy.110 = bf16[1,13,128,2,128]{4,3,2,1,0:T(2,128)(2,1)} copy(bf16[1,13,128,2,128]{4,1,2,0,3:T(8,128)(2,1)S(1)} %copy-done.1) | data formatting | bytes 1703936 | tf_op jit(solution)/shard_map/while/body/eval_jaxpr/slice | solution.py:66
  56.4 3.3 %reshape.422 = bf16[1664,256,1,1]{1,0,2,3:T(8,128)(2,1)} reshape(bf16[1,13,128,2,128]{4,3,2,1,0:T(2,128)(2,1)} %copy.110) | data formatting | bytes 1703936 | tf_op jit(solution)/shard_map/while/body/eval_jaxpr/squeeze | solution.py:66
  59.6 1.6 convolution_subtract_fusion.4
  61.4 1.6 fusion.97
  67.3 1.8 %copy.109 = bf16[1,13,128,2,128]{4,3,2,1,0:T(2,128)(2,1)} copy(bf16[1,13,128,2,128]{4,1,2,0,3:T(8,128)(2,1)S(1)} %get-tuple-element.266) | data formatting | bytes 1703936 | tf_op jit(solution)/shard_map/while/body/eval_jaxpr/slice | solution.py:66
  69.1 2.5 %reshape.421 = bf16[1664,256,1,1]{1,0,2,3:T(8,128)(2,1)S(1)} reshape(bf16[1,13,128,2,128]{4,3,2,1,0:T(2,128)(2,1)} %copy.109) | data formatting | bytes 1703936 | tf_op jit(solution)/shard_map/while/body/eval_jaxpr/squeeze | solution.py:66
  74.4 1.9 %copy.110 = bf16[1,13,128,2,128]{4,3,2,1,0:T(2,128)(2,1)} copy(bf16[1,13,128,2,128]{4,1,2,0,3:T(8,128)(2,1)S(1)} %copy-done.1) | data formatting | bytes 1703936 | tf_op jit(solution)/shard_map/while/body/eval_jaxpr/slice | solution.py:66
  76.2 3.3 %reshape.422 = bf16[1664,256,1,1]{1,0,2,3:T(8,128)(2,1)} reshape(bf16[1,13,128,2,128]{4,3,2,1,0:T(2,128)(2,1)} %copy.110) | data formatting | bytes 1703936 | tf_op jit(solution)/shard_map/while/body/eval_jaxpr/squeeze | solution.py:66
  79.5 1.6 convolution_subtract_fusion.4
  81.3 1.6 fusion.97
  87.2 3.3 %collective-permute-start.2 = (bf16[3,2,2,2,6,128]{5,4,2,1,3,0:T(8,128)(2,1)S(1)}, bf16[3,2,2,2,6,128]{5,4,2,1,3,0:T(8,128)(2,1)S(1)}, u32[]{:S(2)}, u32[]{:S(2)}) collective-permute-start(bf16[3,2,2,2,6,128]{5,4,2,1,3,0:T(8,128)(2,1)S(1)} %get-tuple-element.168), channel_id=1, source_target_pairs={{0,1},{2,3},{4,5},{6,7},{8,9},{10,11},{12,13},{14,15},{16,17},{18,... | collective-permute-start | bytes 110600 | tf_op jit(solution)/shard_map/ppermute | solution.py:22
  91.8 1.7 %pad_maximum_fusion.1 = bf16[3,2,2,2,44,128]{5,4,2,1,3,0:T(8,128)(2,1)} fusion(bf16[3,2,2,2,6,128]{5,4,2,1,3,0:T(8,128)(2,1)S(1)} %collective-permute-done.3, bf16[3,2,2,2,32,128]{5,4,2,1,3,0:T(8,128)(2,1)} %get-tuple-element.76, bf16[3,2,2,2,6,128]{5,4,2,1,3,0:T(8,128)(2,1)S(1)} %collective-permute-done.2), kind=kLoop, calls=%fused_computation.93 | loop fusion | flops 811008 | bytes 540672 | tf_op jit(solution)/shard_map/concatenate | solution.py:26
  93.6 57.7 %while.25 = (s32[]{:T(128)}, f32[3,32,128]{2,1,0:T(8,128)S(1)}, bf16[3,2,2,2,44,128]{5,4,2,1,3,0:T(8,128)(2,1)}, bf16[3,2,2,13,13]{4,3,2,1,0:T(8,128)(2,1)S(1)},...) while((s32[]{:T(128)}, f32[3,32,128]{2,1,0:T(8,128)S(1)}, ...), condition=%wide.region_11.12_spmd.clone, body=%wide.region_9.11_spmd.clone.sunk | while | flops 459075584 | bytes 28377240 | solution.py:134
  94.3 1.4 fusion.106
  95.6 1.8 %copy.111 = bf16[1,13,128,2,128]{4,3,2,1,0:T(2,128)(2,1)} copy(bf16[1,13,128,2,128]{4,1,2,0,3:T(8,128)(2,1)S(1)} %get-tuple-element.280) | data formatting | bytes 1703936 | tf_op jit(solution)/shard_map/while/body/eval_jaxpr/slice | solution.py:66
  97.5 2.5 %reshape.425 = bf16[1664,256,1,1]{1,0,2,3:T(8,128)(2,1)S(1)} reshape(bf16[1,13,128,2,128]{4,3,2,1,0:T(2,128)(2,1)} %copy.111) | data formatting | bytes 1703936 | tf_op jit(solution)/shard_map/while/body/eval_jaxpr/squeeze | solution.py:66
  102.7 1.9 %copy.112 = bf16[1,13,128,2,128]{4,3,2,1,0:T(2,128)(2,1)} copy(bf16[1,13,128,2,128]{4,1,2,0,3:T(8,128)(2,1)S(1)} %copy-done.2) | data formatting | bytes 1703936 | tf_op jit(solution)/shard_map/while/body/eval_jaxpr/slice | solution.py:66
  104.6 3.3 %reshape.426 = bf16[1664,256,1,1]{1,0,2,3:T(8,128)(2,1)} reshape(bf16[1,13,128,2,128]{4,3,2,1,0:T(2,128)(2,1)} %copy.112) | data formatting | bytes 1703936 | tf_op jit(solution)/shard_map/while/body/eval_jaxpr/squeeze | solution.py:66
  107.9 1.6 convolution_subtract_fusion.5
  109.6 1.6 fusion.109
  113.5 1.4 fusion.106
  114.9 1.8 %copy.111 = bf16[1,13,128,2,128]{4,3,2,1,0:T(2,128)(2,1)} copy(bf16[1,13,128,2,128]{4,1,2,0,3:T(8,128)(2,1)S(1)} %get-tuple-element.280) | data formatting | bytes 1703936 | tf_op jit(solution)/shard_map/while/body/eval_jaxpr/slice | solution.py:66
  116.7 2.5 %reshape.425 = bf16[1664,256,1,1]{1,0,2,3:T(8,128)(2,1)S(1)} reshape(bf16[1,13,128,2,128]{4,3,2,1,0:T(2,128)(2,1)} %copy.111) | data formatting | bytes 1703936 | tf_op jit(solution)/shard_map/while/body/eval_jaxpr/squeeze | solution.py:66
  122.0 1.9 %copy.112 = bf16[1,13,128,2,128]{4,3,2,1,0:T(2,128)(2,1)} copy(bf16[1,13,128,2,128]{4,1,2,0,3:T(8,128)(2,1)S(1)} %copy-done.2) | data formatting | bytes 1703936 | tf_op jit(solution)/shard_map/while/body/eval_jaxpr/slice | solution.py:66
  123.8 3.3 %reshape.426 = bf16[1664,256,1,1]{1,0,2,3:T(8,128)(2,1)} reshape(bf16[1,13,128,2,128]{4,3,2,1,0:T(2,128)(2,1)} %copy.112) | data formatting | bytes 1703936 | tf_op jit(solution)/shard_map/while/body/eval_jaxpr/squeeze | solution.py:66
  127.1 1.6 convolution_subtract_fusion.5
  128.9 1.6 fusion.109
  134.1 1.8 %copy.111 = bf16[1,13,128,2,128]{4,3,2,1,0:T(2,128)(2,1)} copy(bf16[1,13,128,2,128]{4,1,2,0,3:T(8,128)(2,1)S(1)} %get-tuple-element.280) | data formatting | bytes 1703936 | tf_op jit(solution)/shard_map/while/body/eval_jaxpr/slice | solution.py:66
  135.9 2.5 %reshape.425 = bf16[1664,256,1,1]{1,0,2,3:T(8,128)(2,1)S(1)} reshape(bf16[1,13,128,2,128]{4,3,2,1,0:T(2,128)(2,1)} %copy.111) | data formatting | bytes 1703936 | tf_op jit(solution)/shard_map/while/body/eval_jaxpr/squeeze | solution.py:66
  141.2 1.9 %copy.112 = bf16[1,13,128,2,128]{4,3,2,1,0:T(2,128)(2,1)} copy(bf16[1,13,128,2,128]{4,1,2,0,3:T(8,128)(2,1)S(1)} %copy-done.2) | data formatting | bytes 1703936 | tf_op jit(solution)/shard_map/while/body/eval_jaxpr/slice | solution.py:66
  143.0 3.3 %reshape.426 = bf16[1664,256,1,1]{1,0,2,3:T(8,128)(2,1)} reshape(bf16[1,13,128,2,128]{4,3,2,1,0:T(2,128)(2,1)} %copy.112) | data formatting | bytes 1703936 | tf_op jit(solution)/shard_map/while/body/eval_jaxpr/squeeze | solution.py:66
  146.3 1.6 convolution_subtract_fusion.5
  148.1 1.6 fusion.109
  151.3 16.8 %all-reduce = f32[32,2,128]{2,1,0:T(2,128)S(1)} all-reduce(f32[32,2,128]{2,1,0:T(2,128)S(1)} %maximum_multiply_fusion), channel_id=2, replica_groups=mesh['group'=2,'freq'=4,'shot'=2,'half'=2] {'freq'}, use_global_device_ids=true, to_apply=%region_13.14.clone | all-reduce | flops 8192 | bytes 65536
  168.1 5.6 %psum.7 = f32[1,8,2,128]{3,2,1,0:T(2,128)} all-reduce(f32[1,8,2,128]{3,2,1,0:T(2,128)S(1)} %dynamic-slice_bitcast_fusion.1), channel_id=1, replica_groups=mesh['group'=2,'freq'=4,'shot'=2,'half'=2] {'shot'}, use_global_device_ids=true, to_apply=%region_14.15 | all-reduce | flops 2048 | bytes 16384 | tf_op jit(solution)/shard_map/psum | solution.py:139
  (242 shorter events, 50.2 us)
Async XLA Ops:
  0.0 3.7 %copy-start = (bf16[2,32,32,512]{3,2,1,0:T(8,128)(2,1)S(1)}, bf16[2,32,32,512]{3,2,1,0:T(8,128)(2,1)}, u32[]{:S(2)}) copy-start(bf16[2,32,32,512]{3,2,1,0:T(8,128)(2,1)} %param.12) | copy-start | bytes 6291460
  3.7 9.2 %copy-start.6 = (bf16[2,32,128]{2,1,0:T(8,128)(2,1)S(1)}, bf16[2,32,128]{2,1,0:T(8,128)(2,1)}, u32[]{:S(2)}) copy-start(bf16[2,32,128]{2,1,0:T(8,128)(2,1)} %param.13) | copy-start | bytes 49156
  3.7 9.2 %copy-start.5 = (bf16[2,2,13,13,256]{4,1,3,2,0:T(2,128)(2,1)S(1)}, bf16[2,2,13,13,256]{4,1,3,2,0:T(2,128)(2,1)}, u32[]{:S(2)}) copy-start(bf16[2,2,13,13,256]{4,1,3,2,0:T(2,128)(2,1)} %param.15) | copy-start | bytes 1038340
  5.3 7.8 %copy-start.8 = (f32[256,2]{0,1:T(2,128)S(1)}, f32[256,2]{0,1:T(2,128)}, u32[]{:S(2)}) copy-start(f32[256,2]{0,1:T(2,128)} %param.14) | copy-start | bytes 6148
  5.3 8.3 %copy-start.7 = (s32[2,32,128]{2,1,0:T(8,128)S(1)}, s32[2,32,128]{2,1,0:T(8,128)}, u32[]{:S(2)}) copy-start(s32[2,32,128]{2,1,0:T(8,128)} %param.17) | copy-start | bytes 98308
  5.4 8.3 %copy-start.9 = (f32[64]{0:T(128)S(1)}, f32[64]{0:T(128)}, u32[]{:S(2)}) copy-start(f32[64]{0:T(128)} %param.16) | copy-start | bytes 772
  6.5 12.2 %all-to-all-start = ((bf16[4,2,6144]{2,1,0:T(2,128)(2,1)}), bf16[4,2,6144]{2,1,0:T(2,128)(2,1)S(1)}, u32[]{:S(2)}, u32[]{:S(2)}) async-start(bf16[4,2,6144]{2,1,0:T(2,128)(2,1)} %reshape.411), calls=%async_computation | async-start | bytes 196608 | tf_op jit(solution)/shard_map/all_to_all | solution.py:97
  19.5 4.7 %collective-permute-start.1 = (bf16[3,2,2,2,6,128]{5,4,3,2,0,1:T(8,128)(2,1)S(1)}, bf16[3,2,2,2,6,128]{5,4,3,2,0,1:T(8,128)(2,1)S(1)}, u32[]{:S(2)}, u32[]{:S(2)}) collective-permute-start(bf16[3,2,2,2,6,128]{5,4,3,2,0,1:T(8,128)(2,1)S(1)} %get-tuple-element.171), channel_id=1, source_target_pairs={{1,0},{3,2},{5,4},{7,6},{9,8},{11,10},{13,12},{15,14},{17,16},{19,... | collective-permute-start | bytes 110600 | tf_op jit(solution)/shard_map/ppermute | solution.py:25
  20.8 3.9 %collective-permute-start = (bf16[3,2,2,2,6,128]{5,4,3,2,0,1:T(8,128)(2,1)S(1)}, bf16[3,2,2,2,6,128]{5,4,3,2,0,1:T(8,128)(2,1)S(1)}, u32[]{:S(2)}, u32[]{:S(2)}) collective-permute-start(bf16[3,2,2,2,6,128]{5,4,3,2,0,1:T(8,128)(2,1)S(1)} %get-tuple-element.170), channel_id=1, source_target_pairs={{0,1},{2,3},{4,5},{6,7},{8,9},{10,11},{12,13},{14,15},{16,17},{18,... | collective-permute-start | bytes 110600 | tf_op jit(solution)/shard_map/ppermute | solution.py:22
  25.5 65.0 %copy-start.10 = (u32[32]{0:T(128)S(1)}, u32[32]{0:T(128)}, u32[]{:S(2)}) copy-start(u32[32]{0:T(128)} %constant.69) | copy-start | bytes 388
  31.9 2.7 %copy-start.1 = (bf16[1,13,128,2,128]{4,1,2,0,3:T(8,128)(2,1)S(1)}, bf16[1,13,128,2,128]{4,1,2,0,3:T(8,128)(2,1)}, u32[]{:S(2)}) copy-start(bf16[1,13,128,2,128]{4,1,2,0,3:T(8,128)(2,1)} %get-tuple-element.267) | copy-start | bytes 2555908 | tf_op jit(solution)/shard_map/while
  33.4 0.9 copy-start.3
  51.8 2.7 %copy-start.1 = (bf16[1,13,128,2,128]{4,1,2,0,3:T(8,128)(2,1)S(1)}, bf16[1,13,128,2,128]{4,1,2,0,3:T(8,128)(2,1)}, u32[]{:S(2)}) copy-start(bf16[1,13,128,2,128]{4,1,2,0,3:T(8,128)(2,1)} %get-tuple-element.267) | copy-start | bytes 2555908 | tf_op jit(solution)/shard_map/while
  53.3 0.9 copy-start.3
  71.7 2.7 %copy-start.1 = (bf16[1,13,128,2,128]{4,1,2,0,3:T(8,128)(2,1)S(1)}, bf16[1,13,128,2,128]{4,1,2,0,3:T(8,128)(2,1)}, u32[]{:S(2)}) copy-start(bf16[1,13,128,2,128]{4,1,2,0,3:T(8,128)(2,1)} %get-tuple-element.267) | copy-start | bytes 2555908 | tf_op jit(solution)/shard_map/while
  73.1 0.9 copy-start.3
  85.9 5.9 %collective-permute-start.3 = (bf16[3,2,2,2,6,128]{5,4,2,1,3,0:T(8,128)(2,1)S(1)}, bf16[3,2,2,2,6,128]{5,4,2,1,3,0:T(8,128)(2,1)S(1)}, u32[]{:S(2)}, u32[]{:S(2)}) collective-permute-start(bf16[3,2,2,2,6,128]{5,4,2,1,3,0:T(8,128)(2,1)S(1)} %get-tuple-element.169), channel_id=1, source_target_pairs={{1,0},{3,2},{5,4},{7,6},{9,8},{11,10},{13,12},{15,14},{17,16},{19,... | collective-permute-start | bytes 110600 | tf_op jit(solution)/shard_map/ppermute | solution.py:25
  87.2 4.6 %collective-permute-start.2 = (bf16[3,2,2,2,6,128]{5,4,2,1,3,0:T(8,128)(2,1)S(1)}, bf16[3,2,2,2,6,128]{5,4,2,1,3,0:T(8,128)(2,1)S(1)}, u32[]{:S(2)}, u32[]{:S(2)}) collective-permute-start(bf16[3,2,2,2,6,128]{5,4,2,1,3,0:T(8,128)(2,1)S(1)} %get-tuple-element.168), channel_id=1, source_target_pairs={{0,1},{2,3},{4,5},{6,7},{8,9},{10,11},{12,13},{14,15},{16,17},{18,... | collective-permute-start | bytes 110600 | tf_op jit(solution)/shard_map/ppermute | solution.py:22
  100.0 2.7 %copy-start.2 = (bf16[1,13,128,2,128]{4,1,2,0,3:T(8,128)(2,1)S(1)}, bf16[1,13,128,2,128]{4,1,2,0,3:T(8,128)(2,1)}, u32[]{:S(2)}) copy-start(bf16[1,13,128,2,128]{4,1,2,0,3:T(8,128)(2,1)} %get-tuple-element.281) | copy-start | bytes 2555908 | tf_op jit(solution)/shard_map/while
  101.5 0.9 copy-start.4
  119.3 2.7 %copy-start.2 = (bf16[1,13,128,2,128]{4,1,2,0,3:T(8,128)(2,1)S(1)}, bf16[1,13,128,2,128]{4,1,2,0,3:T(8,128)(2,1)}, u32[]{:S(2)}) copy-start(bf16[1,13,128,2,128]{4,1,2,0,3:T(8,128)(2,1)} %get-tuple-element.281) | copy-start | bytes 2555908 | tf_op jit(solution)/shard_map/while
  120.7 0.9 copy-start.4
  138.5 2.7 %copy-start.2 = (bf16[1,13,128,2,128]{4,1,2,0,3:T(8,128)(2,1)S(1)}, bf16[1,13,128,2,128]{4,1,2,0,3:T(8,128)(2,1)}, u32[]{:S(2)}) copy-start(bf16[1,13,128,2,128]{4,1,2,0,3:T(8,128)(2,1)} %get-tuple-element.281) | copy-start | bytes 2555908 | tf_op jit(solution)/shard_map/while
  139.9 0.9 copy-start.4
where the time goes:
time: 175 us; the launch traced here: 174 us
  local copies, waits for them, and re-layouts  85.4 us (49%)
  matrix products  35.3 us (20%)
  blocking collectives  22.4 us (13%)
  starting transfers between devices  15.4 us (9%)
  other arithmetic  8.59 us (5%)
  waiting for transfers between devices  4.73 us (3%)
    squeeze x12, local copies, waits for them, and re-layouts, advance(): out_real = product(real_part, band_mat[0]) - product(imag_part, band_mat[1])  34.9 us
    slice x18, local copies, waits for them, and re-layouts, advance(): out_real = product(real_part, band_mat[0]) - product(imag_part, band_mat[1])  30.4 us
    dot_general x24, matrix products, product(): jnp.einsum('fnyk,kj->fnyj', left, right, preferred_element_type=jnp.float32)  28.5 us
    unnamed x1, blocking collectives  16.8 us
    while x96, local copies, waits for them, and re-layouts  7.82 us
    ppermute x2, starting transfers between devices, padded_2(): lax.ppermute(lax.slice_in_dim(block, block.shape[dim] - width, None, axis...  6.46 us
    all_to_all x1, starting transfers between devices, body(): lax.all_to_all(spectra.astype(jnp.bfloat16), 'freq', split_axis=0, concat...  6.32 us
    squeeze x6, local copies, waits for them, and re-layouts, body(): fields, slot_images = lax.map(stepper, (padded, filter_taps))  5.97 us
  transfers between devices with their start and end apart: 5, of which 2 were waited for; matrix products, arithmetic and copies ran while one was open for 1% of the time, Pallas kernels for 0%

commit v1 on v0

v1 whole, which is shorter than its diff:
```python
import functools
import math

import jax
import jax.numpy as jnp
from jax import lax
from jax.experimental import pallas as pl
from jax.experimental.pallas import tpu as pltpu
from jax.sharding import PartitionSpec as P

FPD = 3
LANES = 128
SUB = 8
ROW_PAD = 8
VMEM_BYTES = 40 * 1024 * 1024
BF16 = jnp.bfloat16
F32 = jnp.float32


def list_bins(plan_ref, counts_ref, bins_ref):
    groups, cap = plan_ref.shape
    start = jnp.int32(0)
    for holder in range(groups):
        for slot in range(cap):
            bins_ref[start + slot] = plan_ref[holder, slot]
        start = start + counts_ref[holder]


def lane_iota(shape):
    return lax.broadcasted_iota(jnp.int32, shape, len(shape) - 1)


def row_iota(shape):
    return lax.broadcasted_iota(jnp.int32, shape, 0)


def dft_rows(bins_ref, group, nt):
    shape = (SUB, nt)
    row = row_iota(shape)
    bin_id = jnp.zeros(shape, jnp.int32)
    for slot in range(FPD):
        bin_id = jnp.where(row // 2 == slot, bins_ref[group * FPD + slot], bin_id)
    phase = lax.rem(bin_id * lane_iota(shape), jnp.int32(nt)) if nt & (nt - 1) else (bin_id * lane_iota(shape)) & (nt - 1)
    quarter = nt // 4
    turn = (phase + quarter // 2) // quarter
    angle = (phase - turn * quarter).astype(F32) * (2.0 * math.pi / nt)
    turn = (turn + (row & 1)) & 3
    sq = angle * angle
    cos = 1.0 + sq * (-1.0 / 2 + sq * (1.0 / 24 + sq * (-1.0 / 720 + sq * (1.0 / 40320))))
    sin = angle * (1.0 + sq * (-1.0 / 6 + sq * (1.0 / 120 + sq * (-1.0 / 5040 + sq * (1.0 / 362880)))))
    value = jnp.where((turn & 1) == 1, sin, cos)
    value = jnp.where(((turn + 1) & 2) == 2, -value, value)
    return (value * (1.0 / math.sqrt(nt))).astype(BF16)


def spectra_kernel(groups, plan_ref, counts_ref, rec_ref, out_ref, bins_ref, dft_ref):
    @pl.when(pl.program_id(0) == 0)
    def _():
        list_bins(plan_ref, counts_ref, bins_ref)
        for group in range(groups):
            dft_ref[group * SUB : (group + 1) * SUB] = dft_rows(bins_ref, group, rec_ref.shape[-1]).astype(F32)

    out = lax.dot_general(
        dft_ref[...].astype(BF16), rec_ref[0], (((1,), (1,)), ((), ())), preferred_element_type=F32
    )
    out_ref[0] = out.astype(BF16)


def send_kernel(
    groups, xw, plan_ref, counts_ref, vi_ref, sp_ref, rec_ref, out_ref, bins_ref, dft_ref, extra_ref, block_ref, tmp_ref
):
    shot = pl.program_id(0)
    depth, rows, _ = vi_ref.shape
    shots = sp_ref.shape[0]
    folds = LANES // xw
    block = out_ref.shape[2]

    @pl.when(shot == 0)
    def _():
        list_bins(plan_ref, counts_ref, bins_ref)
        for group in range(groups):
            dft_ref[group * SUB : (group + 1) * SUB] = dft_rows(bins_ref, group, rec_ref.shape[-1]).astype(F32)
        me = lax.axis_index("freq")
        lane = lane_iota((SUB, LANES))
        for item in range(depth + shots):
            if item < depth:
                block_ref[...] = vi_ref[item].astype(F32)
            else:
                block_ref[...] = sp_ref[item - depth].astype(F32)
            kept = jnp.zeros((SUB, LANES), F32)
            for low in range(folds):
                piece = block_ref[pl.ds(low, SUB, stride=folds), :]
                shift = lax.rem((low + folds - me) * xw, jnp.int32(LANES))
                kept = jnp.where(lane // xw == low, pltpu.roll(piece, shift, 1), kept)
            extra_ref[item * SUB : (item + 1) * SUB] = kept

    out = lax.dot_general(
        dft_ref[...].astype(BF16), rec_ref[0], (((1,), (1,)), ((), ())), preferred_element_type=F32
    )
    first = 2 * FPD * SUB
    for group in range(groups):
        base = group * block
        for high in range(SUB):
            tmp_ref[pl.ds(base + high, SUB, stride=SUB), :] = out[
                group * SUB : (group + 1) * SUB, high * LANES : (high + 1) * LANES
            ]
        tmp_ref[base + first : base + first + depth * SUB] = extra_ref[: depth * SUB]
        source = extra_ref[pl.ds(pl.multiple_of((depth + shot) * SUB, SUB), SUB), :]
        tmp_ref[base + first + depth * SUB : base + first + (depth + 1) * SUB] = source
        used = first + (depth + 1) * SUB
        if used < block:
            tmp_ref[base + used : base + block] = jnp.zeros((block - used, LANES), F32)
        out_ref[group, 0] = tmp_ref[base : base + block].astype(BF16)


def band_kernel(taps, ny, plan_ref, counts_ref, filt_ref, out_ref, bins_ref, picked_ref):
    plane = pl.program_id(0)

    @pl.when(plane == 0)
    def _():
        list_bins(plan_ref, counts_ref, bins_ref)

    nbin = filt_ref.shape[1]
    reach = taps // 2
    nref = filt_ref.shape[0] // (2 * taps * taps)
    bin_id = bins_ref[lax.axis_index("freq") * FPD + plane]
    hot = jnp.where(row_iota((nbin, LANES)) == bin_id, 1.0, 0.0).astype(BF16)
    picked_ref[...] = jnp.dot(filt_ref[...], hot, preferred_element_type=F32)
    width = 2 * ny
    lane = lane_iota((taps, LANES))
    full_lane = lane_iota((ny, LANES))
    keep = jnp.abs((full_lane & (ny - 1)) - row_iota((ny, LANES))) <= reach
    sign = jnp.where((lane < ny // 2) | (lane >= ny + ny // 2), -1.0, 1.0)
    for ref in range(nref):
        base = jnp.zeros((taps, LANES), F32)
        for part in range(2):
            for tap in range(taps):
                value = picked_ref[pl.ds((ref * taps + tap) * taps * 2 + part, taps, stride=2), :]
                base = jnp.where(lane == (part * ny + reach - tap) % width, value, base)
        turned = pltpu.roll(base, ny, 1) * sign
        for col_tap in range(taps):
            for part, rows in enumerate((base, turned)):
                spread = jnp.broadcast_to(rows[col_tap : col_tap + 1], (ny, LANES))
                band = pltpu.roll(spread, 0, 1, stride=1, stride_axis=0)
                band = jnp.where(keep, band, 0.0).astype(BF16)
                at = col_tap * width + part * ny
                out_ref[0, at : at + ny, ref * width : (ref + 1) * width] = band


def migrate_kernel(
    dims, plan_ref, counts_ref, wav_ref, table_ref, recv_ref, band_hbm, out_ref,
    bins_ref, grid_ref, field_ref, lhs_ref, band_ref, tab_ref, blend_ref, image_ref, sems,
):
    groups, halves, copies, xw, taps, depth, scale, folded = dims
    for plane in range(FPD):
        pltpu.make_async_copy(band_hbm.at[plane], band_ref.at[plane], sems.at[plane]).start()
    list_bins(plan_ref, counts_ref, bins_ref)
    nx = LANES
    ny = grid_ref.shape[0] // (2 * FPD + depth + 1)
    width = 2 * ny
    reach = taps // 2
    lane = lane_iota((SUB, LANES))
    if folded:
        folds = LANES // xw
        half_rows = ny // halves
        for half in range(halves):
            blocks = [recv_ref[group * halves + half].astype(F32) for group in range(groups)]
            for item in range(2 * FPD + depth + 1):
                for low in range(folds):
                    kept = None
                    for group in range(groups):
                        piece = blocks[group][item * SUB : (item + 1) * SUB]
                        shift = ((group - low) * xw) % LANES
                        if shift:
                            piece = pltpu.roll(piece, shift, 1)
                        kept = piece if kept is None else jnp.where(lane // xw == group, piece, kept)
                    grid_ref[pl.ds(item * ny + half * half_rows + low, SUB, stride=folds), :] = kept
    else:
        grid_ref[...] = recv_ref[...].astype(F32)
    tab_ref[:, : table_ref.shape[1]] = jnp.broadcast_to(table_ref[...], (SUB, table_ref.shape[1]))
    at = 2 * FPD * ny
    for step in range(depth):
        for part in range(2):
            for row in range(0, ny, SUB):
                index = grid_ref[at + row : at + row + SUB].astype(jnp.int32)
                blend_ref[step, part * ny + row : part * ny + row + SUB] = jnp.take_along_axis(
                    tab_ref[...], index, axis=1
                )
        at += ny
        blend_ref[step] = blend_ref[step].T
    pattern = grid_ref[at : at + ny]
    pattern = jnp.concatenate([pattern, pattern], axis=0).T
    full_lane = lane_iota((nx, width))
    first = lax.axis_index("freq") * FPD
    for plane in range(FPD):
        bin_id = bins_ref[first + plane]
        wave = jnp.where(full_lane < ny, wav_ref[0, bin_id], wav_ref[1, bin_id])
        field_ref[plane, 0, ROW_PAD : ROW_PAD + nx] = (pattern * wave).astype(BF16).astype(F32)
        field_ref[plane, 1, ROW_PAD : ROW_PAD + nx] = grid_ref[plane * width : (plane + 1) * width].T
        for field in range(2):
            field_ref[plane, field, :ROW_PAD] = jnp.zeros((ROW_PAD, width), F32)
            field_ref[plane, field, ROW_PAD + nx :] = jnp.zeros((ROW_PAD, width), F32)
    for step in range(depth):
        blend = blend_ref[step]
        total = None
        for plane in range(FPD):
            for field in range(2):
                for tap in range(taps):
                    rows = field_ref[plane, field, pl.ds(ROW_PAD - reach + tap, nx), :]
                    lhs_ref[plane, field * nx : (field + 1) * nx, tap * width : (tap + 1) * width] = rows.astype(BF16)
            if step == 0:
                pltpu.make_async_copy(band_hbm.at[plane], band_ref.at[plane], sems.at[plane]).wait()
            both = jnp.dot(lhs_ref[plane], band_ref[plane], preferred_element_type=F32)
            term = None
            for field in range(2):
                low = both[field * nx : (field + 1) * nx, :width]
                high = both[field * nx : (field + 1) * nx, width:]
                new = (low + blend * (high - low)).astype(BF16).astype(F32)
                if step + 1 < depth:
                    field_ref[plane, field, ROW_PAD : ROW_PAD + nx] = new
                term = new if term is None else term * new
            total = term if total is None else total + term
        turned = total.T
        image_ref[pl.ds(step, ny, stride=depth), :] = (turned[:ny] + turned[ny:]) * scale
    share = ny // (groups * halves) * depth
    for group in range(groups):
        for half in range(halves):
            start = (half * groups + group) * share
            piece = image_ref[start : start + share]
            for copy in range(copies):
                out_ref[(group * halves + half) * copies + copy] = piece


def smem():
    return pl.BlockSpec(memory_space=pltpu.SMEM)


def vmem():
    return pl.BlockSpec(memory_space=pltpu.VMEM)


def body(records, source_pattern, wavelet, filters, vel_table, vel_index, freq_plan, counts):
    groups = lax.axis_size("freq")
    halves = lax.axis_size("half")
    copies = lax.axis_size("shot")
    shots, rows, xw, nt = records.shape
    depth = vel_index.shape[0]
    nref, _, taps, _, nbin = filters.shape
    nx = xw * groups
    ny = rows * halves
    items = 2 * FPD + depth + 1
    cap = freq_plan.shape[1]
    folded = LANES % xw == 0 and rows * xw == SUB * LANES
    bins = pltpu.SMEM((groups * FPD + cap,), jnp.int32)
    params = functools.partial(pltpu.CompilerParams, vmem_limit_bytes=VMEM_BYTES)
    flat = records.reshape(shots, rows * xw, nt)

    if folded:
        block = (items * SUB + 15) // 16 * 16
        send = pl.pallas_call(
            functools.partial(send_kernel, groups, xw),
            out_shape=jax.ShapeDtypeStruct((groups, shots, block, LANES), BF16),
            grid=(shots,),
            in_specs=[
                smem(), smem(),
                pl.BlockSpec(vel_index.shape, lambda s: (0, 0, 0)),
                pl.BlockSpec(source_pattern.shape, lambda s: (0, 0, 0)),
                pl.BlockSpec((1, rows * xw, nt), lambda s: (s, 0, 0)),
            ],
            out_specs=pl.BlockSpec((groups, 1, block, LANES), lambda s: (0, s, 0, 0)),
            scratch_shapes=[
                bins,
                pltpu.VMEM((groups * SUB, nt), F32),
                pltpu.VMEM(((depth + shots) * SUB, LANES), F32),
                pltpu.VMEM((rows, LANES), F32),
                pltpu.VMEM((groups * block, LANES), F32),
            ],
            compiler_params=params(),
            name="send_blocks",
        )(freq_plan, counts, vel_index, source_pattern, flat)
        send = send.reshape(groups * halves, block, LANES)
        recv = lax.all_to_all(send, ("freq", "half"), 0, 0, tiled=True)
    else:
        spectra = pl.pallas_call(
            functools.partial(spectra_kernel, groups),
            out_shape=jax.ShapeDtypeStruct((shots, groups * SUB, rows * xw), BF16),
            grid=(shots,),
            in_specs=[smem(), smem(), pl.BlockSpec((1, rows * xw, nt), lambda s: (s, 0, 0))],
            out_specs=pl.BlockSpec((1, groups * SUB, rows * xw), lambda s: (s, 0, 0)),
            scratch_shapes=[bins, pltpu.VMEM((groups * SUB, nt), F32)],
            compiler_params=params(),
            name="spectra",
        )(freq_plan, counts, flat)
        spectra = spectra.reshape(shots, groups, SUB, rows, xw)[:, :, : 2 * FPD].swapaxes(0, 1)
        start = lax.axis_index("freq") * xw
        classes = lax.dynamic_slice_in_dim(vel_index, start, xw, 2).astype(BF16)
        classes = jnp.broadcast_to(classes, (groups, shots) + classes.shape)
        pattern = lax.dynamic_slice_in_dim(source_pattern, start, xw, 2)[:, None]
        pattern = jnp.broadcast_to(pattern, (groups,) + pattern.shape)
        send = jnp.concatenate([spectra, classes, pattern], axis=2).reshape(groups * halves, items, rows * xw)
        recv = lax.all_to_all(send, ("freq", "half"), 0, 0, tiled=True)
        recv = recv.reshape(groups, halves, items, rows, xw).transpose(2, 1, 3, 0, 4).reshape(items * ny, nx)

    table = filters.transpose(0, 2, 3, 1, 4).reshape(nref * taps * taps * 2, nbin)
    band_shape = (taps * 2 * ny, nref * 2 * ny)
    band = pl.pallas_call(
        functools.partial(band_kernel, taps, ny),
        out_shape=jax.ShapeDtypeStruct((FPD,) + band_shape, BF16),
        grid=(FPD,),
        in_specs=[smem(), smem(), pl.BlockSpec(table.shape, lambda s: (0, 0))],
        out_specs=pl.BlockSpec((1,) + band_shape, lambda s: (s, 0, 0)),
        scratch_shapes=[bins, pltpu.VMEM((table.shape[0], LANES), F32)],
        compiler_params=params(),
        name="bands",
    )(freq_plan, counts, table)

    scale = 1.0 / math.sqrt(FPD * groups * shots * copies)
    dims = (groups, halves, copies, xw, taps, depth, scale, folded)
    share = ny // (groups * halves)
    terms = pl.pallas_call(
        functools.partial(migrate_kernel, dims),
        out_shape=jax.ShapeDtypeStruct((groups * halves * copies, share * depth, nx), F32),
        in_specs=[smem(), smem(), smem(), vmem(), vmem(), pl.BlockSpec(memory_space=pl.ANY)],
        out_specs=vmem(),
        scratch_shapes=[
            bins,
            pltpu.VMEM((items * ny, nx), F32),
            pltpu.VMEM((FPD, 2, nx + 2 * ROW_PAD, 2 * ny), F32),
            pltpu.VMEM((FPD, 2 * nx, taps * 2 * ny), BF16),
            pltpu.VMEM((FPD,) + band_shape, BF16),
            pltpu.VMEM((SUB, LANES), F32),
            pltpu.VMEM((depth, 2 * ny, nx), F32),
            pltpu.VMEM((ny * depth, nx), F32),
            pltpu.SemaphoreType.DMA((FPD,)),
        ],
        compiler_params=params(),
        name="migrate",
    )(freq_plan, counts, wavelet.T, vel_table[None], recv, band)
    terms = lax.all_to_all(terms, ("freq", "half", "shot"), 0, 0, tiled=True)
    return jnp.sum(terms, axis=0).reshape(1, share, depth, nx)


def solution(mesh):
    return jax.shard_map(
        body,
        mesh=mesh,
        in_specs=(
            P(("group", "shot"), "half", "freq", None),
            P(("group", "shot"), "half", None),
            P(),
            P(),
            P(),
            P("group", "half", None),
            P(),
            P(),
        ),
        out_specs=P("half", "freq", "group", None),
        check_vma=False,
    )
```

time: 175 us -> 37 us (0.21)
  local copies, waits for them, and re-layouts: 85.4 us -> 4.57 us
  matrix products: 35.3 us -> 0 us
  blocking collectives: 22.4 us -> 11.3 us
  Pallas kernels: 0 us -> 9.3 us
  starting transfers between devices: 15.4 us -> 6.32 us
  other arithmetic: 8.59 us -> 0.62 us
    squeeze x18 -> x0, local copies, waits for them, and re-layouts: 40.9 us -> none  [the longest x12 34.9 us: advance(): out_real = product(real_part, band_mat[0]) - product(imag_part, band_mat[1])]
    dot_general x34 -> x0, matrix products: 35.3 us -> none  [the longest x24 28.5 us: product(): jnp.einsum('fnyk,kj->fnyj', left, right, preferred_element_type=jnp.float32)]
    slice x32 -> x0, local copies, waits for them, and re-layouts: 32.5 us -> none  [the longest x18 30.4 us: advance(): out_real = product(real_part, band_mat[0]) - product(imag_part, band_mat[1])]
    unnamed x1 -> x0, blocking collectives: 16.8 us -> none
    all_to_all x0 -> x1, blocking collectives: none -> 11.3 us  [body(): terms = lax.all_to_all(terms, ('freq', 'half', 'shot'), 0, 0, tiled=True)]
    pallas_call x0 -> x3, Pallas kernels: none -> 9.3 us  [the longest x1 4.41 us: body(): pl.pallas_call(functools.partial(migrate_kernel, dims), out_shape=jax.Sha...]
    ppermute x4 -> x0, starting transfers between devices: 9.05 us -> none  [the longest x2 6.46 us: padded_2(): lax.ppermute(lax.slice_in_dim(block, block.shape[dim] - width, None, axis...]
    while x96 -> x0, local copies, waits for them, and re-layouts: 7.82 us -> none
  transfers between devices with their start and end apart: 5 -> 1, of which waited for: 2 -> 1; matrix products, arithmetic and copies ran while one was open for 1% -> 0% of each run, Pallas kernels for 0% -> 7%
where the time goes in v1:
time: 37 us; the launch traced here: 36.6 us
  blocking collectives  11.3 us (31%)
  Pallas kernels  9.3 us (25%)
  starting transfers between devices  6.32 us (17%)
  local copies, waits for them, and re-layouts  4.57 us (12%)
  waiting for transfers between devices  4.46 us (12%)
  other arithmetic  0.62 us (2%)
    all_to_all x1, blocking collectives, body(): terms = lax.all_to_all(terms, ('freq', 'half', 'shot'), 0, 0, tiled=True)  11.3 us
    all_to_all x1, starting transfers between devices, body(): recv = lax.all_to_all(send, ('freq', 'half'), 0, 0, tiled=True)  6.32 us
    all_to_all x1, waiting for transfers between devices, body(): recv = lax.all_to_all(send, ('freq', 'half'), 0, 0, tiled=True)  4.46 us
    unnamed x20, local copies, waits for them, and re-layouts  4.43 us
    pallas_call x1, Pallas kernels, body(): pl.pallas_call(functools.partial(migrate_kernel, dims), out_shape=jax.Sha...  4.41 us
    pallas_call x1, Pallas kernels, body(): pl.pallas_call(functools.partial(band_kernel, taps, ny), out_shape=jax.Sh...  2.58 us
    pallas_call x1, Pallas kernels, body(): pl.pallas_call(functools.partial(send_kernel, groups, xw), out_shape=jax....  2.31 us
  transfers between devices with their start and end apart: 1, of which 1 were waited for; matrix products, arithmetic and copies ran while one was open for 0% of the time, Pallas kernels for 7%

profile of v1, /device:TPU:0, one launch (start us, length us, event | category | flops | bytes accessed | tf_op | source)
XLA Modules:
  0.0 36.6 jit_solution(17704423698150869710)
XLA Ops:
  0.0 0.0 copy-start.6
  0.0 0.0 copy-start
  0.0 1.6 %copy-done = bf16[2,32,32,512]{3,2,1,0:T(8,128)(2,1)S(1)} copy-done((bf16[2,32,32,512]{3,2,1,0:T(8,128)(2,1)S(1)}, bf16[2,32,32,512]{3,2,1,0:T(8,128)(2,1)}, u32[]{:S(2)}) %copy-start) | copy-done | bytes 2097176
  1.6 0.0 copy-start.1
  1.6 0.8 %copy-done.1 = s32[2,32,128]{2,1,0:T(8,128)S(1)} copy-done((s32[2,32,128]{2,1,0:T(8,128)S(1)}, s32[2,32,128]{2,1,0:T(8,128)}, u32[]{:S(2)}) %copy-start.1) | copy-done | bytes 32792
  2.4 0.0 copy-start.2
  2.4 0.7 %copy-done.2 = s32[4,6]{1,0:T(4,128)S(1)} copy-done((s32[4,6]{1,0:T(4,128)S(1)}, s32[4,6]{1,0:T(4,128)}, u32[]{:S(2)}) %copy-start.2) | copy-done | bytes 120
  3.0 0.0 copy-start.4
  3.1 0.7 %copy-done.4 = bf16[2,32,128]{2,1,0:T(8,128)(2,1)S(1)} copy-done((bf16[2,32,128]{2,1,0:T(8,128)(2,1)S(1)}, bf16[2,32,128]{2,1,0:T(8,128)(2,1)}, u32[]{:S(2)}) %copy-start.4) | copy-done | bytes 16408
  3.8 0.0 copy-start.5
  3.8 0.7 %copy-done.5 = s32[4]{0:T(128)S(1)} copy-done((s32[4]{0:T(128)S(1)}, s32[4]{0:T(128)}, u32[]{:S(2)}) %copy-start.5) | copy-done | bytes 40
  4.4 0.0 copy-start.9
  4.4 0.0 copy-start.3
  4.4 0.0 copy-start.7
  4.4 0.0 copy-start.8
  4.4 2.3 %send_blocks.1 = bf16[4,2,80,128]{3,2,1,0:T(8,128)(2,1)} custom-call(s32[4,6]{1,0:T(4,128)S(1)} %copy-done.2, s32[4]{0:T(128)S(1)} %copy-done.5, s32[2,32,128]{2,1,0:T(8,128)S(1)} %copy-done.1, bf16[2,32,128]{2,1,0:T(8,128)(2,1)S(1)} %copy-done.4, bf16[2,1024,512]{2,1,0:T(8,128)(2,1)S(1)} %bitcast.6), custom_call_target="tpu_custom_call" | custom-call | tf_op jit(solution)/shard_map/send_blocks/pallas_call | solution.py:260
  6.7 6.3 %all-to-all-start = ((bf16[8,80,128]{2,1,0:T(8,128)(2,1)}), bf16[8,80,128]{2,1,0:T(8,128)(2,1)S(1)}, u32[]{:S(2)}, u32[]{:S(2)}) async-start(bf16[8,80,128]{2,1,0:T(8,128)(2,1)} %bitcast.3), calls=%async_computation | async-start | bytes 327680 | tf_op jit(solution)/shard_map/all_to_all | solution.py:282
  13.1 0.0 copy-done.9
  13.1 0.1 reshape.14.filt_ref
  13.2 0.0 copy-done.6
  13.2 0.0 copy-done.3
  13.2 2.6 %bands.1.band_hbm = bf16[3,1664,256]{2,1,0:T(8,128)(2,1)S(1)} custom-call(s32[4,6]{1,0:T(4,128)S(1)} %copy-done.3, s32[4]{0:T(128)S(1)} %copy-done.6, bf16[676,256]{1,0:T(8,128)(2,1)S(1)} %reshape.14.filt_ref), custom_call_target="tpu_custom_call" | custom-call | tf_op jit(solution)/shard_map/bands/pallas_call | solution.py:306
  15.8 4.5 %all-to-all-done.recv_ref = bf16[8,80,128]{2,1,0:T(8,128)(2,1)S(1)} async-done(((bf16[8,80,128]{2,1,0:T(8,128)(2,1)}), bf16[8,80,128]{2,1,0:T(8,128)(2,1)S(1)}, u32[]{:S(2)}, u32[]{:S(2)}) %all-to-all-start) | async-done | bytes 163872 | tf_op jit(solution)/shard_map/all_to_all | solution.py:282
  20.3 0.0 copy-done.7
  20.3 0.0 copy-done.8
  20.3 4.4 %migrate.1 = f32[16,16,128]{2,1,0:T(8,128)S(1)} custom-call(s32[4,6]{1,0:T(4,128)S(1)} %copy-done.3, s32[4]{0:T(128)S(1)} %copy-done.6, f32[2,256]{1,0:T(2,128)S(1)} %bitcast.7, f32[1,64]{1,0:T(1,128)S(1)} %bitcast.8, bf16[8,80,128]{2,1,0:T(8,128)(2,1)S(1)} %all-to-all-done.recv_ref, bf16[3,1664,256]{2,1,0:T(8,128)(2,1)S(1)} %bands.1.band_hbm), custom_call_target="tpu_custom_call" | custom-call | tf_op jit(solution)/shard_map/migrate/pallas_call | solution.py:320
  24.7 11.3 %all_to_all.10 = f32[16,16,128]{2,1,0:T(8,128)S(1)} all-to-all(f32[16,16,128]{2,1,0:T(8,128)S(1)} %migrate.1), channel_id=1, replica_groups=mesh['group'=2,'freq'=4,'shot'=2,'half'=2] {'freq','half','shot'}, dimensions={0} | all-to-all | bytes 262144 | tf_op jit(solution)/shard_map/all_to_all | solution.py:339
  36.0 0.6 %reduce_sum.9 = f32[16,128]{1,0:T(8,128)} reduce(f32[16,16,128]{2,1,0:T(8,128)S(1)} %all_to_all.10, f32[]{:T(128)} %constant.0.clone.1), dimensions={0}, to_apply=%region_0.0 | reduce | flops 30720 | bytes 139268 | tf_op jit(solution)/shard_map/reduce_sum | solution.py:340
Async XLA Ops:
  0.0 13.2 %copy-start.6 = (s32[4]{0:T(128)S(1)}, s32[4]{0:T(128)}, u32[]{:S(2)}) copy-start(s32[4]{0:T(128)} %counts_ref.5) | copy-start | bytes 52
  0.0 1.6 %copy-start = (bf16[2,32,32,512]{3,2,1,0:T(8,128)(2,1)S(1)}, bf16[2,32,32,512]{3,2,1,0:T(8,128)(2,1)}, u32[]{:S(2)}) copy-start(bf16[2,32,32,512]{3,2,1,0:T(8,128)(2,1)} %param.8) | copy-start | bytes 6291460
  1.6 0.8 %copy-start.1 = (s32[2,32,128]{2,1,0:T(8,128)S(1)}, s32[2,32,128]{2,1,0:T(8,128)}, u32[]{:S(2)}) copy-start(s32[2,32,128]{2,1,0:T(8,128)} %vi_ref.1) | copy-start | bytes 98308
  2.4 0.7 %copy-start.2 = (s32[4,6]{1,0:T(4,128)S(1)}, s32[4,6]{1,0:T(4,128)}, u32[]{:S(2)}) copy-start(s32[4,6]{1,0:T(4,128)} %plan_ref.5) | copy-start | bytes 292
  3.0 0.7 %copy-start.4 = (bf16[2,32,128]{2,1,0:T(8,128)(2,1)S(1)}, bf16[2,32,128]{2,1,0:T(8,128)(2,1)}, u32[]{:S(2)}) copy-start(bf16[2,32,128]{2,1,0:T(8,128)(2,1)} %sp_ref.1) | copy-start | bytes 49156
  3.8 0.7 %copy-start.5 = (s32[4]{0:T(128)S(1)}, s32[4]{0:T(128)}, u32[]{:S(2)}) copy-start(s32[4]{0:T(128)} %counts_ref.5) | copy-start | bytes 52
  4.4 8.6 %copy-start.9 = (bf16[2,2,13,13,256]{4,1,3,2,0:T(2,128)(2,1)S(1)}, bf16[2,2,13,13,256]{4,1,3,2,0:T(2,128)(2,1)}, u32[]{:S(2)}) copy-start(bf16[2,2,13,13,256]{4,1,3,2,0:T(2,128)(2,1)} %param.11) | copy-start | bytes 1038340
  4.4 8.8 %copy-start.3 = (s32[4,6]{1,0:T(4,128)S(1)}, s32[4,6]{1,0:T(4,128)}, u32[]{:S(2)}) copy-start(s32[4,6]{1,0:T(4,128)} %plan_ref.5) | copy-start | bytes 292
  4.4 15.9 %copy-start.7 = (f32[256,2]{0,1:T(2,128)S(1)}, f32[256,2]{0,1:T(2,128)}, u32[]{:S(2)}) copy-start(f32[256,2]{0,1:T(2,128)} %param.10) | copy-start | bytes 6148
  4.4 15.9 %copy-start.8 = (f32[64]{0:T(128)S(1)}, f32[64]{0:T(128)}, u32[]{:S(2)}) copy-start(f32[64]{0:T(128)} %param.12) | copy-start | bytes 772
  6.7 13.5 %all-to-all-start = ((bf16[8,80,128]{2,1,0:T(8,128)(2,1)}), bf16[8,80,128]{2,1,0:T(8,128)(2,1)S(1)}, u32[]{:S(2)}, u32[]{:S(2)}) async-start(bf16[8,80,128]{2,1,0:T(8,128)(2,1)} %bitcast.3), calls=%async_computation | async-start | bytes 327680 | tf_op jit(solution)/shard_map/all_to_all | solution.py:282

commit v2 on v1

v2 whole, which is shorter than its diff:
```python
import functools
import math

import jax
import jax.numpy as jnp
from jax import lax
from jax.experimental import pallas as pl
from jax.experimental.pallas import tpu as pltpu
from jax.sharding import PartitionSpec as P

FPD = 3
LANES = 128
SUB = 8
ROW_PAD = 8
CHUNKS = 2
VMEM_BYTES = 40 * 1024 * 1024
BF16 = jnp.bfloat16
F32 = jnp.float32


def list_bins(plan_ref, counts_ref, bins_ref):
    groups, cap = plan_ref.shape
    start = jnp.int32(0)
    for holder in range(groups):
        for slot in range(cap):
            bins_ref[start + slot] = plan_ref[holder, slot]
        start = start + counts_ref[holder]


def lane_iota(shape):
    return lax.broadcasted_iota(jnp.int32, shape, len(shape) - 1)


def row_iota(shape):
    return lax.broadcasted_iota(jnp.int32, shape, 0)


def dft_rows(bins_ref, group, nt):
    shape = (SUB, nt)
    row = row_iota(shape)
    bin_id = jnp.zeros(shape, jnp.int32)
    for slot in range(FPD):
        bin_id = jnp.where(row // 2 == slot, bins_ref[group * FPD + slot], bin_id)
    phase = bin_id * lane_iota(shape)
    phase = lax.rem(phase, jnp.int32(nt)) if nt & (nt - 1) else phase & (nt - 1)
    quarter = nt // 4
    turn = (phase + quarter // 2) // quarter
    angle = (phase - turn * quarter).astype(F32) * (2.0 * math.pi / nt)
    turn = (turn + (row & 1)) & 3
    sq = angle * angle
    cos = 1.0 + sq * (-1.0 / 2 + sq * (1.0 / 24 + sq * (-1.0 / 720 + sq * (1.0 / 40320))))
    sin = angle * (1.0 + sq * (-1.0 / 6 + sq * (1.0 / 120 + sq * (-1.0 / 5040 + sq * (1.0 / 362880)))))
    value = jnp.where((turn & 1) == 1, sin, cos)
    value = jnp.where(((turn + 1) & 2) == 2, -value, value)
    return value * (1.0 / math.sqrt(nt))


def transform(dft, block):
    return lax.dot_general(dft, block, (((1,), (1,)), ((), ())), preferred_element_type=F32)


def send_kernel(
    groups, folded, plan_hbm, counts_hbm, wav_hbm, filt_hbm, rec_hbm, out_ref, own_ref, wave_ref, filt_ref,
    plan_ref, counts_ref, wav_ref, bins_ref, dft_ref, rec_ref, tmp_ref, small_sems, sems,
):
    shots, cells, nt = rec_hbm.shape
    part = cells // CHUNKS
    small = [
        pltpu.make_async_copy(plan_hbm, plan_ref, small_sems.at[0]),
        pltpu.make_async_copy(counts_hbm, counts_ref, small_sems.at[1]),
        pltpu.make_async_copy(wav_hbm, wav_ref, small_sems.at[2]),
    ]
    for copy in small:
        copy.start()
    copies = []
    for shot in range(shots):
        for chunk in range(CHUNKS):
            rows = pl.ds(chunk * part, part)
            copy = pltpu.make_async_copy(
                rec_hbm.at[shot, rows], rec_ref.at[shot, rows], sems.at[shot * CHUNKS + chunk]
            )
            copy.start()
            copies.append(copy)
    filters = pltpu.make_async_copy(filt_hbm, filt_ref, small_sems.at[3])
    filters.start()
    for copy in small:
        copy.wait()
    list_bins(plan_ref, counts_ref, bins_ref)
    for group in range(groups):
        dft_ref[group * SUB : (group + 1) * SUB] = dft_rows(bins_ref, group, nt)
    dft = dft_ref[...].astype(BF16)
    first = lax.axis_index("freq") * FPD
    lane = lane_iota((1, LANES))
    for plane in range(FPD):
        bin_id = bins_ref[first + plane]
        own_ref[plane : plane + 1] = jnp.full((1, LANES), bin_id, jnp.int32)
        wave_ref[plane : plane + 1] = jnp.where(lane < LANES // 2, wav_ref[0, bin_id], wav_ref[1, bin_id])
    for shot in range(shots):
        for chunk in range(CHUNKS):
            copies[shot * CHUNKS + chunk].wait()
            out = transform(dft, rec_ref[shot, chunk * part : (chunk + 1) * part])
            if not folded:
                out_ref[shot, :, chunk * part : (chunk + 1) * part] = out.astype(BF16)
                continue
            highs = part // LANES
            for group in range(groups):
                base = (group * shots + shot) * SUB * SUB + chunk * highs
                for high in range(highs):
                    tmp_ref[pl.ds(base + high, SUB, stride=SUB), :] = out[
                        group * SUB : (group + 1) * SUB, high * LANES : (high + 1) * LANES
                    ]
        if folded:
            for group in range(groups):
                base = (group * shots + shot) * SUB * SUB
                out_ref[group, shot] = tmp_ref[base : base + 2 * FPD * SUB].astype(BF16)
    filters.wait()


def make_bands(taps, nref, ny, picked_ref, band_ref):
    reach = taps // 2
    width = 2 * ny
    lane = lane_iota((taps, width))
    full_lane = lane_iota((ny, width))
    keep = jnp.abs((full_lane & (ny - 1)) - row_iota((ny, width))) <= reach
    sign = jnp.where((lane < ny // 2) | (lane >= ny + ny // 2), -1.0, 1.0)
    for ref in range(nref):
        base = jnp.zeros((taps, width), F32)
        for part in range(2):
            for tap in range(taps):
                value = picked_ref[pl.ds((ref * taps + tap) * taps * 2 + part, taps, stride=2), :]
                base = jnp.where(lane == (part * ny + reach - tap) % width, value, base)
        turned = pltpu.roll(base, ny, 1) * sign
        for col_tap in range(taps):
            for part, rows in enumerate((base, turned)):
                spread = jnp.broadcast_to(rows[col_tap : col_tap + 1], (ny, width))
                band = pltpu.roll(spread, 0, 1, stride=1, stride_axis=0)
                band = jnp.where(keep, band, 0.0).astype(BF16)
                at = col_tap * width + part * ny
                band_ref[at : at + ny, ref * width : (ref + 1) * width] = band


def set_field(field_ref, value):
    rows, width = value.shape
    field_ref[:ROW_PAD] = jnp.zeros((ROW_PAD, width), F32)
    field_ref[ROW_PAD : ROW_PAD + rows] = value
    field_ref[ROW_PAD + rows :] = jnp.zeros((ROW_PAD, width), F32)


def advance(taps, field_ref, lhs_ref, band_ref, blend):
    rows, width = blend.shape
    for tap in range(taps):
        piece = field_ref[pl.ds(ROW_PAD - taps // 2 + tap, rows), :]
        lhs_ref[:, tap * width : (tap + 1) * width] = piece.astype(BF16)
    both = jnp.dot(lhs_ref[...], band_ref[...], preferred_element_type=F32)
    low, high = both[:, :width], both[:, width:]
    return (low + blend * (high - low)).astype(BF16).astype(F32)


def source_kernel(taps, nref, depth, halves, own_ref, wave_ref, filt_ref, table_hbm, *refs):
    class_hbm, refs = refs[:halves], refs[halves:]
    pattern_hbm, refs = refs[:halves], refs[halves:]
    band_ref, blend_ref, source_ref, class_refs, pattern_refs, table_ref, picked_ref, grid_ref, tab_ref, field_ref, lhs_ref, sems = refs
    copies = [pltpu.make_async_copy(table_hbm, table_ref, sems.at[0])]
    for turn in range(halves):
        copies.append(pltpu.make_async_copy(class_hbm[turn], class_refs.at[turn], sems.at[1 + 2 * turn]))
        copies.append(pltpu.make_async_copy(pattern_hbm[turn], pattern_refs.at[turn], sems.at[2 + 2 * turn]))
    for copy in copies:
        copy.start()
    mine = lax.axis_index("half")
    rows = class_hbm[0].shape[1]
    ny, nx = grid_ref.shape[1:]
    nbin = filt_ref.shape[1]
    for plane in range(FPD):
        hot = jnp.where(row_iota((nbin, LANES)) == own_ref[plane : plane + 1], 1.0, 0.0).astype(BF16)
        picked_ref[plane] = jnp.dot(filt_ref[...], hot, preferred_element_type=F32)
    for plane in range(FPD - 1):
        make_bands(taps, nref, ny, picked_ref.at[plane], band_ref.at[plane])
    for copy in copies:
        copy.wait()
    for turn in range(halves):
        at = pl.ds(pl.multiple_of(lax.rem(mine + turn, halves) * rows, rows), rows)
        for step in range(depth):
            grid_ref[step, at, :] = class_refs[turn, step].astype(F32)
        grid_ref[depth, at, :] = pattern_refs[turn, mine].astype(F32)
    tab_ref[:, : table_ref.shape[1]] = jnp.broadcast_to(table_ref[...], (SUB, table_ref.shape[1]))
    for step in range(depth):
        pieces = []
        for row in range(0, ny, SUB):
            index = grid_ref[step, row : row + SUB].astype(jnp.int32)
            pieces.append(jnp.take_along_axis(tab_ref[...], index, axis=1))
        blend_ref[step] = jnp.concatenate(pieces + pieces, axis=0).T
    pattern = grid_ref[depth]
    pattern = jnp.concatenate([pattern, pattern], axis=0).T
    for plane in range(FPD):
        set_field(field_ref.at[plane], (pattern * wave_ref[plane : plane + 1]).astype(BF16).astype(F32))
    make_bands(taps, nref, ny, picked_ref.at[FPD - 1], band_ref.at[FPD - 1])
    for step in range(depth):
        for plane in range(FPD):
            new = advance(taps, field_ref.at[plane], lhs_ref.at[plane], band_ref.at[plane], blend_ref[step])
            source_ref[step, plane] = new
            if step + 1 < depth:
                field_ref[plane, ROW_PAD : ROW_PAD + nx] = new


def migrate_kernel(dims, recv_ref, band_ref, blend_ref, source_ref, out_ref, grid_ref, field_ref, lhs_ref, image_ref):
    groups, halves, copies, xw, taps, scale, folded = dims
    depth, nx, width = blend_ref.shape
    ny = width // 2
    if folded:
        folds = LANES // xw
        half_rows = ny // halves
        lane = lane_iota((SUB, LANES))
        for half in range(halves):
            blocks = [recv_ref[group * halves + half].astype(F32) for group in range(groups)]
            for item in range(2 * FPD):
                for low in range(folds):
                    kept = None
                    for group in range(groups):
                        piece = blocks[group][item * SUB : (item + 1) * SUB]
                        shift = ((group - low) * xw) % LANES
                        if shift:
                            piece = pltpu.roll(piece, shift, 1)
                        kept = piece if kept is None else jnp.where(lane // xw == group, piece, kept)
                    grid_ref[pl.ds(item * ny + half * half_rows + low, SUB, stride=folds), :] = kept
    else:
        grid_ref[...] = recv_ref[...].astype(F32)
    for plane in range(FPD):
        set_field(field_ref.at[plane], grid_ref[plane * width : (plane + 1) * width].T)
    for step in range(depth):
        total = None
        for plane in range(FPD):
            new = advance(taps, field_ref.at[plane], lhs_ref.at[plane], band_ref.at[plane], blend_ref[step])
            if step + 1 < depth:
                field_ref[plane, ROW_PAD : ROW_PAD + nx] = new
            term = source_ref[step, plane] * new
            total = term if total is None else total + term
        turned = total.T
        image_ref[pl.ds(step, ny, stride=depth), :] = (turned[:ny] + turned[ny:]) * scale
    share = ny // (groups * halves) * depth
    for group in range(groups):
        for half in range(halves):
            start = (half * groups + group) * share
            piece = image_ref[start : start + share].astype(BF16)
            for copy in range(copies):
                out_ref[(group * halves + half) * copies + copy] = piece


def vmem():
    return pl.BlockSpec(memory_space=pltpu.VMEM)


def hbm():
    return pl.BlockSpec(memory_space=pltpu.HBM)


def pinned(*arrays):
    return [pltpu.with_memory_space_constraint(array, pltpu.HBM) for array in arrays]


def from_halves(block, halves):
    blocks = [block]
    for turn in range(1, halves):
        blocks.append(lax.ppermute(block, "half", [((to + turn) % halves, to) for to in range(halves)]))
    return blocks


def body(records, source_pattern, wavelet, filters, vel_table, vel_index, freq_plan, counts):
    groups = lax.axis_size("freq")
    halves = lax.axis_size("half")
    copies = lax.axis_size("shot")
    shots, rows, xw, nt = records.shape
    depth = vel_index.shape[0]
    nref, _, taps, _, nbin = filters.shape
    nx = xw * groups
    ny = rows * halves
    items = 2 * FPD
    cap = freq_plan.shape[1]
    cells = rows * xw
    folded = LANES % xw == 0 and cells == SUB * LANES
    bins = pltpu.SMEM((groups * FPD + cap,), jnp.int32)
    params = pltpu.CompilerParams(vmem_limit_bytes=VMEM_BYTES)

    classes = from_halves(vel_index, halves)
    patterns = from_halves(source_pattern, halves)

    if folded:
        send_shape = (groups, shots, items * SUB, LANES)
    else:
        send_shape = (shots, groups * SUB, cells)
    table = filters.transpose(0, 2, 3, 1, 4)
    send, own, wave, table = pl.pallas_call(
        functools.partial(send_kernel, groups, folded),
        out_shape=[
            jax.ShapeDtypeStruct(send_shape, BF16),
            jax.ShapeDtypeStruct((SUB, LANES), jnp.int32),
            jax.ShapeDtypeStruct((SUB, LANES), F32),
            jax.ShapeDtypeStruct(table.shape, BF16),
        ],
        in_specs=[hbm()] * 5,
        out_specs=[vmem()] * 4,
        scratch_shapes=[
            pltpu.SMEM(freq_plan.shape, jnp.int32),
            pltpu.SMEM(counts.shape, jnp.int32),
            pltpu.SMEM((2, nbin), F32),
            bins,
            pltpu.VMEM((groups * SUB, nt), F32),
            pltpu.VMEM((shots, cells, nt), BF16),
            pltpu.VMEM((groups * shots * SUB * SUB, LANES), F32),
            pltpu.SemaphoreType.DMA((4,)),
            pltpu.SemaphoreType.DMA((shots * CHUNKS,)),
        ],
        compiler_params=params,
        cost_estimate=pl.CostEstimate(flops=2 * groups * SUB * records.size, bytes_accessed=4 * records.size, transcendentals=0),
        name="send_blocks",
    )(*pinned(freq_plan, counts, wavelet.T, table, records.reshape(shots, cells, nt)))
    send, classes, patterns, table = lax.optimization_barrier((send, classes, patterns, table))
    if folded:
        send = send.reshape(groups * halves, items * SUB, LANES)
        recv = lax.all_to_all(send, ("freq", "half"), 0, 0, tiled=True)
    else:
        send = send.reshape(shots, groups, SUB, cells)[:, :, :items].swapaxes(0, 1)
        send = send.reshape(groups * halves, items, cells)
        recv = lax.all_to_all(send, ("freq", "half"), 0, 0, tiled=True)
        recv = recv.reshape(groups, halves, items, rows, xw).transpose(2, 1, 3, 0, 4).reshape(items * ny, nx)

    table = table.reshape(nref * taps * taps * 2, nbin)
    band_shape = (FPD, taps * 2 * ny, nref * 2 * ny)
    lhs = pltpu.VMEM((FPD, nx, taps * 2 * ny), BF16)
    field = pltpu.VMEM((FPD, nx + 2 * ROW_PAD, 2 * ny), F32)
    band, blend, source = pl.pallas_call(
        functools.partial(source_kernel, taps, nref, depth, halves),
        out_shape=[
            jax.ShapeDtypeStruct(band_shape, BF16),
            jax.ShapeDtypeStruct((depth, nx, 2 * ny), F32),
            jax.ShapeDtypeStruct((depth, FPD, nx, 2 * ny), F32),
        ],
        in_specs=[vmem()] * 3 + [hbm()] * (1 + 2 * halves),
        out_specs=[vmem()] * 3,
        scratch_shapes=[
            pltpu.VMEM((halves,) + vel_index.shape, jnp.int32),
            pltpu.VMEM((halves,) + source_pattern.shape, BF16),
            pltpu.VMEM((1,) + vel_table.shape, F32),
            pltpu.VMEM((FPD, table.shape[0], LANES), F32),
            pltpu.VMEM((depth + 1, ny, nx), F32),
            pltpu.VMEM((SUB, LANES), F32),
            field,
            lhs,
            pltpu.SemaphoreType.DMA((1 + 2 * halves,)),
        ],
        compiler_params=params,
        cost_estimate=pl.CostEstimate(flops=4 * 10**9, bytes_accessed=10**7, transcendentals=0),
        name="source_fields",
    )(own, wave, table, *pinned(vel_table[None], *classes, *patterns))

    scale = 1.0 / math.sqrt(FPD * groups * shots * copies)
    share = ny // (groups * halves)
    terms = pl.pallas_call(
        functools.partial(migrate_kernel, (groups, halves, copies, xw, taps, scale, folded)),
        out_shape=jax.ShapeDtypeStruct((groups * halves * copies, share * depth, nx), BF16),
        in_specs=[vmem()] * 4,
        out_specs=vmem(),
        scratch_shapes=[
            pltpu.VMEM((items * ny, nx), F32),
            field,
            lhs,
            pltpu.VMEM((ny * depth, nx), F32),
        ],
        compiler_params=params,
        name="migrate",
    )(recv, band, blend, source)
    terms = lax.all_to_all(terms, ("freq", "half", "shot"), 0, 0, tiled=True)
    return jnp.sum(terms.astype(F32), axis=0).reshape(1, share, depth, nx)


def solution(mesh):
    return jax.shard_map(
        body,
        mesh=mesh,
        in_specs=(
            P(("group", "shot"), "half", "freq", None),
            P(("group", "shot"), "half", None),
            P(),
            P(),
            P(),
            P("group", "half", None),
            P(),
            P(),
        ),
        out_specs=P("half", "freq", "group", None),
        check_vma=False,
    )
```

time: 37 us -> 28.4 us (0.77)
  local copies, waits for them, and re-layouts: 4.57 us -> 0.14 us
  Pallas kernels: 9.3 us -> 7.15 us
  blocking collectives: 11.3 us -> 9.94 us
  waiting for transfers between devices: 4.46 us -> 3.24 us
  starting transfers between devices: 6.32 us -> 6.85 us
    unnamed x20 -> x4, local copies, waits for them, and re-layouts: 4.43 us -> 0.01 us
    pallas_call x3, Pallas kernels: 9.3 us -> 7.15 us  [the longest x1 2.94 us: body(): pl.pallas_call(functools.partial(source_kernel, taps, nref, depth, halves...]
    all_to_all x1, blocking collectives: 11.3 us -> 9.94 us  [body(): terms = lax.all_to_all(terms, ('freq', 'half', 'shot'), 0, 0, tiled=True)]
    all_to_all x1, waiting for transfers between devices: 4.46 us -> 3.24 us  [body(): recv = lax.all_to_all(send, ('freq', 'half'), 0, 0, tiled=True)]
    ppermute x0 -> x2, starting transfers between devices: none -> 0.51 us  [from_halves(): lax.ppermute(block, 'half', [((to + turn) % halves, to) for to in range(h...]
  transfers between devices with their start and end apart: 1 -> 3, of which waited for: 1 -> 1; matrix products, arithmetic and copies ran while one was open for 0% -> 0% of each run, Pallas kernels for 7% -> 21%
where the time goes in v2:
time: 28.4 us; the launch traced here: 28 us
  blocking collectives  9.94 us (35%)
  Pallas kernels  7.15 us (25%)
  starting transfers between devices  6.85 us (24%)
  waiting for transfers between devices  3.24 us (11%)
  other arithmetic  0.62 us (2%)
    all_to_all x1, blocking collectives, body(): terms = lax.all_to_all(terms, ('freq', 'half', 'shot'), 0, 0, tiled=True)  9.94 us
    all_to_all x1, starting transfers between devices, body(): recv = lax.all_to_all(send, ('freq', 'half'), 0, 0, tiled=True)  6.34 us
    all_to_all x1, waiting for transfers between devices, body(): recv = lax.all_to_all(send, ('freq', 'half'), 0, 0, tiled=True)  3.24 us
    pallas_call x1, Pallas kernels, body(): pl.pallas_call(functools.partial(source_kernel, taps, nref, depth, halves...  2.94 us
    pallas_call x1, Pallas kernels, body(): pl.pallas_call(functools.partial(send_kernel, groups, folded), out_shape=...  2.84 us
    pallas_call x1, Pallas kernels, body(): pl.pallas_call(functools.partial(migrate_kernel, (groups, halves, copies,...  1.37 us
    reduce_sum x1, other arithmetic, body(): return jnp.sum(terms.astype(F32), axis=0).reshape(1, share, depth, nx)  0.62 us
  transfers between devices with their start and end apart: 3, of which 1 were waited for; matrix products, arithmetic and copies ran while one was open for 0% of the time, Pallas kernels for 21%

profile of v2, /device:TPU:0, one launch (start us, length us, event | category | flops | bytes accessed | tf_op | source)
XLA Modules:
  0.0 28.0 jit_solution(11497825763855037979)
XLA Ops:
  0.0 0.5 %collective-permute-start = (s32[2,32,128]{2,1,0:T(8,128)}, s32[2,32,128]{2,1,0:T(8,128)S(1)}, u32[]{:S(2)}, u32[]{:S(2)}) collective-permute-start(s32[2,32,128]{2,1,0:T(8,128)} %refs_0_), channel_id=1, source_target_pairs={{1,0},{0,1},{3,2},{2,3},{5,4},{4,5},{7,6},{6,7},{9,8},{8,9},{11,10... | collective-permute-start | bytes 98312 | tf_op jit(solution)/shard_map/ppermute | solution.py:263
  0.5 0.1 collective-permute-start.1
  0.5 2.8 %send_blocks.1 = (bf16[4,2,48,128]{3,2,1,0:T(8,128)(2,1)}, s32[8,128]{1,0:T(8,128)S(1)}, f32[8,128]{1,0:T(8,128)S(1)}, bf16[2,13,13,2,256]{4,3,2,1,0:T(2,128)(2,1)S(1)}) custom-call(s32[4,6]{1,0:T(4,128)} %plan_hbm.1, s32[4]{0:T(128)} %counts_hbm.1, f32[2,256]{1,0:T(2,128)} %bitcast.8, bf16[2,13,13,2,256]{4,3,2,1,0:T(2,128)(2,1)} %bitcast.7, ...), custom_call_target="tpu_custom_call" | custom-call | flops 67108864 | bytes 4194304 | tf_op jit(solution)/shard_map/send_blocks/pallas_call | solution.py:291
  3.4 0.0 collective-permute-done.1.refs_3_
  3.4 0.0 copy-start.1
  3.4 0.0 collective-permute-done.refs_1_
  3.4 0.0 copy-start
  3.4 6.3 %all-to-all-start = ((bf16[8,48,128]{2,1,0:T(8,128)(2,1)}), bf16[8,48,128]{2,1,0:T(8,128)(2,1)S(1)}, u32[]{:S(2)}, u32[]{:S(2)}) async-start(bf16[8,48,128]{2,1,0:T(8,128)(2,1)} %bitcast.3), calls=%async_computation | async-start | bytes 196608 | tf_op jit(solution)/shard_map/all_to_all | solution.py:319
  9.7 0.1 reshape.14.filt_ref
  9.9 0.0 copy-done
  9.9 0.0 copy-done.1
  9.9 2.9 %source_fields.1 = (bf16[3,1664,256]{2,1,0:T(8,128)(2,1)S(1)}, f32[2,128,128]{2,1,0:T(8,128)S(1)}, f32[2,3,128,128]{3,2,1,0:T(8,128)S(1)}) custom-call(s32[8,128]{1,0:T(8,128)S(1)} %get-tuple-element.21.own_ref, f32[8,128]{1,0:T(8,128)S(1)} %get-tuple-element.22.wave_ref, bf16[676,256]{1,0:T(8,128)(2,1)S(1)} %reshape.14.filt_ref, f32[1,64]{1,0:T(1,128)} %bitcast.9, ...), custom_call_target="tpu_custom_call" | custom-call | flops 4000000000 | bytes 10000000 | tf_op jit(solution)/shard_map/source_fields/pallas_call | solution.py:330
  12.8 3.2 %all-to-all-done.recv_ref = bf16[8,48,128]{2,1,0:T(8,128)(2,1)S(1)} async-done(((bf16[8,48,128]{2,1,0:T(8,128)(2,1)}), bf16[8,48,128]{2,1,0:T(8,128)(2,1)S(1)}, u32[]{:S(2)}, u32[]{:S(2)}) %all-to-all-start) | async-done | bytes 98336 | tf_op jit(solution)/shard_map/all_to_all | solution.py:319
  16.1 1.4 %migrate.1 = bf16[16,16,128]{2,1,0:T(8,128)(2,1)S(1)} custom-call(bf16[8,48,128]{2,1,0:T(8,128)(2,1)S(1)} %all-to-all-done.recv_ref, bf16[3,1664,256]{2,1,0:T(8,128)(2,1)S(1)} %get-tuple-element.28.band_ref, f32[2,128,128]{2,1,0:T(8,128)S(1)} %get-tuple-element.29.blend_ref, f32[2,3,128,128]{3,2,1,0:T(8,128)S(1)} %get-tuple-element.30.source_ref), custom_call_target="tpu_custom_call" | custom-call | tf_op jit(solution)/shard_map/migrate/pallas_call | solution.py:357
  17.5 9.9 %all_to_all.10 = bf16[16,16,128]{2,1,0:T(8,128)(2,1)S(1)} all-to-all(bf16[16,16,128]{2,1,0:T(8,128)(2,1)S(1)} %migrate.1), channel_id=1, replica_groups=mesh['group'=2,'freq'=4,'shot'=2,'half'=2] {'freq','half','shot'}, dimensions={0} | all-to-all | bytes 131072 | tf_op jit(solution)/shard_map/all_to_all | solution.py:371
  27.4 0.6 %convert_reduce_fusion = f32[16,128]{1,0:T(8,128)} fusion(bf16[16,16,128]{2,1,0:T(8,128)(2,1)S(1)} %all_to_all.10), kind=kLoop, calls=%fused_computation | loop fusion | flops 63488 | bytes 73728 | tf_op jit(solution)/shard_map/reduce_sum | solution.py:372
Async XLA Ops:
  0.0 3.4 %collective-permute-start = (s32[2,32,128]{2,1,0:T(8,128)}, s32[2,32,128]{2,1,0:T(8,128)S(1)}, u32[]{:S(2)}, u32[]{:S(2)}) collective-permute-start(s32[2,32,128]{2,1,0:T(8,128)} %refs_0_), channel_id=1, source_target_pairs={{1,0},{0,1},{3,2},{2,3},{5,4},{4,5},{7,6},{6,7},{9,8},{8,9},{11,10... | collective-permute-start | bytes 98312 | tf_op jit(solution)/shard_map/ppermute | solution.py:263
  0.5 2.9 %collective-permute-start.1 = (bf16[2,32,128]{2,1,0:T(8,128)(2,1)}, bf16[2,32,128]{2,1,0:T(8,128)(2,1)S(1)}, u32[]{:S(2)}, u32[]{:S(2)}) collective-permute-start(bf16[2,32,128]{2,1,0:T(8,128)(2,1)} %refs_2_), channel_id=1, source_target_pairs={{1,0},{0,1},{3,2},{2,3},{5,4},{4,5},{7,6},{6,7},{9,8},{8,9},{11,10... | collective-permute-start | bytes 49160 | tf_op jit(solution)/shard_map/ppermute | solution.py:263
  3.4 6.5 %copy-start.1 = (bf16[2,32,128]{2,1,0:T(8,128)(2,1)}, bf16[2,32,128]{2,1,0:T(8,128)(2,1)S(1)}, u32[]{:S(2)}) copy-start(bf16[2,32,128]{2,1,0:T(8,128)(2,1)S(1)} %collective-permute-done.1.refs_3_) | copy-start | bytes 49156
  3.4 6.5 %copy-start = (s32[2,32,128]{2,1,0:T(8,128)}, s32[2,32,128]{2,1,0:T(8,128)S(1)}, u32[]{:S(2)}) copy-start(s32[2,32,128]{2,1,0:T(8,128)S(1)} %collective-permute-done.refs_1_) | copy-start | bytes 98308
  3.4 12.7 %all-to-all-start = ((bf16[8,48,128]{2,1,0:T(8,128)(2,1)}), bf16[8,48,128]{2,1,0:T(8,128)(2,1)S(1)}, u32[]{:S(2)}, u32[]{:S(2)}) async-start(bf16[8,48,128]{2,1,0:T(8,128)(2,1)} %bitcast.3), calls=%async_computation | async-start | bytes 196608 | tf_op jit(solution)/shard_map/all_to_all | solution.py:319

commit v3 on v2

--- a/solution.py
+++ b/solution.py
@@ -146,12 +146,11 @@
     field_ref[ROW_PAD + rows :] = jnp.zeros((ROW_PAD, width), F32)
 
 
-def advance(taps, field_ref, lhs_ref, band_ref, blend):
+def advance(taps, field_ref, band_ref, blend):
     rows, width = blend.shape
-    for tap in range(taps):
-        piece = field_ref[pl.ds(ROW_PAD - taps // 2 + tap, rows), :]
-        lhs_ref[:, tap * width : (tap + 1) * width] = piece.astype(BF16)
-    both = jnp.dot(lhs_ref[...], band_ref[...], preferred_element_type=F32)
+    first = ROW_PAD - taps // 2
+    pieces = [field_ref[pl.ds(first + tap, rows), :].astype(BF16) for tap in range(taps)]
+    both = jnp.dot(jnp.concatenate(pieces, axis=1), band_ref[...], preferred_element_type=F32)
     low, high = both[:, :width], both[:, width:]
     return (low + blend * (high - low)).astype(BF16).astype(F32)
 
@@ -159,7 +158,7 @@
 def source_kernel(taps, nref, depth, halves, own_ref, wave_ref, filt_ref, table_hbm, *refs):
     class_hbm, refs = refs[:halves], refs[halves:]
     pattern_hbm, refs = refs[:halves], refs[halves:]
-    band_ref, blend_ref, source_ref, class_refs, pattern_refs, table_ref, picked_ref, grid_ref, tab_ref, field_ref, lhs_ref, sems = refs
+    band_ref, blend_ref, source_ref, class_refs, pattern_refs, table_ref, picked_ref, grid_ref, tab_ref, field_ref, sems = refs
     copies = [pltpu.make_async_copy(table_hbm, table_ref, sems.at[0])]
     for turn in range(halves):
         copies.append(pltpu.make_async_copy(class_hbm[turn], class_refs.at[turn], sems.at[1 + 2 * turn]))
@@ -196,13 +195,13 @@
     make_bands(taps, nref, ny, picked_ref.at[FPD - 1], band_ref.at[FPD - 1])
     for step in range(depth):
         for plane in range(FPD):
-            new = advance(taps, field_ref.at[plane], lhs_ref.at[plane], band_ref.at[plane], blend_ref[step])
+            new = advance(taps, field_ref.at[plane], band_ref.at[plane], blend_ref[step])
             source_ref[step, plane] = new
             if step + 1 < depth:
                 field_ref[plane, ROW_PAD : ROW_PAD + nx] = new
 
 
-def migrate_kernel(dims, recv_ref, band_ref, blend_ref, source_ref, out_ref, grid_ref, field_ref, lhs_ref, image_ref):
+def migrate_kernel(dims, recv_ref, band_ref, blend_ref, source_ref, out_ref, grid_ref, field_ref, image_ref):
     groups, halves, copies, xw, taps, scale, folded = dims
     depth, nx, width = blend_ref.shape
     ny = width // 2
@@ -210,31 +209,42 @@
         folds = LANES // xw
         half_rows = ny // halves
         lane = lane_iota((SUB, LANES))
-        for half in range(halves):
-            blocks = [recv_ref[group * halves + half].astype(F32) for group in range(groups)]
-            for item in range(2 * FPD):
-                for low in range(folds):
-                    kept = None
-                    for group in range(groups):
-                        piece = blocks[group][item * SUB : (item + 1) * SUB]
-                        shift = ((group - low) * xw) % LANES
-                        if shift:
-                            piece = pltpu.roll(piece, shift, 1)
-                        kept = piece if kept is None else jnp.where(lane // xw == group, piece, kept)
-                    grid_ref[pl.ds(item * ny + half * half_rows + low, SUB, stride=folds), :] = kept
+        blocks = [recv_ref[block].astype(F32) for block in range(groups * halves)]
     else:
         grid_ref[...] = recv_ref[...].astype(F32)
+    steps = [None] * depth
+
+    def gather(plane):
+        if folded:
+            for half in range(halves):
+                for item in range(2 * plane, 2 * plane + 2):
+                    for low in range(folds):
+                        kept = None
+                        for group in range(groups):
+                            piece = blocks[group * halves + half][item * SUB : (item + 1) * SUB]
+                            shift = ((group - low) * xw) % LANES
+                            if shift:
+                                piece = pltpu.roll(piece, shift, 1)
+                            kept = piece if kept is None else jnp.where(lane // xw == group, piece, kept)
+                        grid_ref[pl.ds(item * ny + half * half_rows + low, SUB, stride=folds), :] = kept
+        set_field(field_ref.at[plane], grid_ref[plane * width : (plane + 1) * width].T)
+
+    def move(step, plane):
+        new = advance(taps, field_ref.at[plane], band_ref.at[plane], blend_ref[step])
+        if step + 1 < depth:
+            field_ref[plane, ROW_PAD : ROW_PAD + nx] = new
+        term = source_ref[step, plane] * new
+        steps[step] = term if steps[step] is None else steps[step] + term
+
+    gather(0)
     for plane in range(FPD):
-        set_field(field_ref.at[plane], grid_ref[plane * width : (plane + 1) * width].T)
+        if plane + 1 < FPD:
+            gather(plane + 1)
+        move(0, plane)
     for step in range(depth):
-        total = None
-        for plane in range(FPD):
-            new = advance(taps, field_ref.at[plane], lhs_ref.at[plane], band_ref.at[plane], blend_ref[step])
-            if step + 1 < depth:
-                field_ref[plane, ROW_PAD : ROW_PAD + nx] = new
-            term = source_ref[step, plane] * new
-            total = term if total is None else total + term
-        turned = total.T
+        for plane in range(FPD if step else 0):
+            move(step, plane)
+        turned = steps[step].T
         image_ref[pl.ds(step, ny, stride=depth), :] = (turned[:ny] + turned[ny:]) * scale
     share = ny // (groups * halves) * depth
     for group in range(groups):
@@ -325,7 +335,6 @@
 
     table = table.reshape(nref * taps * taps * 2, nbin)
     band_shape = (FPD, taps * 2 * ny, nref * 2 * ny)
-    lhs = pltpu.VMEM((FPD, nx, taps * 2 * ny), BF16)
     field = pltpu.VMEM((FPD, nx + 2 * ROW_PAD, 2 * ny), F32)
     band, blend, source = pl.pallas_call(
         functools.partial(source_kernel, taps, nref, depth, halves),
@@ -344,7 +353,6 @@
             pltpu.VMEM((depth + 1, ny, nx), F32),
             pltpu.VMEM((SUB, LANES), F32),
             field,
-            lhs,
             pltpu.SemaphoreType.DMA((1 + 2 * halves,)),
         ],
         compiler_params=params,
@@ -362,7 +370,6 @@
         scratch_shapes=[
             pltpu.VMEM((items * ny, nx), F32),
             field,
-            lhs,
             pltpu.VMEM((ny * depth, nx), F32),
         ],
         compiler_params=params,

time: 28.4 us -> 28.3 us (level)
  transfers between devices with their start and end apart: 3 -> 3, of which waited for: 1 -> 1; matrix products, arithmetic and copies ran while one was open for 0% -> 0% of each run, Pallas kernels for 21% -> 20%
where the time goes in v3:
time: 28.3 us; the launch traced here: 27.9 us
  blocking collectives  9.94 us (35%)
  Pallas kernels  6.88 us (24%)
  starting transfers between devices  6.85 us (24%)
  waiting for transfers between devices  3.4 us (12%)
  other arithmetic  0.62 us (2%)
    all_to_all x1, blocking collectives, body(): terms = lax.all_to_all(terms, ('freq', 'half', 'shot'), 0, 0, tiled=True)  9.94 us
    all_to_all x1, starting transfers between devices, body(): recv = lax.all_to_all(send, ('freq', 'half'), 0, 0, tiled=True)  6.34 us
    all_to_all x1, waiting for transfers between devices, body(): recv = lax.all_to_all(send, ('freq', 'half'), 0, 0, tiled=True)  3.4 us
    pallas_call x1, Pallas kernels, body(): pl.pallas_call(functools.partial(send_kernel, groups, folded), out_shape=...  2.84 us
    pallas_call x1, Pallas kernels, body(): pl.pallas_call(functools.partial(source_kernel, taps, nref, depth, halves...  2.78 us
    pallas_call x1, Pallas kernels, body(): pl.pallas_call(functools.partial(migrate_kernel, (groups, halves, copies,...  1.26 us
    reduce_sum x1, other arithmetic, body(): return jnp.sum(terms.astype(F32), axis=0).reshape(1, share, depth, nx)  0.62 us
  transfers between devices with their start and end apart: 3, of which 1 were waited for; matrix products, arithmetic and copies ran while one was open for 0% of the time, Pallas kernels for 20%

profile of v3, /device:TPU:0, one launch (start us, length us, event | category | flops | bytes accessed | tf_op | source)
XLA Modules:
  0.0 27.9 jit_solution(597010846352334964)
XLA Ops:
  0.0 0.5 %collective-permute-start = (s32[2,32,128]{2,1,0:T(8,128)}, s32[2,32,128]{2,1,0:T(8,128)S(1)}, u32[]{:S(2)}, u32[]{:S(2)}) collective-permute-start(s32[2,32,128]{2,1,0:T(8,128)} %refs_0_), channel_id=1, source_target_pairs={{1,0},{0,1},{3,2},{2,3},{5,4},{4,5},{7,6},{6,7},{9,8},{8,9},{11,10... | collective-permute-start | bytes 98312 | tf_op jit(solution)/shard_map/ppermute | solution.py:273
  0.5 0.1 collective-permute-start.1
  0.5 2.8 %send_blocks.1 = (bf16[4,2,48,128]{3,2,1,0:T(8,128)(2,1)}, s32[8,128]{1,0:T(8,128)S(1)}, f32[8,128]{1,0:T(8,128)S(1)}, bf16[2,13,13,2,256]{4,3,2,1,0:T(2,128)(2,1)S(1)}) custom-call(s32[4,6]{1,0:T(4,128)} %plan_hbm.1, s32[4]{0:T(128)} %counts_hbm.1, f32[2,256]{1,0:T(2,128)} %bitcast.8, bf16[2,13,13,2,256]{4,3,2,1,0:T(2,128)(2,1)} %bitcast.7, ...), custom_call_target="tpu_custom_call" | custom-call | flops 67108864 | bytes 4194304 | tf_op jit(solution)/shard_map/send_blocks/pallas_call | solution.py:301
  3.4 0.0 collective-permute-done.1.refs_3_
  3.4 0.0 copy-start.1
  3.4 0.0 collective-permute-done.refs_1_
  3.4 0.0 copy-start
  3.4 6.3 %all-to-all-start = ((bf16[8,48,128]{2,1,0:T(8,128)(2,1)}), bf16[8,48,128]{2,1,0:T(8,128)(2,1)S(1)}, u32[]{:S(2)}, u32[]{:S(2)}) async-start(bf16[8,48,128]{2,1,0:T(8,128)(2,1)} %bitcast.3), calls=%async_computation | async-start | bytes 196608 | tf_op jit(solution)/shard_map/all_to_all | solution.py:329
  9.7 0.1 reshape.14.filt_ref
  9.9 0.0 copy-done
  9.9 0.0 copy-done.1
  9.9 2.8 %source_fields.1 = (bf16[3,1664,256]{2,1,0:T(8,128)(2,1)S(1)}, f32[2,128,128]{2,1,0:T(8,128)S(1)}, f32[2,3,128,128]{3,2,1,0:T(8,128)S(1)}) custom-call(s32[8,128]{1,0:T(8,128)S(1)} %get-tuple-element.21.own_ref, f32[8,128]{1,0:T(8,128)S(1)} %get-tuple-element.22.wave_ref, bf16[676,256]{1,0:T(8,128)(2,1)S(1)} %reshape.14.filt_ref, f32[1,64]{1,0:T(1,128)} %bitcast.9, ...), custom_call_target="tpu_custom_call" | custom-call | flops 4000000000 | bytes 10000000 | tf_op jit(solution)/shard_map/source_fields/pallas_call | solution.py:339
  12.7 3.4 %all-to-all-done.recv_ref = bf16[8,48,128]{2,1,0:T(8,128)(2,1)S(1)} async-done(((bf16[8,48,128]{2,1,0:T(8,128)(2,1)}), bf16[8,48,128]{2,1,0:T(8,128)(2,1)S(1)}, u32[]{:S(2)}, u32[]{:S(2)}) %all-to-all-start) | async-done | bytes 98336 | tf_op jit(solution)/shard_map/all_to_all | solution.py:329
  16.1 1.3 %migrate.1 = bf16[16,16,128]{2,1,0:T(8,128)(2,1)S(1)} custom-call(bf16[8,48,128]{2,1,0:T(8,128)(2,1)S(1)} %all-to-all-done.recv_ref, bf16[3,1664,256]{2,1,0:T(8,128)(2,1)S(1)} %get-tuple-element.28.band_ref, f32[2,128,128]{2,1,0:T(8,128)S(1)} %get-tuple-element.29.blend_ref, f32[2,3,128,128]{3,2,1,0:T(8,128)S(1)} %get-tuple-element.30.source_ref), custom_call_target="tpu_custom_call" | custom-call | tf_op jit(solution)/shard_map/migrate/pallas_call | solution.py:365
  17.3 9.9 %all_to_all.10 = bf16[16,16,128]{2,1,0:T(8,128)(2,1)S(1)} all-to-all(bf16[16,16,128]{2,1,0:T(8,128)(2,1)S(1)} %migrate.1), channel_id=1, replica_groups=mesh['group'=2,'freq'=4,'shot'=2,'half'=2] {'freq','half','shot'}, dimensions={0} | all-to-all | bytes 131072 | tf_op jit(solution)/shard_map/all_to_all | solution.py:378
  27.3 0.6 %convert_reduce_fusion = f32[16,128]{1,0:T(8,128)} fusion(bf16[16,16,128]{2,1,0:T(8,128)(2,1)S(1)} %all_to_all.10), kind=kLoop, calls=%fused_computation | loop fusion | flops 63488 | bytes 73728 | tf_op jit(solution)/shard_map/reduce_sum | solution.py:379
Async XLA Ops:
  0.0 3.4 %collective-permute-start = (s32[2,32,128]{2,1,0:T(8,128)}, s32[2,32,128]{2,1,0:T(8,128)S(1)}, u32[]{:S(2)}, u32[]{:S(2)}) collective-permute-start(s32[2,32,128]{2,1,0:T(8,128)} %refs_0_), channel_id=1, source_target_pairs={{1,0},{0,1},{3,2},{2,3},{5,4},{4,5},{7,6},{6,7},{9,8},{8,9},{11,10... | collective-permute-start | bytes 98312 | tf_op jit(solution)/shard_map/ppermute | solution.py:273
  0.5 2.9 %collective-permute-start.1 = (bf16[2,32,128]{2,1,0:T(8,128)(2,1)}, bf16[2,32,128]{2,1,0:T(8,128)(2,1)S(1)}, u32[]{:S(2)}, u32[]{:S(2)}) collective-permute-start(bf16[2,32,128]{2,1,0:T(8,128)(2,1)} %refs_2_), channel_id=1, source_target_pairs={{1,0},{0,1},{3,2},{2,3},{5,4},{4,5},{7,6},{6,7},{9,8},{8,9},{11,10... | collective-permute-start | bytes 49160 | tf_op jit(solution)/shard_map/ppermute | solution.py:273
  3.4 6.5 %copy-start.1 = (bf16[2,32,128]{2,1,0:T(8,128)(2,1)}, bf16[2,32,128]{2,1,0:T(8,128)(2,1)S(1)}, u32[]{:S(2)}) copy-start(bf16[2,32,128]{2,1,0:T(8,128)(2,1)S(1)} %collective-permute-done.1.refs_3_) | copy-start | bytes 49156
  3.4 6.5 %copy-start = (s32[2,32,128]{2,1,0:T(8,128)}, s32[2,32,128]{2,1,0:T(8,128)S(1)}, u32[]{:S(2)}) copy-start(s32[2,32,128]{2,1,0:T(8,128)S(1)} %collective-permute-done.refs_1_) | copy-start | bytes 98308
  3.4 12.7 %all-to-all-start = ((bf16[8,48,128]{2,1,0:T(8,128)(2,1)}), bf16[8,48,128]{2,1,0:T(8,128)(2,1)S(1)}, u32[]{:S(2)}, u32[]{:S(2)}) async-start(bf16[8,48,128]{2,1,0:T(8,128)(2,1)} %bitcast.3), calls=%async_computation | async-start | bytes 196608 | tf_op jit(solution)/shard_map/all_to_all | solution.py:329

commit v4 on v3

--- a/solution.py
+++ b/solution.py
@@ -12,7 +12,6 @@
 LANES = 128
 SUB = 8
 ROW_PAD = 8
-CHUNKS = 2
 VMEM_BYTES = 40 * 1024 * 1024
 BF16 = jnp.bfloat16
 F32 = jnp.float32
@@ -59,61 +58,49 @@
     return lax.dot_general(dft, block, (((1,), (1,)), ((), ())), preferred_element_type=F32)
 
 
-def send_kernel(
-    groups, folded, plan_hbm, counts_hbm, wav_hbm, filt_hbm, rec_hbm, out_ref, own_ref, wave_ref, filt_ref,
-    plan_ref, counts_ref, wav_ref, bins_ref, dft_ref, rec_ref, tmp_ref, small_sems, sems,
+def prepare_kernel(
+    groups, plan_hbm, counts_hbm, wav_hbm, filt_hbm, dft_ref, own_ref, wave_ref, filt_ref,
+    plan_ref, counts_ref, wav_ref, bins_ref, sems,
 ):
-    shots, cells, nt = rec_hbm.shape
-    part = cells // CHUNKS
+    nt = dft_ref.shape[1]
+    filters = pltpu.make_async_copy(filt_hbm, filt_ref, sems.at[3])
     small = [
-        pltpu.make_async_copy(plan_hbm, plan_ref, small_sems.at[0]),
-        pltpu.make_async_copy(counts_hbm, counts_ref, small_sems.at[1]),
-        pltpu.make_async_copy(wav_hbm, wav_ref, small_sems.at[2]),
+        pltpu.make_async_copy(plan_hbm, plan_ref, sems.at[0]),
+        pltpu.make_async_copy(counts_hbm, counts_ref, sems.at[1]),
+        pltpu.make_async_copy(wav_hbm, wav_ref, sems.at[2]),
     ]
-    for copy in small:
+    for copy in small + [filters]:
         copy.start()
-    copies = []
-    for shot in range(shots):
-        for chunk in range(CHUNKS):
-            rows = pl.ds(chunk * part, part)
-            copy = pltpu.make_async_copy(
-                rec_hbm.at[shot, rows], rec_ref.at[shot, rows], sems.at[shot * CHUNKS + chunk]
-            )
-            copy.start()
-            copies.append(copy)
-    filters = pltpu.make_async_copy(filt_hbm, filt_ref, small_sems.at[3])
-    filters.start()
     for copy in small:
         copy.wait()
     list_bins(plan_ref, counts_ref, bins_ref)
-    for group in range(groups):
-        dft_ref[group * SUB : (group + 1) * SUB] = dft_rows(bins_ref, group, nt)
-    dft = dft_ref[...].astype(BF16)
+    for pair in range(0, groups, 2):
+        both = [dft_rows(bins_ref, group, nt) for group in range(pair, min(pair + 2, groups))]
+        dft_ref[pair * SUB : (pair + len(both)) * SUB] = jnp.concatenate(both, axis=0).astype(BF16)
     first = lax.axis_index("freq") * FPD
     lane = lane_iota((1, LANES))
     for plane in range(FPD):
         bin_id = bins_ref[first + plane]
         own_ref[plane : plane + 1] = jnp.full((1, LANES), bin_id, jnp.int32)
         wave_ref[plane : plane + 1] = jnp.where(lane < LANES // 2, wav_ref[0, bin_id], wav_ref[1, bin_id])
+    filters.wait()
+
+
+def send_kernel(groups, folded, dft_ref, rec_ref, out_ref, tmp_ref):
+    shots, cells, _ = rec_ref.shape
+    dft = dft_ref[...]
     for shot in range(shots):
-        for chunk in range(CHUNKS):
-            copies[shot * CHUNKS + chunk].wait()
-            out = transform(dft, rec_ref[shot, chunk * part : (chunk + 1) * part])
-            if not folded:
-                out_ref[shot, :, chunk * part : (chunk + 1) * part] = out.astype(BF16)
-                continue
-            highs = part // LANES
-            for group in range(groups):
-                base = (group * shots + shot) * SUB * SUB + chunk * highs
-                for high in range(highs):
-                    tmp_ref[pl.ds(base + high, SUB, stride=SUB), :] = out[
-                        group * SUB : (group + 1) * SUB, high * LANES : (high + 1) * LANES
-                    ]
-        if folded:
-            for group in range(groups):
-                base = (group * shots + shot) * SUB * SUB
-                out_ref[group, shot] = tmp_ref[base : base + 2 * FPD * SUB].astype(BF16)
-    filters.wait()
+        out = transform(dft, rec_ref[shot])
+        if not folded:
+            out_ref[shot] = out.astype(BF16)
+            continue
+        for group in range(groups):
+            base = (group * shots + shot) * SUB * SUB
+            for high in range(SUB):
+                tmp_ref[pl.ds(base + high, SUB, stride=SUB), :] = out[
+                    group * SUB : (group + 1) * SUB, high * LANES : (high + 1) * LANES
+                ]
+            out_ref[group, shot] = tmp_ref[base : base + 2 * FPD * SUB].astype(BF16)
 
 
 def make_bands(taps, nref, ny, picked_ref, band_ref):
@@ -146,13 +133,37 @@
     field_ref[ROW_PAD + rows :] = jnp.zeros((ROW_PAD, width), F32)
 
 
-def advance(taps, field_ref, band_ref, blend):
-    rows, width = blend.shape
+def shifted(taps, field_ref):
     first = ROW_PAD - taps // 2
+    rows = field_ref.shape[0] - 2 * ROW_PAD
     pieces = [field_ref[pl.ds(first + tap, rows), :].astype(BF16) for tap in range(taps)]
-    both = jnp.dot(jnp.concatenate(pieces, axis=1), band_ref[...], preferred_element_type=F32)
+    return jnp.concatenate(pieces, axis=1)
+
+
+def advance(left, band_ref, blend):
+    width = blend.shape[1]
+    both = jnp.dot(left, band_ref[...], preferred_element_type=F32)
     low, high = both[:, :width], both[:, width:]
     return (low + blend * (high - low)).astype(BF16).astype(F32)
+
+
+def run_steps(taps, depth, field_ref, band_ref, blend_ref, prepare, use):
+    rows = field_ref.shape[1] - 2 * ROW_PAD
+    order = [(step, plane) for step in range(depth) for plane in range(FPD)]
+    prepare(0)
+    left = shifted(taps, field_ref.at[0])
+    for at, (step, plane) in enumerate(order):
+        follow = None
+        if at + 1 < len(order):
+            after = order[at + 1][1]
+            if order[at + 1][0] == 0:
+                prepare(after)
+            follow = shifted(taps, field_ref.at[after])
+        new = advance(left, band_ref.at[plane], blend_ref[step])
+        if step + 1 < depth:
+            field_ref[plane, ROW_PAD : ROW_PAD + rows] = new
+        use(step, plane, new)
+        left = follow
 
 
 def source_kernel(taps, nref, depth, halves, own_ref, wave_ref, filt_ref, table_hbm, *refs):
@@ -171,7 +182,7 @@
     nbin = filt_ref.shape[1]
     for plane in range(FPD):
         hot = jnp.where(row_iota((nbin, LANES)) == own_ref[plane : plane + 1], 1.0, 0.0).astype(BF16)
-        picked_ref[plane] = jnp.dot(filt_ref[...], hot, preferred_element_type=F32)
+        picked_ref[plane, : filt_ref.shape[0]] = jnp.dot(filt_ref[...], hot, preferred_element_type=F32)
     for plane in range(FPD - 1):
         make_bands(taps, nref, ny, picked_ref.at[plane], band_ref.at[plane])
     for copy in copies:
@@ -190,15 +201,15 @@
         blend_ref[step] = jnp.concatenate(pieces + pieces, axis=0).T
     pattern = grid_ref[depth]
     pattern = jnp.concatenate([pattern, pattern], axis=0).T
-    for plane in range(FPD):
+    make_bands(taps, nref, ny, picked_ref.at[FPD - 1], band_ref.at[FPD - 1])
+
+    def start(plane):
         set_field(field_ref.at[plane], (pattern * wave_ref[plane : plane + 1]).astype(BF16).astype(F32))
-    make_bands(taps, nref, ny, picked_ref.at[FPD - 1], band_ref.at[FPD - 1])
-    for step in range(depth):
-        for plane in range(FPD):
-            new = advance(taps, field_ref.at[plane], band_ref.at[plane], blend_ref[step])
-            source_ref[step, plane] = new
-            if step + 1 < depth:
-                field_ref[plane, ROW_PAD : ROW_PAD + nx] = new
+
+    def keep(step, plane, new):
+        source_ref[step, plane] = new
+
+    run_steps(taps, depth, field_ref, band_ref, blend_ref, start, keep)
 
 
 def migrate_kernel(dims, recv_ref, band_ref, blend_ref, source_ref, out_ref, grid_ref, field_ref, image_ref):
@@ -211,7 +222,7 @@
         lane = lane_iota((SUB, LANES))
         blocks = [recv_ref[block].astype(F32) for block in range(groups * halves)]
     else:
-        grid_ref[...] = recv_ref[...].astype(F32)
+        grid_ref[: recv_ref.shape[0]] = recv_ref[...].astype(F32)
     steps = [None] * depth
 
     def gather(plane):
@@ -229,23 +240,14 @@
                         grid_ref[pl.ds(item * ny + half * half_rows + low, SUB, stride=folds), :] = kept
         set_field(field_ref.at[plane], grid_ref[plane * width : (plane + 1) * width].T)
 
-    def move(step, plane):
-        new = advance(taps, field_ref.at[plane], band_ref.at[plane], blend_ref[step])
-        if step + 1 < depth:
-            field_ref[plane, ROW_PAD : ROW_PAD + nx] = new
+    def correlate(step, plane, new):
         term = source_ref[step, plane] * new
         steps[step] = term if steps[step] is None else steps[step] + term
-
-    gather(0)
-    for plane in range(FPD):
-        if plane + 1 < FPD:
-            gather(plane + 1)
-        move(0, plane)
-    for step in range(depth):
-        for plane in range(FPD if step else 0):
-            move(step, plane)
-        turned = steps[step].T
-        image_ref[pl.ds(step, ny, stride=depth), :] = (turned[:ny] + turned[ny:]) * scale
+        if plane == FPD - 1:
+            turned = steps[step].T
+            image_ref[pl.ds(step, ny, stride=depth), :] = (turned[:ny] + turned[ny:]) * scale
+
+    run_steps(taps, depth, field_ref, band_ref, blend_ref, gather, correlate)
     share = ny // (groups * halves) * depth
     for group in range(groups):
         for half in range(halves):
@@ -290,40 +292,45 @@
     bins = pltpu.SMEM((groups * FPD + cap,), jnp.int32)
     params = pltpu.CompilerParams(vmem_limit_bytes=VMEM_BYTES)
 
-    classes = from_halves(vel_index, halves)
-    patterns = from_halves(source_pattern, halves)
 
     if folded:
         send_shape = (groups, shots, items * SUB, LANES)
     else:
         send_shape = (shots, groups * SUB, cells)
     table = filters.transpose(0, 2, 3, 1, 4)
-    send, own, wave, table = pl.pallas_call(
-        functools.partial(send_kernel, groups, folded),
+    dft, own, wave, table = pl.pallas_call(
+        functools.partial(prepare_kernel, groups),
         out_shape=[
-            jax.ShapeDtypeStruct(send_shape, BF16),
+            jax.ShapeDtypeStruct((groups * SUB, nt), BF16),
             jax.ShapeDtypeStruct((SUB, LANES), jnp.int32),
             jax.ShapeDtypeStruct((SUB, LANES), F32),
             jax.ShapeDtypeStruct(table.shape, BF16),
         ],
-        in_specs=[hbm()] * 5,
+        in_specs=[hbm()] * 4,
         out_specs=[vmem()] * 4,
         scratch_shapes=[
             pltpu.SMEM(freq_plan.shape, jnp.int32),
             pltpu.SMEM(counts.shape, jnp.int32),
             pltpu.SMEM((2, nbin), F32),
             bins,
-            pltpu.VMEM((groups * SUB, nt), F32),
-            pltpu.VMEM((shots, cells, nt), BF16),
-            pltpu.VMEM((groups * shots * SUB * SUB, LANES), F32),
             pltpu.SemaphoreType.DMA((4,)),
-            pltpu.SemaphoreType.DMA((shots * CHUNKS,)),
         ],
         compiler_params=params,
-        cost_estimate=pl.CostEstimate(flops=2 * groups * SUB * records.size, bytes_accessed=4 * records.size, transcendentals=0),
+        cost_estimate=pl.CostEstimate(flops=3 * 10**9, bytes_accessed=4 * 10**6, transcendentals=0),
+        name="prepare",
+    )(*pinned(freq_plan, counts, wavelet.T, table))
+    own, vel_index, source_pattern = lax.optimization_barrier((own, vel_index, source_pattern))
+    classes = from_halves(vel_index, halves)
+    patterns = from_halves(source_pattern, halves)
+    send = pl.pallas_call(
+        functools.partial(send_kernel, groups, folded),
+        out_shape=jax.ShapeDtypeStruct(send_shape, BF16),
+        in_specs=[vmem()] * 2,
+        out_specs=vmem(),
+        scratch_shapes=[pltpu.VMEM((groups * shots * SUB * SUB + SUB, LANES), F32)],
+        compiler_params=params,
         name="send_blocks",
-    )(*pinned(freq_plan, counts, wavelet.T, table, records.reshape(shots, cells, nt)))
-    send, classes, patterns, table = lax.optimization_barrier((send, classes, patterns, table))
+    )(dft, records.reshape(shots, cells, nt))
     if folded:
         send = send.reshape(groups * halves, items * SUB, LANES)
         recv = lax.all_to_all(send, ("freq", "half"), 0, 0, tiled=True)
@@ -343,13 +350,13 @@
             jax.ShapeDtypeStruct((depth, nx, 2 * ny), F32),
             jax.ShapeDtypeStruct((depth, FPD, nx, 2 * ny), F32),
         ],
-        in_specs=[vmem()] * 3 + [hbm()] * (1 + 2 * halves),
+        in_specs=[vmem()] * 3 + [hbm()] * (2 + halves) + [pl.BlockSpec(memory_space=pl.ANY)] * (halves - 1),
         out_specs=[vmem()] * 3,
         scratch_shapes=[
             pltpu.VMEM((halves,) + vel_index.shape, jnp.int32),
             pltpu.VMEM((halves,) + source_pattern.shape, BF16),
             pltpu.VMEM((1,) + vel_table.shape, F32),
-            pltpu.VMEM((FPD, table.shape[0], LANES), F32),
+            pltpu.VMEM((FPD, (table.shape[0] + 2 * taps + SUB) // SUB * SUB + 2 * SUB, LANES), F32),
             pltpu.VMEM((depth + 1, ny, nx), F32),
             pltpu.VMEM((SUB, LANES), F32),
             field,
@@ -358,7 +365,7 @@
         compiler_params=params,
         cost_estimate=pl.CostEstimate(flops=4 * 10**9, bytes_accessed=10**7, transcendentals=0),
         name="source_fields",
-    )(own, wave, table, *pinned(vel_table[None], *classes, *patterns))
+    )(own, wave, table, *pinned(vel_table[None], *classes, patterns[0]), *patterns[1:])
 
     scale = 1.0 / math.sqrt(FPD * groups * shots * copies)
     share = ny // (groups * halves)
@@ -368,9 +375,9 @@
         in_specs=[vmem()] * 4,
         out_specs=vmem(),
         scratch_shapes=[
-            pltpu.VMEM((items * ny, nx), F32),
+            pltpu.VMEM((items * ny + SUB, nx), F32),
             field,
-            pltpu.VMEM((ny * depth, nx), F32),
+            pltpu.VMEM((ny * depth + SUB, nx), F32),
         ],
         compiler_params=params,
         name="migrate",

time: 28.3 us -> 27.9 us (0.986)
  Pallas kernels: 6.88 us -> 5.97 us
  local copies, waits for them, and re-layouts: 0.14 us -> 0.74 us
    pallas_call x1, Pallas kernels: 2.84 us -> 1.37 us  [body(): pl.pallas_call(functools.partial(send_kernel, groups, folded), out_shape=...]
    pallas_call x0 -> x1, Pallas kernels: none -> 1.17 us  [body(): pl.pallas_call(functools.partial(prepare_kernel, groups), out_shape=[jax....]
    pallas_call x1, Pallas kernels: 2.78 us -> 2.17 us  [body(): pl.pallas_call(functools.partial(source_kernel, taps, nref, depth, halves...]
    unnamed x4 -> x8, local copies, waits for them, and re-layouts: 0.01 us -> 0.61 us
  transfers between devices with their start and end apart: 3 -> 3, of which waited for: 1 -> 1; matrix products, arithmetic and copies ran while one was open for 0% -> 0% of each run, Pallas kernels for 20% -> 13%
where the time goes in v4:
time: 27.9 us; the launch traced here: 27.6 us
  blocking collectives  9.94 us (36%)
  starting transfers between devices  6.9 us (25%)
  Pallas kernels  5.97 us (21%)
  waiting for transfers between devices  3.41 us (12%)
  local copies, waits for them, and re-layouts  0.74 us (3%)
  other arithmetic  0.62 us (2%)
    all_to_all x1, blocking collectives, body(): terms = lax.all_to_all(terms, ('freq', 'half', 'shot'), 0, 0, tiled=True)  9.94 us
    all_to_all x1, starting transfers between devices, body(): recv = lax.all_to_all(send, ('freq', 'half'), 0, 0, tiled=True)  6.3 us
    all_to_all x1, waiting for transfers between devices, body(): recv = lax.all_to_all(send, ('freq', 'half'), 0, 0, tiled=True)  3.4 us
    pallas_call x1, Pallas kernels, body(): pl.pallas_call(functools.partial(source_kernel, taps, nref, depth, halves...  2.17 us
    pallas_call x1, Pallas kernels, body(): pl.pallas_call(functools.partial(send_kernel, groups, folded), out_shape=...  1.37 us
    pallas_call x1, Pallas kernels, body(): pl.pallas_call(functools.partial(migrate_kernel, (groups, halves, copies,...  1.27 us
    pallas_call x1, Pallas kernels, body(): pl.pallas_call(functools.partial(prepare_kernel, groups), out_shape=[jax....  1.17 us
    reduce_sum x1, other arithmetic, body(): return jnp.sum(terms.astype(F32), axis=0).reshape(1, share, depth, nx)  0.62 us
  transfers between devices with their start and end apart: 3, of which 1 were waited for; matrix products, arithmetic and copies ran while one was open for 0% of the time, Pallas kernels for 13%

profile of v4, /device:TPU:0, one launch (start us, length us, event | category | flops | bytes accessed | tf_op | source)
XLA Modules:
  0.0 27.6 jit_solution(1560045300246377231)
XLA Ops:
  0.0 0.0 copy-start.1
  0.0 0.0 copy-start.3
  0.0 0.0 copy-start
  0.0 1.2 %prepare.1 = (bf16[32,512]{1,0:T(8,128)(2,1)S(1)}, s32[8,128]{1,0:T(8,128)S(1)}, f32[8,128]{1,0:T(8,128)S(1)}, bf16[2,13,13,2,256]{4,3,2,1,0:T(2,128)(2,1)S(1)}) custom-call(s32[4,6]{1,0:T(4,128)} %plan_hbm.1, s32[4]{0:T(128)} %counts_hbm.1, f32[2,256]{1,0:T(2,128)} %bitcast.8, bf16[2,13,13,2,256]{4,3,2,1,0:T(2,128)(2,1)} %bitcast.7), custom_call_target="tpu_custom_call" | custom-call | flops 3000000000 | bytes 4000000 | tf_op jit(solution)/shard_map/prepare/pallas_call | solution.py:301
  1.2 0.0 copy-done.1
  1.2 0.5 %collective-permute-start = (s32[2,32,128]{2,1,0:T(8,128)S(1)}, s32[2,32,128]{2,1,0:T(8,128)S(1)}, u32[]{:S(2)}, u32[]{:S(2)}) collective-permute-start(s32[2,32,128]{2,1,0:T(8,128)S(1)} %copy-done.1), channel_id=1, source_target_pairs={{1,0},{0,1},{3,2},{2,3},{5,4},{4,5},{7,6},{6,7},{9,8},{8,9},{11,10... | collective-permute-start | bytes 98312 | tf_op jit(solution)/shard_map/ppermute | solution.py:275
  1.7 0.0 copy-done.3
  1.7 0.1 collective-permute-start.1
  1.8 0.0 copy-done
  1.8 1.4 %send_blocks.1 = bf16[4,2,48,128]{3,2,1,0:T(8,128)(2,1)} custom-call(bf16[32,512]{1,0:T(8,128)(2,1)S(1)} %get-tuple-element.15.dft_ref, bf16[2,1024,512]{2,1,0:T(8,128)(2,1)S(1)} %bitcast.6), custom_call_target="tpu_custom_call" | custom-call | tf_op jit(solution)/shard_map/send_blocks/pallas_call | solution.py:325
  3.2 6.3 %all-to-all-start = ((bf16[8,48,128]{2,1,0:T(8,128)(2,1)}), bf16[8,48,128]{2,1,0:T(8,128)(2,1)S(1)}, u32[]{:S(2)}, u32[]{:S(2)}) async-start(bf16[8,48,128]{2,1,0:T(8,128)(2,1)} %bitcast.3), calls=%async_computation | async-start | bytes 196608 | tf_op jit(solution)/shard_map/all_to_all | solution.py:336
  9.5 0.1 reshape.14.filt_ref
  9.6 0.0 collective-permute-done.1.refs_3_
  9.6 0.0 collective-permute-done.refs_1_
  9.6 0.0 copy-start.2
  9.6 0.6 %copy-done.2 = s32[2,32,128]{2,1,0:T(8,128)} copy-done((s32[2,32,128]{2,1,0:T(8,128)}, s32[2,32,128]{2,1,0:T(8,128)S(1)}, u32[]{:S(2)}) %copy-start.2) | copy-done | bytes 32792
  10.2 2.2 %source_fields.1 = (bf16[3,1664,256]{2,1,0:T(8,128)(2,1)S(1)}, f32[2,128,128]{2,1,0:T(8,128)S(1)}, f32[2,3,128,128]{3,2,1,0:T(8,128)S(1)}) custom-call(s32[8,128]{1,0:T(8,128)S(1)} %get-tuple-element.17.own_ref, f32[8,128]{1,0:T(8,128)S(1)} %get-tuple-element.18.wave_ref, bf16[676,256]{1,0:T(8,128)(2,1)S(1)} %reshape.14.filt_ref, f32[1,64]{1,0:T(1,128)} %bitcast.9, ...), custom_call_target="tpu_custom_call" | custom-call | flops 4000000000 | bytes 10000000 | tf_op jit(solution)/shard_map/source_fields/pallas_call | solution.py:346
  12.4 3.4 %all-to-all-done.recv_ref = bf16[8,48,128]{2,1,0:T(8,128)(2,1)S(1)} async-done(((bf16[8,48,128]{2,1,0:T(8,128)(2,1)}), bf16[8,48,128]{2,1,0:T(8,128)(2,1)S(1)}, u32[]{:S(2)}, u32[]{:S(2)}) %all-to-all-start) | async-done | bytes 98336 | tf_op jit(solution)/shard_map/all_to_all | solution.py:336
  15.8 1.3 %migrate.1 = bf16[16,16,128]{2,1,0:T(8,128)(2,1)S(1)} custom-call(bf16[8,48,128]{2,1,0:T(8,128)(2,1)S(1)} %all-to-all-done.recv_ref, bf16[3,1664,256]{2,1,0:T(8,128)(2,1)S(1)} %get-tuple-element.22.band_ref, f32[2,128,128]{2,1,0:T(8,128)S(1)} %get-tuple-element.23.blend_ref, f32[2,3,128,128]{3,2,1,0:T(8,128)S(1)} %get-tuple-element.24.source_ref), custom_call_target="tpu_custom_call" | custom-call | tf_op jit(solution)/shard_map/migrate/pallas_call | solution.py:372
  17.1 9.9 %all_to_all.10 = bf16[16,16,128]{2,1,0:T(8,128)(2,1)S(1)} all-to-all(bf16[16,16,128]{2,1,0:T(8,128)(2,1)S(1)} %migrate.1), channel_id=1, replica_groups=mesh['group'=2,'freq'=4,'shot'=2,'half'=2] {'freq','half','shot'}, dimensions={0} | all-to-all | bytes 131072 | tf_op jit(solution)/shard_map/all_to_all | solution.py:385
  27.0 0.6 %convert_reduce_fusion = f32[16,128]{1,0:T(8,128)} fusion(bf16[16,16,128]{2,1,0:T(8,128)(2,1)S(1)} %all_to_all.10), kind=kLoop, calls=%fused_computation | loop fusion | flops 63488 | bytes 73728 | tf_op jit(solution)/shard_map/reduce_sum | solution.py:386
Async XLA Ops:
  0.0 1.2 %copy-start.1 = (s32[2,32,128]{2,1,0:T(8,128)S(1)}, s32[2,32,128]{2,1,0:T(8,128)}, u32[]{:S(2)}) copy-start(s32[2,32,128]{2,1,0:T(8,128)} %refs_0_) | copy-start | bytes 98308
  0.0 1.7 %copy-start.3 = (bf16[2,32,128]{2,1,0:T(8,128)(2,1)S(1)}, bf16[2,32,128]{2,1,0:T(8,128)(2,1)}, u32[]{:S(2)}) copy-start(bf16[2,32,128]{2,1,0:T(8,128)(2,1)} %refs_2_) | copy-start | bytes 49156
  0.0 1.8 %copy-start = (bf16[2,32,32,512]{3,2,1,0:T(8,128)(2,1)S(1)}, bf16[2,32,32,512]{3,2,1,0:T(8,128)(2,1)}, u32[]{:S(2)}) copy-start(bf16[2,32,32,512]{3,2,1,0:T(8,128)(2,1)} %param.8) | copy-start | bytes 6291460
  1.2 8.4 %collective-permute-start = (s32[2,32,128]{2,1,0:T(8,128)S(1)}, s32[2,32,128]{2,1,0:T(8,128)S(1)}, u32[]{:S(2)}, u32[]{:S(2)}) collective-permute-start(s32[2,32,128]{2,1,0:T(8,128)S(1)} %copy-done.1), channel_id=1, source_target_pairs={{1,0},{0,1},{3,2},{2,3},{5,4},{4,5},{7,6},{6,7},{9,8},{8,9},{11,10... | collective-permute-start | bytes 98312 | tf_op jit(solution)/shard_map/ppermute | solution.py:275
  1.7 7.9 %collective-permute-start.1 = (bf16[2,32,128]{2,1,0:T(8,128)(2,1)S(1)}, bf16[2,32,128]{2,1,0:T(8,128)(2,1)S(1)}, u32[]{:S(2)}, u32[]{:S(2)}) collective-permute-start(bf16[2,32,128]{2,1,0:T(8,128)(2,1)S(1)} %copy-done.3), channel_id=1, source_target_pairs={{1,0},{0,1},{3,2},{2,3},{5,4},{4,5},{7,6},{6,7},{9,8},{8,9},{11,10... | collective-permute-start | bytes 49160 | tf_op jit(solution)/shard_map/ppermute | solution.py:275
  3.2 12.6 %all-to-all-start = ((bf16[8,48,128]{2,1,0:T(8,128)(2,1)}), bf16[8,48,128]{2,1,0:T(8,128)(2,1)S(1)}, u32[]{:S(2)}, u32[]{:S(2)}) async-start(bf16[8,48,128]{2,1,0:T(8,128)(2,1)} %bitcast.3), calls=%async_computation | async-start | bytes 196608 | tf_op jit(solution)/shard_map/all_to_all | solution.py:336
  9.6 0.6 %copy-start.2 = (s32[2,32,128]{2,1,0:T(8,128)}, s32[2,32,128]{2,1,0:T(8,128)S(1)}, u32[]{:S(2)}) copy-start(s32[2,32,128]{2,1,0:T(8,128)S(1)} %collective-permute-done.refs_1_) | copy-start | bytes 98308

commit v5 on v4

--- a/solution.py
+++ b/solution.py
@@ -100,7 +100,7 @@
                 tmp_ref[pl.ds(base + high, SUB, stride=SUB), :] = out[
                     group * SUB : (group + 1) * SUB, high * LANES : (high + 1) * LANES
                 ]
-            out_ref[group, shot] = tmp_ref[base : base + 2 * FPD * SUB].astype(BF16)
+            out_ref[shot, group] = tmp_ref[base : base + 2 * FPD * SUB].astype(BF16)
 
 
 def make_bands(taps, nref, ny, picked_ref, band_ref):
@@ -232,7 +232,7 @@
                     for low in range(folds):
                         kept = None
                         for group in range(groups):
-                            piece = blocks[group * halves + half][item * SUB : (item + 1) * SUB]
+                            piece = blocks[half * groups + group][item * SUB : (item + 1) * SUB]
                             shift = ((group - low) * xw) % LANES
                             if shift:
                                 piece = pltpu.roll(piece, shift, 1)
@@ -294,7 +294,7 @@
 
 
     if folded:
-        send_shape = (groups, shots, items * SUB, LANES)
+        send_shape = (shots, groups, items * SUB, LANES)
     else:
         send_shape = (shots, groups * SUB, cells)
     table = filters.transpose(0, 2, 3, 1, 4)
@@ -333,7 +333,7 @@
     )(dft, records.reshape(shots, cells, nt))
     if folded:
         send = send.reshape(groups * halves, items * SUB, LANES)
-        recv = lax.all_to_all(send, ("freq", "half"), 0, 0, tiled=True)
+        recv = lax.all_to_all(send, ("half", "freq"), 0, 0, tiled=True)
     else:
         send = send.reshape(shots, groups, SUB, cells)[:, :, :items].swapaxes(0, 1)
         send = send.reshape(groups * halves, items, cells)

time: 27.9 us -> 27.5 us (0.986)
  blocking collectives: 9.94 us -> 9.35 us
    all_to_all x1, blocking collectives: 9.94 us -> 9.35 us  [body(): terms = lax.all_to_all(terms, ('freq', 'half', 'shot'), 0, 0, tiled=True)]
where the time goes in v5:
time: 27.5 us; the launch traced here: 27.2 us
  blocking collectives  9.35 us (34%)
  starting transfers between devices  6.9 us (25%)
  Pallas kernels  5.97 us (22%)
  waiting for transfers between devices  3.54 us (13%)
  local copies, waits for them, and re-layouts  0.74 us (3%)
  other arithmetic  0.62 us (2%)
    all_to_all x1, blocking collectives, body(): terms = lax.all_to_all(terms, ('freq', 'half', 'shot'), 0, 0, tiled=True)  9.35 us
    all_to_all x1, starting transfers between devices, body(): recv = lax.all_to_all(send, ('half', 'freq'), 0, 0, tiled=True)  6.3 us
    all_to_all x1, waiting for transfers between devices, body(): recv = lax.all_to_all(send, ('half', 'freq'), 0, 0, tiled=True)  3.53 us
    pallas_call x1, Pallas kernels, body(): pl.pallas_call(functools.partial(source_kernel, taps, nref, depth, halves...  2.17 us
    pallas_call x1, Pallas kernels, body(): pl.pallas_call(functools.partial(send_kernel, groups, folded), out_shape=...  1.37 us
    pallas_call x1, Pallas kernels, body(): pl.pallas_call(functools.partial(migrate_kernel, (groups, halves, copies,...  1.27 us
    pallas_call x1, Pallas kernels, body(): pl.pallas_call(functools.partial(prepare_kernel, groups), out_shape=[jax....  1.17 us
    reduce_sum x1, other arithmetic, body(): return jnp.sum(terms.astype(F32), axis=0).reshape(1, share, depth, nx)  0.62 us
  transfers between devices with their start and end apart: 3, of which 1 were waited for; matrix products, arithmetic and copies ran while one was open for 0% of the time, Pallas kernels for 13%

profile of v5, /device:TPU:0, one launch (start us, length us, event | category | flops | bytes accessed | tf_op | source)
XLA Modules:
  0.0 27.2 jit_solution(6435006021945153387)
XLA Ops:
  0.0 0.0 copy-start.1
  0.0 0.0 copy-start.3
  0.0 0.0 copy-start
  0.0 1.2 %prepare.1 = (bf16[32,512]{1,0:T(8,128)(2,1)S(1)}, s32[8,128]{1,0:T(8,128)S(1)}, f32[8,128]{1,0:T(8,128)S(1)}, bf16[2,13,13,2,256]{4,3,2,1,0:T(2,128)(2,1)S(1)}) custom-call(s32[4,6]{1,0:T(4,128)} %plan_hbm.1, s32[4]{0:T(128)} %counts_hbm.1, f32[2,256]{1,0:T(2,128)} %bitcast.8, bf16[2,13,13,2,256]{4,3,2,1,0:T(2,128)(2,1)} %bitcast.7), custom_call_target="tpu_custom_call" | custom-call | flops 3000000000 | bytes 4000000 | tf_op jit(solution)/shard_map/prepare/pallas_call | solution.py:301
  1.2 0.0 copy-done.1
  1.2 0.5 %collective-permute-start = (s32[2,32,128]{2,1,0:T(8,128)S(1)}, s32[2,32,128]{2,1,0:T(8,128)S(1)}, u32[]{:S(2)}, u32[]{:S(2)}) collective-permute-start(s32[2,32,128]{2,1,0:T(8,128)S(1)} %copy-done.1), channel_id=1, source_target_pairs={{1,0},{0,1},{3,2},{2,3},{5,4},{4,5},{7,6},{6,7},{9,8},{8,9},{11,10... | collective-permute-start | bytes 98312 | tf_op jit(solution)/shard_map/ppermute | solution.py:275
  1.7 0.0 copy-done.3
  1.7 0.1 collective-permute-start.1
  1.8 0.0 copy-done
  1.8 1.4 %send_blocks.1 = bf16[2,4,48,128]{3,2,1,0:T(8,128)(2,1)} custom-call(bf16[32,512]{1,0:T(8,128)(2,1)S(1)} %get-tuple-element.15.dft_ref, bf16[2,1024,512]{2,1,0:T(8,128)(2,1)S(1)} %bitcast.6), custom_call_target="tpu_custom_call" | custom-call | tf_op jit(solution)/shard_map/send_blocks/pallas_call | solution.py:325
  3.2 6.3 %all-to-all-start = ((bf16[8,48,128]{2,1,0:T(8,128)(2,1)}), bf16[8,48,128]{2,1,0:T(8,128)(2,1)S(1)}, u32[]{:S(2)}, u32[]{:S(2)}) async-start(bf16[8,48,128]{2,1,0:T(8,128)(2,1)} %bitcast.3), calls=%async_computation | async-start | bytes 196608 | tf_op jit(solution)/shard_map/all_to_all | solution.py:336
  9.5 0.1 reshape.14.filt_ref
  9.6 0.0 collective-permute-done.1.refs_3_
  9.6 0.0 collective-permute-done.refs_1_
  9.6 0.0 copy-start.2
  9.6 0.6 %copy-done.2 = s32[2,32,128]{2,1,0:T(8,128)} copy-done((s32[2,32,128]{2,1,0:T(8,128)}, s32[2,32,128]{2,1,0:T(8,128)S(1)}, u32[]{:S(2)}) %copy-start.2) | copy-done | bytes 32792
  10.2 2.2 %source_fields.1 = (bf16[3,1664,256]{2,1,0:T(8,128)(2,1)S(1)}, f32[2,128,128]{2,1,0:T(8,128)S(1)}, f32[2,3,128,128]{3,2,1,0:T(8,128)S(1)}) custom-call(s32[8,128]{1,0:T(8,128)S(1)} %get-tuple-element.17.own_ref, f32[8,128]{1,0:T(8,128)S(1)} %get-tuple-element.18.wave_ref, bf16[676,256]{1,0:T(8,128)(2,1)S(1)} %reshape.14.filt_ref, f32[1,64]{1,0:T(1,128)} %bitcast.9, ...), custom_call_target="tpu_custom_call" | custom-call | flops 4000000000 | bytes 10000000 | tf_op jit(solution)/shard_map/source_fields/pallas_call | solution.py:346
  12.4 3.5 %all-to-all-done.recv_ref = bf16[8,48,128]{2,1,0:T(8,128)(2,1)S(1)} async-done(((bf16[8,48,128]{2,1,0:T(8,128)(2,1)}), bf16[8,48,128]{2,1,0:T(8,128)(2,1)S(1)}, u32[]{:S(2)}, u32[]{:S(2)}) %all-to-all-start) | async-done | bytes 98336 | tf_op jit(solution)/shard_map/all_to_all | solution.py:336
  15.9 1.3 %migrate.1 = bf16[16,16,128]{2,1,0:T(8,128)(2,1)S(1)} custom-call(bf16[8,48,128]{2,1,0:T(8,128)(2,1)S(1)} %all-to-all-done.recv_ref, bf16[3,1664,256]{2,1,0:T(8,128)(2,1)S(1)} %get-tuple-element.22.band_ref, f32[2,128,128]{2,1,0:T(8,128)S(1)} %get-tuple-element.23.blend_ref, f32[2,3,128,128]{3,2,1,0:T(8,128)S(1)} %get-tuple-element.24.source_ref), custom_call_target="tpu_custom_call" | custom-call | tf_op jit(solution)/shard_map/migrate/pallas_call | solution.py:372
  17.2 9.4 %all_to_all.10 = bf16[16,16,128]{2,1,0:T(8,128)(2,1)S(1)} all-to-all(bf16[16,16,128]{2,1,0:T(8,128)(2,1)S(1)} %migrate.1), channel_id=1, replica_groups=mesh['group'=2,'freq'=4,'shot'=2,'half'=2] {'freq','half','shot'}, dimensions={0} | all-to-all | bytes 131072 | tf_op jit(solution)/shard_map/all_to_all | solution.py:385
  26.6 0.6 %convert_reduce_fusion = f32[16,128]{1,0:T(8,128)} fusion(bf16[16,16,128]{2,1,0:T(8,128)(2,1)S(1)} %all_to_all.10), kind=kLoop, calls=%fused_computation | loop fusion | flops 63488 | bytes 73728 | tf_op jit(solution)/shard_map/reduce_sum | solution.py:386
Async XLA Ops:
  0.0 1.2 %copy-start.1 = (s32[2,32,128]{2,1,0:T(8,128)S(1)}, s32[2,32,128]{2,1,0:T(8,128)}, u32[]{:S(2)}) copy-start(s32[2,32,128]{2,1,0:T(8,128)} %refs_0_) | copy-start | bytes 98308
  0.0 1.7 %copy-start.3 = (bf16[2,32,128]{2,1,0:T(8,128)(2,1)S(1)}, bf16[2,32,128]{2,1,0:T(8,128)(2,1)}, u32[]{:S(2)}) copy-start(bf16[2,32,128]{2,1,0:T(8,128)(2,1)} %refs_2_) | copy-start | bytes 49156
  0.0 1.8 %copy-start = (bf16[2,32,32,512]{3,2,1,0:T(8,128)(2,1)S(1)}, bf16[2,32,32,512]{3,2,1,0:T(8,128)(2,1)}, u32[]{:S(2)}) copy-start(bf16[2,32,32,512]{3,2,1,0:T(8,128)(2,1)} %param.8) | copy-start | bytes 6291460
  1.2 8.4 %collective-permute-start = (s32[2,32,128]{2,1,0:T(8,128)S(1)}, s32[2,32,128]{2,1,0:T(8,128)S(1)}, u32[]{:S(2)}, u32[]{:S(2)}) collective-permute-start(s32[2,32,128]{2,1,0:T(8,128)S(1)} %copy-done.1), channel_id=1, source_target_pairs={{1,0},{0,1},{3,2},{2,3},{5,4},{4,5},{7,6},{6,7},{9,8},{8,9},{11,10... | collective-permute-start | bytes 98312 | tf_op jit(solution)/shard_map/ppermute | solution.py:275
  1.7 7.9 %collective-permute-start.1 = (bf16[2,32,128]{2,1,0:T(8,128)(2,1)S(1)}, bf16[2,32,128]{2,1,0:T(8,128)(2,1)S(1)}, u32[]{:S(2)}, u32[]{:S(2)}) collective-permute-start(bf16[2,32,128]{2,1,0:T(8,128)(2,1)S(1)} %copy-done.3), channel_id=1, source_target_pairs={{1,0},{0,1},{3,2},{2,3},{5,4},{4,5},{7,6},{6,7},{9,8},{8,9},{11,10... | collective-permute-start | bytes 49160 | tf_op jit(solution)/shard_map/ppermute | solution.py:275
  3.2 12.8 %all-to-all-start = ((bf16[8,48,128]{2,1,0:T(8,128)(2,1)}), bf16[8,48,128]{2,1,0:T(8,128)(2,1)S(1)}, u32[]{:S(2)}, u32[]{:S(2)}) async-start(bf16[8,48,128]{2,1,0:T(8,128)(2,1)} %bitcast.3), calls=%async_computation | async-start | bytes 196608 | tf_op jit(solution)/shard_map/all_to_all | solution.py:336
  9.6 0.6 %copy-start.2 = (s32[2,32,128]{2,1,0:T(8,128)}, s32[2,32,128]{2,1,0:T(8,128)S(1)}, u32[]{:S(2)}) copy-start(s32[2,32,128]{2,1,0:T(8,128)S(1)} %collective-permute-done.refs_1_) | copy-start | bytes 98308

commit v6 on v5

--- a/solution.py
+++ b/solution.py
@@ -59,17 +59,16 @@
 
 
 def prepare_kernel(
-    groups, plan_hbm, counts_hbm, wav_hbm, filt_hbm, dft_ref, own_ref, wave_ref, filt_ref,
+    groups, plan_hbm, counts_hbm, wav_hbm, dft_ref, own_ref, wave_ref,
     plan_ref, counts_ref, wav_ref, bins_ref, sems,
 ):
     nt = dft_ref.shape[1]
-    filters = pltpu.make_async_copy(filt_hbm, filt_ref, sems.at[3])
     small = [
         pltpu.make_async_copy(plan_hbm, plan_ref, sems.at[0]),
         pltpu.make_async_copy(counts_hbm, counts_ref, sems.at[1]),
         pltpu.make_async_copy(wav_hbm, wav_ref, sems.at[2]),
     ]
-    for copy in small + [filters]:
+    for copy in small:
         copy.start()
     for copy in small:
         copy.wait()
@@ -83,7 +82,6 @@
         bin_id = bins_ref[first + plane]
         own_ref[plane : plane + 1] = jnp.full((1, LANES), bin_id, jnp.int32)
         wave_ref[plane : plane + 1] = jnp.where(lane < LANES // 2, wav_ref[0, bin_id], wav_ref[1, bin_id])
-    filters.wait()
 
 
 def send_kernel(groups, folded, dft_ref, rec_ref, out_ref, tmp_ref):
@@ -298,27 +296,26 @@
     else:
         send_shape = (shots, groups * SUB, cells)
     table = filters.transpose(0, 2, 3, 1, 4)
-    dft, own, wave, table = pl.pallas_call(
+    dft, own, wave = pl.pallas_call(
         functools.partial(prepare_kernel, groups),
         out_shape=[
             jax.ShapeDtypeStruct((groups * SUB, nt), BF16),
             jax.ShapeDtypeStruct((SUB, LANES), jnp.int32),
             jax.ShapeDtypeStruct((SUB, LANES), F32),
-            jax.ShapeDtypeStruct(table.shape, BF16),
         ],
-        in_specs=[hbm()] * 4,
-        out_specs=[vmem()] * 4,
+        in_specs=[hbm()] * 3,
+        out_specs=[vmem()] * 3,
         scratch_shapes=[
             pltpu.SMEM(freq_plan.shape, jnp.int32),
             pltpu.SMEM(counts.shape, jnp.int32),
             pltpu.SMEM((2, nbin), F32),
             bins,
-            pltpu.SemaphoreType.DMA((4,)),
+            pltpu.SemaphoreType.DMA((3,)),
         ],
         compiler_params=params,
         cost_estimate=pl.CostEstimate(flops=3 * 10**9, bytes_accessed=4 * 10**6, transcendentals=0),
         name="prepare",
-    )(*pinned(freq_plan, counts, wavelet.T, table))
+    )(*pinned(freq_plan, counts, wavelet.T))
     own, vel_index, source_pattern = lax.optimization_barrier((own, vel_index, source_pattern))
     classes = from_halves(vel_index, halves)
     patterns = from_halves(source_pattern, halves)

time: 27.5 us -> 27.4 us (level)
    unnamed x8 -> x10, local copies, waits for them, and re-layouts: 0.61 us -> 0.62 us
where the time goes in v6:
time: 27.4 us; the launch traced here: 27.1 us
  blocking collectives  9.35 us (34%)
  starting transfers between devices  6.91 us (25%)
  Pallas kernels  5.84 us (21%)
  waiting for transfers between devices  3.52 us (13%)
  local copies, waits for them, and re-layouts  0.75 us (3%)
  other arithmetic  0.62 us (2%)
    all_to_all x1, blocking collectives, body(): terms = lax.all_to_all(terms, ('freq', 'half', 'shot'), 0, 0, tiled=True)  9.35 us
    all_to_all x1, starting transfers between devices, body(): recv = lax.all_to_all(send, ('half', 'freq'), 0, 0, tiled=True)  6.3 us
    all_to_all x1, waiting for transfers between devices, body(): recv = lax.all_to_all(send, ('half', 'freq'), 0, 0, tiled=True)  3.52 us
    pallas_call x1, Pallas kernels, body(): pl.pallas_call(functools.partial(source_kernel, taps, nref, depth, halves...  2.17 us
    pallas_call x1, Pallas kernels, body(): pl.pallas_call(functools.partial(send_kernel, groups, folded), out_shape=...  1.37 us
    pallas_call x1, Pallas kernels, body(): pl.pallas_call(functools.partial(migrate_kernel, (groups, halves, copies,...  1.27 us
    pallas_call x1, Pallas kernels, body(): pl.pallas_call(functools.partial(prepare_kernel, groups), out_shape=[jax....  1.04 us
    unnamed x10, local copies, waits for them, and re-layouts  0.62 us
  transfers between devices with their start and end apart: 3, of which 1 were waited for; matrix products, arithmetic and copies ran while one was open for 0% of the time, Pallas kernels for 13%

profile of v6, /device:TPU:0, one launch (start us, length us, event | category | flops | bytes accessed | tf_op | source)
XLA Modules:
  0.0 27.1 jit_solution(4346957347333467836)
XLA Ops:
  0.0 0.0 copy-start.2
  0.0 0.0 copy-start.4
  0.0 0.0 copy-start
  0.0 1.0 %prepare.1 = (bf16[32,512]{1,0:T(8,128)(2,1)S(1)}, s32[8,128]{1,0:T(8,128)S(1)}, f32[8,128]{1,0:T(8,128)S(1)}) custom-call(s32[4,6]{1,0:T(4,128)} %plan_hbm.1, s32[4]{0:T(128)} %counts_hbm.1, f32[2,256]{1,0:T(2,128)} %bitcast.8), custom_call_target="tpu_custom_call" | custom-call | flops 3000000000 | bytes 4000000 | tf_op jit(solution)/shard_map/prepare/pallas_call | solution.py:299
  1.1 0.0 copy-start.1
  1.1 0.0 copy-done.2
  1.1 0.5 %collective-permute-start = (s32[2,32,128]{2,1,0:T(8,128)S(1)}, s32[2,32,128]{2,1,0:T(8,128)S(1)}, u32[]{:S(2)}, u32[]{:S(2)}) collective-permute-start(s32[2,32,128]{2,1,0:T(8,128)S(1)} %copy-done.2), channel_id=1, source_target_pairs={{1,0},{0,1},{3,2},{2,3},{5,4},{4,5},{7,6},{6,7},{9,8},{8,9},{11,10... | collective-permute-start | bytes 98312 | tf_op jit(solution)/shard_map/ppermute | solution.py:273
  1.6 0.0 copy-done.4
  1.6 0.1 collective-permute-start.1
  1.7 0.0 copy-done
  1.7 1.4 %send_blocks.1 = bf16[2,4,48,128]{3,2,1,0:T(8,128)(2,1)} custom-call(bf16[32,512]{1,0:T(8,128)(2,1)S(1)} %get-tuple-element.14.dft_ref, bf16[2,1024,512]{2,1,0:T(8,128)(2,1)S(1)} %bitcast.6), custom_call_target="tpu_custom_call" | custom-call | tf_op jit(solution)/shard_map/send_blocks/pallas_call | solution.py:322
  3.1 6.3 %all-to-all-start = ((bf16[8,48,128]{2,1,0:T(8,128)(2,1)}), bf16[8,48,128]{2,1,0:T(8,128)(2,1)S(1)}, u32[]{:S(2)}, u32[]{:S(2)}) async-start(bf16[8,48,128]{2,1,0:T(8,128)(2,1)} %bitcast.2), calls=%async_computation | async-start | bytes 196608 | tf_op jit(solution)/shard_map/all_to_all | solution.py:333
  9.4 0.0 copy-done.1
  9.4 0.1 reshape.14.filt_ref
  9.5 0.0 collective-permute-done.1.refs_3_
  9.5 0.0 collective-permute-done.refs_1_
  9.5 0.0 copy-start.3
  9.5 0.6 %copy-done.3 = s32[2,32,128]{2,1,0:T(8,128)} copy-done((s32[2,32,128]{2,1,0:T(8,128)}, s32[2,32,128]{2,1,0:T(8,128)S(1)}, u32[]{:S(2)}) %copy-start.3) | copy-done | bytes 32792
  10.1 2.2 %source_fields.1 = (bf16[3,1664,256]{2,1,0:T(8,128)(2,1)S(1)}, f32[2,128,128]{2,1,0:T(8,128)S(1)}, f32[2,3,128,128]{3,2,1,0:T(8,128)S(1)}) custom-call(s32[8,128]{1,0:T(8,128)S(1)} %get-tuple-element.16.own_ref, f32[8,128]{1,0:T(8,128)S(1)} %get-tuple-element.17.wave_ref, bf16[676,256]{1,0:T(8,128)(2,1)S(1)} %reshape.14.filt_ref, f32[1,64]{1,0:T(1,128)} %bitcast.9, ...), custom_call_target="tpu_custom_call" | custom-call | flops 4000000000 | bytes 10000000 | tf_op jit(solution)/shard_map/source_fields/pallas_call | solution.py:343
  12.3 3.5 %all-to-all-done.recv_ref = bf16[8,48,128]{2,1,0:T(8,128)(2,1)S(1)} async-done(((bf16[8,48,128]{2,1,0:T(8,128)(2,1)}), bf16[8,48,128]{2,1,0:T(8,128)(2,1)S(1)}, u32[]{:S(2)}, u32[]{:S(2)}) %all-to-all-start) | async-done | bytes 98336 | tf_op jit(solution)/shard_map/all_to_all | solution.py:333
  15.8 1.3 %migrate.1 = bf16[16,16,128]{2,1,0:T(8,128)(2,1)S(1)} custom-call(bf16[8,48,128]{2,1,0:T(8,128)(2,1)S(1)} %all-to-all-done.recv_ref, bf16[3,1664,256]{2,1,0:T(8,128)(2,1)S(1)} %get-tuple-element.20.band_ref, f32[2,128,128]{2,1,0:T(8,128)S(1)} %get-tuple-element.21.blend_ref, f32[2,3,128,128]{3,2,1,0:T(8,128)S(1)} %get-tuple-element.22.source_ref), custom_call_target="tpu_custom_call" | custom-call | tf_op jit(solution)/shard_map/migrate/pallas_call | solution.py:369
  17.1 9.3 %all_to_all.10 = bf16[16,16,128]{2,1,0:T(8,128)(2,1)S(1)} all-to-all(bf16[16,16,128]{2,1,0:T(8,128)(2,1)S(1)} %migrate.1), channel_id=1, replica_groups=mesh['group'=2,'freq'=4,'shot'=2,'half'=2] {'freq','half','shot'}, dimensions={0} | all-to-all | bytes 131072 | tf_op jit(solution)/shard_map/all_to_all | solution.py:382
  26.5 0.6 %convert_reduce_fusion = f32[16,128]{1,0:T(8,128)} fusion(bf16[16,16,128]{2,1,0:T(8,128)(2,1)S(1)} %all_to_all.10), kind=kLoop, calls=%fused_computation | loop fusion | flops 63488 | bytes 73728 | tf_op jit(solution)/shard_map/reduce_sum | solution.py:383
Async XLA Ops:
  0.0 1.1 %copy-start.2 = (s32[2,32,128]{2,1,0:T(8,128)S(1)}, s32[2,32,128]{2,1,0:T(8,128)}, u32[]{:S(2)}) copy-start(s32[2,32,128]{2,1,0:T(8,128)} %refs_0_) | copy-start | bytes 98308
  0.0 1.6 %copy-start.4 = (bf16[2,32,128]{2,1,0:T(8,128)(2,1)S(1)}, bf16[2,32,128]{2,1,0:T(8,128)(2,1)}, u32[]{:S(2)}) copy-start(bf16[2,32,128]{2,1,0:T(8,128)(2,1)} %refs_2_) | copy-start | bytes 49156
  0.0 1.7 %copy-start = (bf16[2,32,32,512]{3,2,1,0:T(8,128)(2,1)S(1)}, bf16[2,32,32,512]{3,2,1,0:T(8,128)(2,1)}, u32[]{:S(2)}) copy-start(bf16[2,32,32,512]{3,2,1,0:T(8,128)(2,1)} %param.8) | copy-start | bytes 6291460
  1.1 8.3 %copy-start.1 = (bf16[2,2,13,13,256]{4,1,3,2,0:T(2,128)(2,1)S(1)}, bf16[2,2,13,13,256]{4,1,3,2,0:T(2,128)(2,1)}, u32[]{:S(2)}) copy-start(bf16[2,2,13,13,256]{4,1,3,2,0:T(2,128)(2,1)} %param.11) | copy-start | bytes 1038340
  1.1 8.4 %collective-permute-start = (s32[2,32,128]{2,1,0:T(8,128)S(1)}, s32[2,32,128]{2,1,0:T(8,128)S(1)}, u32[]{:S(2)}, u32[]{:S(2)}) collective-permute-start(s32[2,32,128]{2,1,0:T(8,128)S(1)} %copy-done.2), channel_id=1, source_target_pairs={{1,0},{0,1},{3,2},{2,3},{5,4},{4,5},{7,6},{6,7},{9,8},{8,9},{11,10... | collective-permute-start | bytes 98312 | tf_op jit(solution)/shard_map/ppermute | solution.py:273
  1.6 7.9 %collective-permute-start.1 = (bf16[2,32,128]{2,1,0:T(8,128)(2,1)S(1)}, bf16[2,32,128]{2,1,0:T(8,128)(2,1)S(1)}, u32[]{:S(2)}, u32[]{:S(2)}) collective-permute-start(bf16[2,32,128]{2,1,0:T(8,128)(2,1)S(1)} %copy-done.4), channel_id=1, source_target_pairs={{1,0},{0,1},{3,2},{2,3},{5,4},{4,5},{7,6},{6,7},{9,8},{8,9},{11,10... | collective-permute-start | bytes 49160 | tf_op jit(solution)/shard_map/ppermute | solution.py:273
  3.1 12.8 %all-to-all-start = ((bf16[8,48,128]{2,1,0:T(8,128)(2,1)}), bf16[8,48,128]{2,1,0:T(8,128)(2,1)S(1)}, u32[]{:S(2)}, u32[]{:S(2)}) async-start(bf16[8,48,128]{2,1,0:T(8,128)(2,1)} %bitcast.2), calls=%async_computation | async-start | bytes 196608 | tf_op jit(solution)/shard_map/all_to_all | solution.py:333
  9.5 0.6 %copy-start.3 = (s32[2,32,128]{2,1,0:T(8,128)}, s32[2,32,128]{2,1,0:T(8,128)S(1)}, u32[]{:S(2)}) copy-start(s32[2,32,128]{2,1,0:T(8,128)S(1)} %collective-permute-done.refs_1_) | copy-start | bytes 98308

commit v7 on v6

--- a/solution.py
+++ b/solution.py
@@ -58,17 +58,35 @@
     return lax.dot_general(dft, block, (((1,), (1,)), ((), ())), preferred_element_type=F32)
 
 
+def put_spectra(groups, folded, out, put, tmp_ref):
+    if not folded:
+        put[...] = out.astype(BF16)
+        return
+    for group in range(groups):
+        base = group * SUB * SUB
+        for high in range(SUB):
+            tmp_ref[pl.ds(base + high, SUB, stride=SUB), :] = out[
+                group * SUB : (group + 1) * SUB, high * LANES : (high + 1) * LANES
+            ]
+        put[group] = tmp_ref[base : base + 2 * FPD * SUB].astype(BF16)
+
+
 def prepare_kernel(
-    groups, plan_hbm, counts_hbm, wav_hbm, dft_ref, own_ref, wave_ref,
-    plan_ref, counts_ref, wav_ref, bins_ref, sems,
+    groups, folded, plan_hbm, counts_hbm, wav_hbm, rec_hbm, dft_ref, own_ref, wave_ref, early_ref, last_ref,
+    plan_ref, counts_ref, wav_ref, bins_ref, rec_ref, tmp_ref, sems,
 ):
     nt = dft_ref.shape[1]
+    shots = rec_hbm.shape[0]
     small = [
         pltpu.make_async_copy(plan_hbm, plan_ref, sems.at[0]),
         pltpu.make_async_copy(counts_hbm, counts_ref, sems.at[1]),
         pltpu.make_async_copy(wav_hbm, wav_ref, sems.at[2]),
     ]
-    for copy in small:
+    records = [
+        pltpu.make_async_copy(rec_hbm.at[shot], rec_ref.at[shot] if shot < shots - 1 else last_ref, sems.at[3 + shot])
+        for shot in range(shots)
+    ]
+    for copy in small + records:
         copy.start()
     for copy in small:
         copy.wait()
@@ -82,23 +100,18 @@
         bin_id = bins_ref[first + plane]
         own_ref[plane : plane + 1] = jnp.full((1, LANES), bin_id, jnp.int32)
         wave_ref[plane : plane + 1] = jnp.where(lane < LANES // 2, wav_ref[0, bin_id], wav_ref[1, bin_id])
-
-
-def send_kernel(groups, folded, dft_ref, rec_ref, out_ref, tmp_ref):
-    shots, cells, _ = rec_ref.shape
-    dft = dft_ref[...]
-    for shot in range(shots):
-        out = transform(dft, rec_ref[shot])
-        if not folded:
-            out_ref[shot] = out.astype(BF16)
-            continue
-        for group in range(groups):
-            base = (group * shots + shot) * SUB * SUB
-            for high in range(SUB):
-                tmp_ref[pl.ds(base + high, SUB, stride=SUB), :] = out[
-                    group * SUB : (group + 1) * SUB, high * LANES : (high + 1) * LANES
-                ]
-            out_ref[shot, group] = tmp_ref[base : base + 2 * FPD * SUB].astype(BF16)
+    for shot in range(shots - 1):
+        records[shot].wait()
+        put_spectra(groups, folded, transform(dft_ref[...], rec_ref[shot]), early_ref.at[shot], tmp_ref)
+    records[shots - 1].wait()
+
+
+def send_kernel(groups, folded, dft_ref, early_ref, last_ref, out_ref, tmp_ref):
+    early = early_ref.shape[0]
+    out = transform(dft_ref[...], last_ref[...])
+    for shot in range(early):
+        out_ref[shot] = early_ref[shot]
+    put_spectra(groups, folded, out, out_ref.at[early], tmp_ref)
 
 
 def make_bands(taps, nref, ny, picked_ref, band_ref):
@@ -296,38 +309,43 @@
     else:
         send_shape = (shots, groups * SUB, cells)
     table = filters.transpose(0, 2, 3, 1, 4)
-    dft, own, wave = pl.pallas_call(
-        functools.partial(prepare_kernel, groups),
+    classes = from_halves(vel_index, halves)
+    tmp = pltpu.VMEM((groups * SUB * SUB + SUB, LANES), F32)
+    dft, own, wave, early, last = pl.pallas_call(
+        functools.partial(prepare_kernel, groups, folded),
         out_shape=[
             jax.ShapeDtypeStruct((groups * SUB, nt), BF16),
             jax.ShapeDtypeStruct((SUB, LANES), jnp.int32),
             jax.ShapeDtypeStruct((SUB, LANES), F32),
+            jax.ShapeDtypeStruct((shots - 1,) + send_shape[1:], BF16),
+            jax.ShapeDtypeStruct((cells, nt), BF16),
         ],
-        in_specs=[hbm()] * 3,
-        out_specs=[vmem()] * 3,
+        in_specs=[hbm()] * 4,
+        out_specs=[vmem()] * 5,
         scratch_shapes=[
             pltpu.SMEM(freq_plan.shape, jnp.int32),
             pltpu.SMEM(counts.shape, jnp.int32),
             pltpu.SMEM((2, nbin), F32),
             bins,
-            pltpu.SemaphoreType.DMA((3,)),
+            pltpu.VMEM((shots - 1, cells, nt), BF16),
+            tmp,
+            pltpu.SemaphoreType.DMA((3 + shots,)),
         ],
         compiler_params=params,
-        cost_estimate=pl.CostEstimate(flops=3 * 10**9, bytes_accessed=4 * 10**6, transcendentals=0),
+        cost_estimate=pl.CostEstimate(flops=2 * 10**9, bytes_accessed=4 * 10**6, transcendentals=0),
         name="prepare",
-    )(*pinned(freq_plan, counts, wavelet.T))
-    own, vel_index, source_pattern = lax.optimization_barrier((own, vel_index, source_pattern))
-    classes = from_halves(vel_index, halves)
+    )(*pinned(freq_plan, counts, wavelet.T, records.reshape(shots, cells, nt)))
+    own, source_pattern = lax.optimization_barrier((own, source_pattern))
     patterns = from_halves(source_pattern, halves)
     send = pl.pallas_call(
         functools.partial(send_kernel, groups, folded),
         out_shape=jax.ShapeDtypeStruct(send_shape, BF16),
-        in_specs=[vmem()] * 2,
+        in_specs=[vmem()] * 3,
         out_specs=vmem(),
-        scratch_shapes=[pltpu.VMEM((groups * shots * SUB * SUB + SUB, LANES), F32)],
+        scratch_shapes=[tmp],
         compiler_params=params,
         name="send_blocks",
-    )(dft, records.reshape(shots, cells, nt))
+    )(dft, early, last)
     if folded:
         send = send.reshape(groups * halves, items * SUB, LANES)
         recv = lax.all_to_all(send, ("half", "freq"), 0, 0, tiled=True)

time: 27.4 us -> 27.7 us (1.011)
  Pallas kernels: 5.84 us -> 6.25 us
    pallas_call x1, Pallas kernels: 1.04 us -> 1.75 us  [body(): pl.pallas_call(functools.partial(prepare_kernel, groups, folded), out_sha...]
    pallas_call x1, Pallas kernels: 1.37 us -> 1.07 us  [body(): pl.pallas_call(functools.partial(send_kernel, groups, folded), out_shape=...]
    unnamed x10 -> x6, local copies, waits for them, and re-layouts: 0.62 us -> 0.61 us
  transfers between devices with their start and end apart: 3 -> 3, of which waited for: 1 -> 1; matrix products, arithmetic and copies ran while one was open for 0% -> 0% of each run, Pallas kernels for 13% -> 18%
where the time goes in v7:
time: 27.7 us; the launch traced here: 27.5 us
  blocking collectives  9.35 us (34%)
  starting transfers between devices  6.9 us (25%)
  Pallas kernels  6.25 us (23%)
  waiting for transfers between devices  3.52 us (13%)
  local copies, waits for them, and re-layouts  0.75 us (3%)
  other arithmetic  0.62 us (2%)
    all_to_all x1, blocking collectives, body(): terms = lax.all_to_all(terms, ('freq', 'half', 'shot'), 0, 0, tiled=True)  9.35 us
    all_to_all x1, starting transfers between devices, body(): recv = lax.all_to_all(send, ('half', 'freq'), 0, 0, tiled=True)  6.32 us
    all_to_all x1, waiting for transfers between devices, body(): recv = lax.all_to_all(send, ('half', 'freq'), 0, 0, tiled=True)  3.51 us
    pallas_call x1, Pallas kernels, body(): pl.pallas_call(functools.partial(source_kernel, taps, nref, depth, halves...  2.17 us
    pallas_call x1, Pallas kernels, body(): pl.pallas_call(functools.partial(prepare_kernel, groups, folded), out_sha...  1.75 us
    pallas_call x1, Pallas kernels, body(): pl.pallas_call(functools.partial(migrate_kernel, (groups, halves, copies,...  1.27 us
    pallas_call x1, Pallas kernels, body(): pl.pallas_call(functools.partial(send_kernel, groups, folded), out_shape=...  1.07 us
    reduce_sum x1, other arithmetic, body(): return jnp.sum(terms.astype(F32), axis=0).reshape(1, share, depth, nx)  0.62 us
  transfers between devices with their start and end apart: 3, of which 1 were waited for; matrix products, arithmetic and copies ran while one was open for 0% of the time, Pallas kernels for 18%

profile of v7, /device:TPU:0, one launch (start us, length us, event | category | flops | bytes accessed | tf_op | source)
XLA Modules:
  0.0 27.5 jit_solution(13810987440600666308)
XLA Ops:
  0.0 0.5 %collective-permute-start = (s32[2,32,128]{2,1,0:T(8,128)}, s32[2,32,128]{2,1,0:T(8,128)S(1)}, u32[]{:S(2)}, u32[]{:S(2)}) collective-permute-start(s32[2,32,128]{2,1,0:T(8,128)} %refs_0_.1), channel_id=1, source_target_pairs={{1,0},{0,1},{3,2},{2,3},{5,4},{4,5},{7,6},{6,7},{9,8},{8,9},{11,10... | collective-permute-start | bytes 98312 | tf_op jit(solution)/shard_map/ppermute | solution.py:286
  0.5 0.0 copy-start.2
  0.5 0.0 copy-start
  0.5 1.7 %prepare.1 = (bf16[32,512]{1,0:T(8,128)(2,1)S(1)}, s32[8,128]{1,0:T(8,128)S(1)}, f32[8,128]{1,0:T(8,128)S(1)}, bf16[1,4,48,128]{3,2,1,0:T(8,128)(2,1)S(1)}, bf16[1024,512]{1,0:T(8,128)(2,1)S(1)}) custom-call(s32[4,6]{1,0:T(4,128)} %plan_hbm.1, s32[4]{0:T(128)} %counts_hbm.1, f32[2,256]{1,0:T(2,128)} %bitcast.8, bf16[2,1024,512]{2,1,0:T(8,128)(2,1)} %bitcast.7), custom_call_target="tpu_custom_call" | custom-call | flops 2000000000 | bytes 4000000 | tf_op jit(solution)/shard_map/prepare/pallas_call | solution.py:314
  2.2 0.0 copy-done.2
  2.2 0.1 collective-permute-start.1
  2.3 1.1 %send_blocks.1 = bf16[2,4,48,128]{3,2,1,0:T(8,128)(2,1)} custom-call(bf16[32,512]{1,0:T(8,128)(2,1)S(1)} %get-tuple-element.15.dft_ref, bf16[1,4,48,128]{3,2,1,0:T(8,128)(2,1)S(1)} %get-tuple-element.16.early_ref, bf16[1024,512]{1,0:T(8,128)(2,1)S(1)} %get-tuple-element.17.last_ref), custom_call_target="tpu_custom_call" | custom-call | tf_op jit(solution)/shard_map/send_blocks/pallas_call | solution.py:340
  3.4 6.3 %all-to-all-start = ((bf16[8,48,128]{2,1,0:T(8,128)(2,1)}), bf16[8,48,128]{2,1,0:T(8,128)(2,1)S(1)}, u32[]{:S(2)}, u32[]{:S(2)}) async-start(bf16[8,48,128]{2,1,0:T(8,128)(2,1)} %bitcast.2), calls=%async_computation | async-start | bytes 196608 | tf_op jit(solution)/shard_map/all_to_all | solution.py:351
  9.7 0.0 copy-done
  9.7 0.1 reshape.14.filt_ref
  9.9 0.0 collective-permute-done.1.refs_3_
  9.9 0.0 collective-permute-done.refs_1_
  9.9 0.0 copy-start.1
  9.9 0.6 %copy-done.1 = s32[2,32,128]{2,1,0:T(8,128)} copy-done((s32[2,32,128]{2,1,0:T(8,128)}, s32[2,32,128]{2,1,0:T(8,128)S(1)}, u32[]{:S(2)}) %copy-start.1) | copy-done | bytes 32792
  10.5 2.2 %source_fields.1 = (bf16[3,1664,256]{2,1,0:T(8,128)(2,1)S(1)}, f32[2,128,128]{2,1,0:T(8,128)S(1)}, f32[2,3,128,128]{3,2,1,0:T(8,128)S(1)}) custom-call(s32[8,128]{1,0:T(8,128)S(1)} %get-tuple-element.19.own_ref, f32[8,128]{1,0:T(8,128)S(1)} %get-tuple-element.20.wave_ref, bf16[676,256]{1,0:T(8,128)(2,1)S(1)} %reshape.14.filt_ref, f32[1,64]{1,0:T(1,128)} %bitcast.9, ...), custom_call_target="tpu_custom_call" | custom-call | flops 4000000000 | bytes 10000000 | tf_op jit(solution)/shard_map/source_fields/pallas_call | solution.py:361
  12.7 3.5 %all-to-all-done.recv_ref = bf16[8,48,128]{2,1,0:T(8,128)(2,1)S(1)} async-done(((bf16[8,48,128]{2,1,0:T(8,128)(2,1)}), bf16[8,48,128]{2,1,0:T(8,128)(2,1)S(1)}, u32[]{:S(2)}, u32[]{:S(2)}) %all-to-all-start) | async-done | bytes 98336 | tf_op jit(solution)/shard_map/all_to_all | solution.py:351
  16.2 1.3 %migrate.1 = bf16[16,16,128]{2,1,0:T(8,128)(2,1)S(1)} custom-call(bf16[8,48,128]{2,1,0:T(8,128)(2,1)S(1)} %all-to-all-done.recv_ref, bf16[3,1664,256]{2,1,0:T(8,128)(2,1)S(1)} %get-tuple-element.22.band_ref, f32[2,128,128]{2,1,0:T(8,128)S(1)} %get-tuple-element.23.blend_ref, f32[2,3,128,128]{3,2,1,0:T(8,128)S(1)} %get-tuple-element.24.source_ref), custom_call_target="tpu_custom_call" | custom-call | tf_op jit(solution)/shard_map/migrate/pallas_call | solution.py:387
  17.5 9.3 %all_to_all.10 = bf16[16,16,128]{2,1,0:T(8,128)(2,1)S(1)} all-to-all(bf16[16,16,128]{2,1,0:T(8,128)(2,1)S(1)} %migrate.1), channel_id=1, replica_groups=mesh['group'=2,'freq'=4,'shot'=2,'half'=2] {'freq','half','shot'}, dimensions={0} | all-to-all | bytes 131072 | tf_op jit(solution)/shard_map/all_to_all | solution.py:400
  26.8 0.6 %convert_reduce_fusion = f32[16,128]{1,0:T(8,128)} fusion(bf16[16,16,128]{2,1,0:T(8,128)(2,1)S(1)} %all_to_all.10), kind=kLoop, calls=%fused_computation | loop fusion | flops 63488 | bytes 73728 | tf_op jit(solution)/shard_map/reduce_sum | solution.py:401
Async XLA Ops:
  0.0 9.9 %collective-permute-start = (s32[2,32,128]{2,1,0:T(8,128)}, s32[2,32,128]{2,1,0:T(8,128)S(1)}, u32[]{:S(2)}, u32[]{:S(2)}) collective-permute-start(s32[2,32,128]{2,1,0:T(8,128)} %refs_0_.1), channel_id=1, source_target_pairs={{1,0},{0,1},{3,2},{2,3},{5,4},{4,5},{7,6},{6,7},{9,8},{8,9},{11,10... | collective-permute-start | bytes 98312 | tf_op jit(solution)/shard_map/ppermute | solution.py:286
  0.5 1.8 %copy-start.2 = (bf16[2,32,128]{2,1,0:T(8,128)(2,1)S(1)}, bf16[2,32,128]{2,1,0:T(8,128)(2,1)}, u32[]{:S(2)}) copy-start(bf16[2,32,128]{2,1,0:T(8,128)(2,1)} %refs_2_) | copy-start | bytes 49156
  0.5 9.3 %copy-start = (bf16[2,2,13,13,256]{4,1,3,2,0:T(2,128)(2,1)S(1)}, bf16[2,2,13,13,256]{4,1,3,2,0:T(2,128)(2,1)}, u32[]{:S(2)}) copy-start(bf16[2,2,13,13,256]{4,1,3,2,0:T(2,128)(2,1)} %param.11) | copy-start | bytes 1038340
  2.2 7.7 %collective-permute-start.1 = (bf16[2,32,128]{2,1,0:T(8,128)(2,1)S(1)}, bf16[2,32,128]{2,1,0:T(8,128)(2,1)S(1)}, u32[]{:S(2)}, u32[]{:S(2)}) collective-permute-start(bf16[2,32,128]{2,1,0:T(8,128)(2,1)S(1)} %copy-done.2), channel_id=1, source_target_pairs={{1,0},{0,1},{3,2},{2,3},{5,4},{4,5},{7,6},{6,7},{9,8},{8,9},{11,10... | collective-permute-start | bytes 49160 | tf_op jit(solution)/shard_map/ppermute | solution.py:286
  3.4 12.8 %all-to-all-start = ((bf16[8,48,128]{2,1,0:T(8,128)(2,1)}), bf16[8,48,128]{2,1,0:T(8,128)(2,1)S(1)}, u32[]{:S(2)}, u32[]{:S(2)}) async-start(bf16[8,48,128]{2,1,0:T(8,128)(2,1)} %bitcast.2), calls=%async_computation | async-start | bytes 196608 | tf_op jit(solution)/shard_map/all_to_all | solution.py:351
  9.9 0.6 %copy-start.1 = (s32[2,32,128]{2,1,0:T(8,128)}, s32[2,32,128]{2,1,0:T(8,128)S(1)}, u32[]{:S(2)}) copy-start(s32[2,32,128]{2,1,0:T(8,128)S(1)} %collective-permute-done.refs_1_) | copy-start | bytes 98308

commit v8 on v6

--- a/solution.py
+++ b/solution.py
@@ -59,16 +59,21 @@
 
 
 def prepare_kernel(
-    groups, plan_hbm, counts_hbm, wav_hbm, dft_ref, own_ref, wave_ref,
-    plan_ref, counts_ref, wav_ref, bins_ref, sems,
+    groups, plan_hbm, counts_hbm, wav_hbm, class_hbm, pattern_hbm, dft_ref, own_ref, wave_ref, shared_ref,
+    plan_ref, counts_ref, wav_ref, class_ref, bins_ref, sems,
 ):
     nt = dft_ref.shape[1]
+    depth, shots = class_hbm.shape[0], pattern_hbm.shape[0]
+    later = [
+        pltpu.make_async_copy(class_hbm, class_ref, sems.at[3]),
+        pltpu.make_async_copy(pattern_hbm, shared_ref.at[pl.ds(depth, shots)], sems.at[4]),
+    ]
     small = [
         pltpu.make_async_copy(plan_hbm, plan_ref, sems.at[0]),
         pltpu.make_async_copy(counts_hbm, counts_ref, sems.at[1]),
         pltpu.make_async_copy(wav_hbm, wav_ref, sems.at[2]),
     ]
-    for copy in small:
+    for copy in small + later:
         copy.start()
     for copy in small:
         copy.wait()
@@ -82,6 +87,9 @@
         bin_id = bins_ref[first + plane]
         own_ref[plane : plane + 1] = jnp.full((1, LANES), bin_id, jnp.int32)
         wave_ref[plane : plane + 1] = jnp.where(lane < LANES // 2, wav_ref[0, bin_id], wav_ref[1, bin_id])
+    for copy in later:
+        copy.wait()
+    shared_ref[:depth] = class_ref[...].astype(BF16)
 
 
 def send_kernel(groups, folded, dft_ref, rec_ref, out_ref, tmp_ref):
@@ -164,18 +172,21 @@
         left = follow
 
 
-def source_kernel(taps, nref, depth, halves, own_ref, wave_ref, filt_ref, table_hbm, *refs):
-    class_hbm, refs = refs[:halves], refs[halves:]
-    pattern_hbm, refs = refs[:halves], refs[halves:]
-    band_ref, blend_ref, source_ref, class_refs, pattern_refs, table_ref, picked_ref, grid_ref, tab_ref, field_ref, sems = refs
-    copies = [pltpu.make_async_copy(table_hbm, table_ref, sems.at[0])]
-    for turn in range(halves):
-        copies.append(pltpu.make_async_copy(class_hbm[turn], class_refs.at[turn], sems.at[1 + 2 * turn]))
-        copies.append(pltpu.make_async_copy(pattern_hbm[turn], pattern_refs.at[turn], sems.at[2 + 2 * turn]))
+def source_kernel(taps, nref, depth, halves, own_ref, wave_ref, filt_ref, table_hbm, class_hbm, pattern_hbm, *refs):
+    others_hbm, refs = refs[: halves - 1], refs[halves - 1 :]
+    (band_ref, blend_ref, source_ref, table_ref, class_ref, pattern_ref, others_ref,
+     picked_ref, grid_ref, tab_ref, field_ref, sems) = refs
+    copies = [
+        pltpu.make_async_copy(table_hbm, table_ref, sems.at[0]),
+        pltpu.make_async_copy(class_hbm, class_ref, sems.at[1]),
+        pltpu.make_async_copy(pattern_hbm, pattern_ref, sems.at[2]),
+    ]
+    for turn in range(halves - 1):
+        copies.append(pltpu.make_async_copy(others_hbm[turn], others_ref.at[turn], sems.at[3 + turn]))
     for copy in copies:
         copy.start()
     mine = lax.axis_index("half")
-    rows = class_hbm[0].shape[1]
+    rows = class_ref.shape[1]
     ny, nx = grid_ref.shape[1:]
     nbin = filt_ref.shape[1]
     for plane in range(FPD):
@@ -188,8 +199,10 @@
     for turn in range(halves):
         at = pl.ds(pl.multiple_of(lax.rem(mine + turn, halves) * rows, rows), rows)
         for step in range(depth):
-            grid_ref[step, at, :] = class_refs[turn, step].astype(F32)
-        grid_ref[depth, at, :] = pattern_refs[turn, mine].astype(F32)
+            one = others_ref[turn - 1, step] if turn else class_ref[step]
+            grid_ref[step, at, :] = one.astype(F32)
+        one = others_ref[turn - 1, depth + mine] if turn else pattern_ref[mine]
+        grid_ref[depth, at, :] = one.astype(F32)
     tab_ref[:, : table_ref.shape[1]] = jnp.broadcast_to(table_ref[...], (SUB, table_ref.shape[1]))
     for step in range(depth):
         pieces = []
@@ -296,29 +309,29 @@
     else:
         send_shape = (shots, groups * SUB, cells)
     table = filters.transpose(0, 2, 3, 1, 4)
-    dft, own, wave = pl.pallas_call(
+    dft, own, wave, shared = pl.pallas_call(
         functools.partial(prepare_kernel, groups),
         out_shape=[
             jax.ShapeDtypeStruct((groups * SUB, nt), BF16),
             jax.ShapeDtypeStruct((SUB, LANES), jnp.int32),
             jax.ShapeDtypeStruct((SUB, LANES), F32),
+            jax.ShapeDtypeStruct((depth + shots, rows, nx), BF16),
         ],
-        in_specs=[hbm()] * 3,
-        out_specs=[vmem()] * 3,
+        in_specs=[hbm()] * 5,
+        out_specs=[vmem()] * 4,
         scratch_shapes=[
             pltpu.SMEM(freq_plan.shape, jnp.int32),
             pltpu.SMEM(counts.shape, jnp.int32),
             pltpu.SMEM((2, nbin), F32),
+            pltpu.VMEM(vel_index.shape, jnp.int32),
             bins,
-            pltpu.SemaphoreType.DMA((3,)),
+            pltpu.SemaphoreType.DMA((5,)),
         ],
         compiler_params=params,
         cost_estimate=pl.CostEstimate(flops=3 * 10**9, bytes_accessed=4 * 10**6, transcendentals=0),
         name="prepare",
-    )(*pinned(freq_plan, counts, wavelet.T))
-    own, vel_index, source_pattern = lax.optimization_barrier((own, vel_index, source_pattern))
-    classes = from_halves(vel_index, halves)
-    patterns = from_halves(source_pattern, halves)
+    )(*pinned(freq_plan, counts, wavelet.T, vel_index, source_pattern))
+    others = from_halves(shared, halves)[1:]
     send = pl.pallas_call(
         functools.partial(send_kernel, groups, folded),
         out_shape=jax.ShapeDtypeStruct(send_shape, BF16),
@@ -347,22 +360,23 @@
             jax.ShapeDtypeStruct((depth, nx, 2 * ny), F32),
             jax.ShapeDtypeStruct((depth, FPD, nx, 2 * ny), F32),
         ],
-        in_specs=[vmem()] * 3 + [hbm()] * (2 + halves) + [pl.BlockSpec(memory_space=pl.ANY)] * (halves - 1),
+        in_specs=[vmem()] * 3 + [hbm()] * 2 + [pl.BlockSpec(memory_space=pl.ANY)] + [hbm()] * (halves - 1),
         out_specs=[vmem()] * 3,
         scratch_shapes=[
-            pltpu.VMEM((halves,) + vel_index.shape, jnp.int32),
-            pltpu.VMEM((halves,) + source_pattern.shape, BF16),
             pltpu.VMEM((1,) + vel_table.shape, F32),
+            pltpu.VMEM(vel_index.shape, jnp.int32),
+            pltpu.VMEM(source_pattern.shape, BF16),
+            pltpu.VMEM((halves - 1,) + shared.shape, BF16),
             pltpu.VMEM((FPD, (table.shape[0] + 2 * taps + SUB) // SUB * SUB + 2 * SUB, LANES), F32),
             pltpu.VMEM((depth + 1, ny, nx), F32),
             pltpu.VMEM((SUB, LANES), F32),
             field,
-            pltpu.SemaphoreType.DMA((1 + 2 * halves,)),
+            pltpu.SemaphoreType.DMA((2 + halves,)),
         ],
         compiler_params=params,
         cost_estimate=pl.CostEstimate(flops=4 * 10**9, bytes_accessed=10**7, transcendentals=0),
         name="source_fields",
-    )(own, wave, table, *pinned(vel_table[None], *classes, patterns[0]), *patterns[1:])
+    )(own, wave, table, *pinned(vel_table[None], vel_index), source_pattern, *pinned(*others))
 
     scale = 1.0 / math.sqrt(FPD * groups * shots * copies)
     share = ny // (groups * halves)

time: 27.4 us -> 27.3 us (level)
    ppermute x2 -> x1, starting transfers between devices: 0.61 us -> 0.52 us  [from_halves(): lax.ppermute(block, 'half', [((to + turn) % halves, to) for to in range(h...]
    unnamed x10 -> x8, local copies, waits for them, and re-layouts: 0.62 us -> 0.63 us
  transfers between devices with their start and end apart: 3 -> 2, of which waited for: 1 -> 1; matrix products, arithmetic and copies ran while one was open for 0% -> 0% of each run, Pallas kernels for 13% -> 13%
where the time goes in v8:
time: 27.3 us; the launch traced here: 27 us
  blocking collectives  9.35 us (34%)
  starting transfers between devices  6.84 us (25%)
  Pallas kernels  5.86 us (21%)
  waiting for transfers between devices  3.55 us (13%)
  local copies, waits for them, and re-layouts  0.76 us (3%)
  other arithmetic  0.62 us (2%)
    all_to_all x1, blocking collectives, body(): terms = lax.all_to_all(terms, ('freq', 'half', 'shot'), 0, 0, tiled=True)  9.35 us
    all_to_all x1, starting transfers between devices, body(): recv = lax.all_to_all(send, ('half', 'freq'), 0, 0, tiled=True)  6.32 us
    all_to_all x1, waiting for transfers between devices, body(): recv = lax.all_to_all(send, ('half', 'freq'), 0, 0, tiled=True)  3.54 us
    pallas_call x1, Pallas kernels, body(): pl.pallas_call(functools.partial(source_kernel, taps, nref, depth, halves...  2.15 us
    pallas_call x1, Pallas kernels, body(): pl.pallas_call(functools.partial(send_kernel, groups, folded), out_shape=...  1.38 us
    pallas_call x1, Pallas kernels, body(): pl.pallas_call(functools.partial(migrate_kernel, (groups, halves, copies,...  1.27 us
    pallas_call x1, Pallas kernels, body(): pl.pallas_call(functools.partial(prepare_kernel, groups), out_shape=[jax....  1.06 us
    unnamed x8, local copies, waits for them, and re-layouts  0.63 us
  transfers between devices with their start and end apart: 2, of which 1 were waited for; matrix products, arithmetic and copies ran while one was open for 0% of the time, Pallas kernels for 13%

profile of v8, /device:TPU:0, one launch (start us, length us, event | category | flops | bytes accessed | tf_op | source)
XLA Modules:
  0.0 27.0 jit_solution(13200723889488631838)
XLA Ops:
  0.0 0.0 copy-start
  0.0 1.1 %prepare.1 = (bf16[32,512]{1,0:T(8,128)(2,1)S(1)}, s32[8,128]{1,0:T(8,128)S(1)}, f32[8,128]{1,0:T(8,128)S(1)}, bf16[4,32,128]{2,1,0:T(8,128)(2,1)S(1)}) custom-call(s32[4,6]{1,0:T(4,128)} %plan_hbm.1, s32[4]{0:T(128)} %counts_hbm.1, f32[2,256]{1,0:T(2,128)} %bitcast.8, s32[2,32,128]{2,1,0:T(8,128)} %class_hbm.3, bf16[2,32,128]{2,1,0:T(8,128)(2,1)} %pattern_hbm.3), custom_call_target="tpu_custom_call" | custom-call | flops 3000000000 | bytes 4000000 | tf_op jit(solution)/shard_map/prepare/pallas_call | solution.py:312
  1.1 0.0 copy-start.2
  1.1 0.0 copy-start.1
  1.1 0.5 %collective-permute-start = (bf16[4,32,128]{2,1,0:T(8,128)(2,1)S(1)}, bf16[4,32,128]{2,1,0:T(8,128)(2,1)S(1)}, u32[]{:S(2)}, u32[]{:S(2)}) collective-permute-start(bf16[4,32,128]{2,1,0:T(8,128)(2,1)S(1)} %get-tuple-element.15), channel_id=1, source_target_pairs={{1,0},{0,1},{3,2},{2,3},{5,4},{4,5},{7,6},{6,7},{9,8},{8,9},{11,10... | collective-permute-start | bytes 98312 | tf_op jit(solution)/shard_map/ppermute | solution.py:286
  1.6 0.0 copy-done
  1.6 1.4 %send_blocks.1 = bf16[2,4,48,128]{3,2,1,0:T(8,128)(2,1)} custom-call(bf16[32,512]{1,0:T(8,128)(2,1)S(1)} %get-tuple-element.12.dft_ref, bf16[2,1024,512]{2,1,0:T(8,128)(2,1)S(1)} %bitcast.6), custom_call_target="tpu_custom_call" | custom-call | tf_op jit(solution)/shard_map/send_blocks/pallas_call | solution.py:335
  3.0 6.3 %all-to-all-start = ((bf16[8,48,128]{2,1,0:T(8,128)(2,1)}), bf16[8,48,128]{2,1,0:T(8,128)(2,1)S(1)}, u32[]{:S(2)}, u32[]{:S(2)}) async-start(bf16[8,48,128]{2,1,0:T(8,128)(2,1)} %bitcast.2), calls=%async_computation | async-start | bytes 196608 | tf_op jit(solution)/shard_map/all_to_all | solution.py:346
  9.3 0.0 copy-done.2
  9.3 0.1 reshape.14.filt_ref
  9.5 0.0 collective-permute-done.refs_0_
  9.5 0.0 copy-start.3
  9.5 0.6 %copy-done.3 = bf16[4,32,128]{2,1,0:T(8,128)(2,1)} copy-done((bf16[4,32,128]{2,1,0:T(8,128)(2,1)}, bf16[4,32,128]{2,1,0:T(8,128)(2,1)S(1)}, u32[]{:S(2)}) %copy-start.3) | copy-done | bytes 32792
  10.1 0.0 copy-done.1
  10.1 2.1 %source_fields.1 = (bf16[3,1664,256]{2,1,0:T(8,128)(2,1)S(1)}, f32[2,128,128]{2,1,0:T(8,128)S(1)}, f32[2,3,128,128]{3,2,1,0:T(8,128)S(1)}) custom-call(s32[8,128]{1,0:T(8,128)S(1)} %get-tuple-element.13.own_ref, f32[8,128]{1,0:T(8,128)S(1)} %get-tuple-element.14.wave_ref, bf16[676,256]{1,0:T(8,128)(2,1)S(1)} %reshape.14.filt_ref, f32[1,64]{1,0:T(1,128)} %bitcast.9, ...), custom_call_target="tpu_custom_call" | custom-call | flops 4000000000 | bytes 10000000 | tf_op jit(solution)/shard_map/source_fields/pallas_call | solution.py:356
  12.3 3.5 %all-to-all-done.recv_ref = bf16[8,48,128]{2,1,0:T(8,128)(2,1)S(1)} async-done(((bf16[8,48,128]{2,1,0:T(8,128)(2,1)}), bf16[8,48,128]{2,1,0:T(8,128)(2,1)S(1)}, u32[]{:S(2)}, u32[]{:S(2)}) %all-to-all-start) | async-done | bytes 98336 | tf_op jit(solution)/shard_map/all_to_all | solution.py:346
  15.8 1.3 %migrate.1 = bf16[16,16,128]{2,1,0:T(8,128)(2,1)S(1)} custom-call(bf16[8,48,128]{2,1,0:T(8,128)(2,1)S(1)} %all-to-all-done.recv_ref, bf16[3,1664,256]{2,1,0:T(8,128)(2,1)S(1)} %get-tuple-element.16.band_ref, f32[2,128,128]{2,1,0:T(8,128)S(1)} %get-tuple-element.17.blend_ref, f32[2,3,128,128]{3,2,1,0:T(8,128)S(1)} %get-tuple-element.18.source_ref), custom_call_target="tpu_custom_call" | custom-call | tf_op jit(solution)/shard_map/migrate/pallas_call | solution.py:383
  17.1 9.3 %all_to_all.10 = bf16[16,16,128]{2,1,0:T(8,128)(2,1)S(1)} all-to-all(bf16[16,16,128]{2,1,0:T(8,128)(2,1)S(1)} %migrate.1), channel_id=1, replica_groups=mesh['group'=2,'freq'=4,'shot'=2,'half'=2] {'freq','half','shot'}, dimensions={0} | all-to-all | bytes 131072 | tf_op jit(solution)/shard_map/all_to_all | solution.py:396
  26.4 0.6 %convert_reduce_fusion = f32[16,128]{1,0:T(8,128)} fusion(bf16[16,16,128]{2,1,0:T(8,128)(2,1)S(1)} %all_to_all.10), kind=kLoop, calls=%fused_computation | loop fusion | flops 63488 | bytes 73728 | tf_op jit(solution)/shard_map/reduce_sum | solution.py:397
Async XLA Ops:
  0.0 1.6 %copy-start = (bf16[2,32,32,512]{3,2,1,0:T(8,128)(2,1)S(1)}, bf16[2,32,32,512]{3,2,1,0:T(8,128)(2,1)}, u32[]{:S(2)}) copy-start(bf16[2,32,32,512]{3,2,1,0:T(8,128)(2,1)} %param.8) | copy-start | bytes 6291460
  1.1 8.3 %copy-start.2 = (bf16[2,2,13,13,256]{4,1,3,2,0:T(2,128)(2,1)S(1)}, bf16[2,2,13,13,256]{4,1,3,2,0:T(2,128)(2,1)}, u32[]{:S(2)}) copy-start(bf16[2,2,13,13,256]{4,1,3,2,0:T(2,128)(2,1)} %param.11) | copy-start | bytes 1038340
  1.1 9.0 %copy-start.1 = (bf16[2,32,128]{2,1,0:T(8,128)(2,1)S(1)}, bf16[2,32,128]{2,1,0:T(8,128)(2,1)}, u32[]{:S(2)}) copy-start(bf16[2,32,128]{2,1,0:T(8,128)(2,1)} %pattern_hbm.3) | copy-start | bytes 49156
  1.1 8.4 %collective-permute-start = (bf16[4,32,128]{2,1,0:T(8,128)(2,1)S(1)}, bf16[4,32,128]{2,1,0:T(8,128)(2,1)S(1)}, u32[]{:S(2)}, u32[]{:S(2)}) collective-permute-start(bf16[4,32,128]{2,1,0:T(8,128)(2,1)S(1)} %get-tuple-element.15), channel_id=1, source_target_pairs={{1,0},{0,1},{3,2},{2,3},{5,4},{4,5},{7,6},{6,7},{9,8},{8,9},{11,10... | collective-permute-start | bytes 98312 | tf_op jit(solution)/shard_map/ppermute | solution.py:286
  3.0 12.8 %all-to-all-start = ((bf16[8,48,128]{2,1,0:T(8,128)(2,1)}), bf16[8,48,128]{2,1,0:T(8,128)(2,1)S(1)}, u32[]{:S(2)}, u32[]{:S(2)}) async-start(bf16[8,48,128]{2,1,0:T(8,128)(2,1)} %bitcast.2), calls=%async_computation | async-start | bytes 196608 | tf_op jit(solution)/shard_map/all_to_all | solution.py:346
  9.5 0.6 %copy-start.3 = (bf16[4,32,128]{2,1,0:T(8,128)(2,1)}, bf16[4,32,128]{2,1,0:T(8,128)(2,1)S(1)}, u32[]{:S(2)}) copy-start(bf16[4,32,128]{2,1,0:T(8,128)(2,1)S(1)} %collective-permute-done.refs_0_) | copy-start | bytes 98308

commit v9 on v6

--- a/solution.py
+++ b/solution.py
@@ -148,14 +148,13 @@
 def run_steps(taps, depth, field_ref, band_ref, blend_ref, prepare, use):
     rows = field_ref.shape[1] - 2 * ROW_PAD
     order = [(step, plane) for step in range(depth) for plane in range(FPD)]
-    prepare(0)
+    for plane in range(FPD):
+        prepare(plane)
     left = shifted(taps, field_ref.at[0])
     for at, (step, plane) in enumerate(order):
         follow = None
         if at + 1 < len(order):
             after = order[at + 1][1]
-            if order[at + 1][0] == 0:
-                prepare(after)
             follow = shifted(taps, field_ref.at[after])
         new = advance(left, band_ref.at[plane], blend_ref[step])
         if step + 1 < depth:

time: 27.4 us -> 27.4 us (level)
  no operation moved by 1% of the time
where the time goes in v9:
time: 27.4 us; the launch traced here: 27.1 us
  blocking collectives  9.35 us (34%)
  starting transfers between devices  6.91 us (25%)
  Pallas kernels  5.84 us (21%)
  waiting for transfers between devices  3.52 us (13%)
  local copies, waits for them, and re-layouts  0.75 us (3%)
  other arithmetic  0.62 us (2%)
    all_to_all x1, blocking collectives, body(): terms = lax.all_to_all(terms, ('freq', 'half', 'shot'), 0, 0, tiled=True)  9.35 us
    all_to_all x1, starting transfers between devices, body(): recv = lax.all_to_all(send, ('half', 'freq'), 0, 0, tiled=True)  6.3 us
    all_to_all x1, waiting for transfers between devices, body(): recv = lax.all_to_all(send, ('half', 'freq'), 0, 0, tiled=True)  3.52 us
    pallas_call x1, Pallas kernels, body(): pl.pallas_call(functools.partial(source_kernel, taps, nref, depth, halves...  2.17 us
    pallas_call x1, Pallas kernels, body(): pl.pallas_call(functools.partial(send_kernel, groups, folded), out_shape=...  1.37 us
    pallas_call x1, Pallas kernels, body(): pl.pallas_call(functools.partial(migrate_kernel, (groups, halves, copies,...  1.27 us
    pallas_call x1, Pallas kernels, body(): pl.pallas_call(functools.partial(prepare_kernel, groups), out_shape=[jax....  1.04 us
    unnamed x10, local copies, waits for them, and re-layouts  0.62 us
  transfers between devices with their start and end apart: 3, of which 1 were waited for; matrix products, arithmetic and copies ran while one was open for 0% of the time, Pallas kernels for 13%

profile of v9, /device:TPU:0, one launch (start us, length us, event | category | flops | bytes accessed | tf_op | source)
XLA Modules:
  0.0 27.1 jit_solution(4346957347333467836)
XLA Ops:
  0.0 0.0 copy-start.2
  0.0 0.0 copy-start.4
  0.0 0.0 copy-start
  0.0 1.0 %prepare.1 = (bf16[32,512]{1,0:T(8,128)(2,1)S(1)}, s32[8,128]{1,0:T(8,128)S(1)}, f32[8,128]{1,0:T(8,128)S(1)}) custom-call(s32[4,6]{1,0:T(4,128)} %plan_hbm.1, s32[4]{0:T(128)} %counts_hbm.1, f32[2,256]{1,0:T(2,128)} %bitcast.8), custom_call_target="tpu_custom_call" | custom-call | flops 3000000000 | bytes 4000000 | tf_op jit(solution)/shard_map/prepare/pallas_call | solution.py:298
  1.1 0.0 copy-start.1
  1.1 0.0 copy-done.2
  1.1 0.5 %collective-permute-start = (s32[2,32,128]{2,1,0:T(8,128)S(1)}, s32[2,32,128]{2,1,0:T(8,128)S(1)}, u32[]{:S(2)}, u32[]{:S(2)}) collective-permute-start(s32[2,32,128]{2,1,0:T(8,128)S(1)} %copy-done.2), channel_id=1, source_target_pairs={{1,0},{0,1},{3,2},{2,3},{5,4},{4,5},{7,6},{6,7},{9,8},{8,9},{11,10... | collective-permute-start | bytes 98312 | tf_op jit(solution)/shard_map/ppermute | solution.py:272
  1.6 0.0 copy-done.4
  1.6 0.1 collective-permute-start.1
  1.7 0.0 copy-done
  1.7 1.4 %send_blocks.1 = bf16[2,4,48,128]{3,2,1,0:T(8,128)(2,1)} custom-call(bf16[32,512]{1,0:T(8,128)(2,1)S(1)} %get-tuple-element.14.dft_ref, bf16[2,1024,512]{2,1,0:T(8,128)(2,1)S(1)} %bitcast.6), custom_call_target="tpu_custom_call" | custom-call | tf_op jit(solution)/shard_map/send_blocks/pallas_call | solution.py:321
  3.1 6.3 %all-to-all-start = ((bf16[8,48,128]{2,1,0:T(8,128)(2,1)}), bf16[8,48,128]{2,1,0:T(8,128)(2,1)S(1)}, u32[]{:S(2)}, u32[]{:S(2)}) async-start(bf16[8,48,128]{2,1,0:T(8,128)(2,1)} %bitcast.2), calls=%async_computation | async-start | bytes 196608 | tf_op jit(solution)/shard_map/all_to_all | solution.py:332
  9.4 0.0 copy-done.1
  9.4 0.1 reshape.14.filt_ref
  9.5 0.0 collective-permute-done.1.refs_3_
  9.5 0.0 collective-permute-done.refs_1_
  9.5 0.0 copy-start.3
  9.5 0.6 %copy-done.3 = s32[2,32,128]{2,1,0:T(8,128)} copy-done((s32[2,32,128]{2,1,0:T(8,128)}, s32[2,32,128]{2,1,0:T(8,128)S(1)}, u32[]{:S(2)}) %copy-start.3) | copy-done | bytes 32792
  10.1 2.2 %source_fields.1 = (bf16[3,1664,256]{2,1,0:T(8,128)(2,1)S(1)}, f32[2,128,128]{2,1,0:T(8,128)S(1)}, f32[2,3,128,128]{3,2,1,0:T(8,128)S(1)}) custom-call(s32[8,128]{1,0:T(8,128)S(1)} %get-tuple-element.16.own_ref, f32[8,128]{1,0:T(8,128)S(1)} %get-tuple-element.17.wave_ref, bf16[676,256]{1,0:T(8,128)(2,1)S(1)} %reshape.14.filt_ref, f32[1,64]{1,0:T(1,128)} %bitcast.9, ...), custom_call_target="tpu_custom_call" | custom-call | flops 4000000000 | bytes 10000000 | tf_op jit(solution)/shard_map/source_fields/pallas_call | solution.py:342
  12.3 3.5 %all-to-all-done.recv_ref = bf16[8,48,128]{2,1,0:T(8,128)(2,1)S(1)} async-done(((bf16[8,48,128]{2,1,0:T(8,128)(2,1)}), bf16[8,48,128]{2,1,0:T(8,128)(2,1)S(1)}, u32[]{:S(2)}, u32[]{:S(2)}) %all-to-all-start) | async-done | bytes 98336 | tf_op jit(solution)/shard_map/all_to_all | solution.py:332
  15.8 1.3 %migrate.1 = bf16[16,16,128]{2,1,0:T(8,128)(2,1)S(1)} custom-call(bf16[8,48,128]{2,1,0:T(8,128)(2,1)S(1)} %all-to-all-done.recv_ref, bf16[3,1664,256]{2,1,0:T(8,128)(2,1)S(1)} %get-tuple-element.20.band_ref, f32[2,128,128]{2,1,0:T(8,128)S(1)} %get-tuple-element.21.blend_ref, f32[2,3,128,128]{3,2,1,0:T(8,128)S(1)} %get-tuple-element.22.source_ref), custom_call_target="tpu_custom_call" | custom-call | tf_op jit(solution)/shard_map/migrate/pallas_call | solution.py:368
  17.1 9.3 %all_to_all.10 = bf16[16,16,128]{2,1,0:T(8,128)(2,1)S(1)} all-to-all(bf16[16,16,128]{2,1,0:T(8,128)(2,1)S(1)} %migrate.1), channel_id=1, replica_groups=mesh['group'=2,'freq'=4,'shot'=2,'half'=2] {'freq','half','shot'}, dimensions={0} | all-to-all | bytes 131072 | tf_op jit(solution)/shard_map/all_to_all | solution.py:381
  26.5 0.6 %convert_reduce_fusion = f32[16,128]{1,0:T(8,128)} fusion(bf16[16,16,128]{2,1,0:T(8,128)(2,1)S(1)} %all_to_all.10), kind=kLoop, calls=%fused_computation | loop fusion | flops 63488 | bytes 73728 | tf_op jit(solution)/shard_map/reduce_sum | solution.py:382
Async XLA Ops:
  0.0 1.1 %copy-start.2 = (s32[2,32,128]{2,1,0:T(8,128)S(1)}, s32[2,32,128]{2,1,0:T(8,128)}, u32[]{:S(2)}) copy-start(s32[2,32,128]{2,1,0:T(8,128)} %refs_0_) | copy-start | bytes 98308
  0.0 1.6 %copy-start.4 = (bf16[2,32,128]{2,1,0:T(8,128)(2,1)S(1)}, bf16[2,32,128]{2,1,0:T(8,128)(2,1)}, u32[]{:S(2)}) copy-start(bf16[2,32,128]{2,1,0:T(8,128)(2,1)} %refs_2_) | copy-start | bytes 49156
  0.0 1.7 %copy-start = (bf16[2,32,32,512]{3,2,1,0:T(8,128)(2,1)S(1)}, bf16[2,32,32,512]{3,2,1,0:T(8,128)(2,1)}, u32[]{:S(2)}) copy-start(bf16[2,32,32,512]{3,2,1,0:T(8,128)(2,1)} %param.8) | copy-start | bytes 6291460
  1.1 8.3 %copy-start.1 = (bf16[2,2,13,13,256]{4,1,3,2,0:T(2,128)(2,1)S(1)}, bf16[2,2,13,13,256]{4,1,3,2,0:T(2,128)(2,1)}, u32[]{:S(2)}) copy-start(bf16[2,2,13,13,256]{4,1,3,2,0:T(2,128)(2,1)} %param.11) | copy-start | bytes 1038340
  1.1 8.4 %collective-permute-start = (s32[2,32,128]{2,1,0:T(8,128)S(1)}, s32[2,32,128]{2,1,0:T(8,128)S(1)}, u32[]{:S(2)}, u32[]{:S(2)}) collective-permute-start(s32[2,32,128]{2,1,0:T(8,128)S(1)} %copy-done.2), channel_id=1, source_target_pairs={{1,0},{0,1},{3,2},{2,3},{5,4},{4,5},{7,6},{6,7},{9,8},{8,9},{11,10... | collective-permute-start | bytes 98312 | tf_op jit(solution)/shard_map/ppermute | solution.py:272
  1.6 7.9 %collective-permute-start.1 = (bf16[2,32,128]{2,1,0:T(8,128)(2,1)S(1)}, bf16[2,32,128]{2,1,0:T(8,128)(2,1)S(1)}, u32[]{:S(2)}, u32[]{:S(2)}) collective-permute-start(bf16[2,32,128]{2,1,0:T(8,128)(2,1)S(1)} %copy-done.4), channel_id=1, source_target_pairs={{1,0},{0,1},{3,2},{2,3},{5,4},{4,5},{7,6},{6,7},{9,8},{8,9},{11,10... | collective-permute-start | bytes 49160 | tf_op jit(solution)/shard_map/ppermute | solution.py:272
  3.1 12.8 %all-to-all-start = ((bf16[8,48,128]{2,1,0:T(8,128)(2,1)}), bf16[8,48,128]{2,1,0:T(8,128)(2,1)S(1)}, u32[]{:S(2)}, u32[]{:S(2)}) async-start(bf16[8,48,128]{2,1,0:T(8,128)(2,1)} %bitcast.2), calls=%async_computation | async-start | bytes 196608 | tf_op jit(solution)/shard_map/all_to_all | solution.py:332
  9.5 0.6 %copy-start.3 = (s32[2,32,128]{2,1,0:T(8,128)}, s32[2,32,128]{2,1,0:T(8,128)S(1)}, u32[]{:S(2)}) copy-start(s32[2,32,128]{2,1,0:T(8,128)S(1)} %collective-permute-done.refs_1_) | copy-start | bytes 98308

commit v10 on v8

--- a/solution.py
+++ b/solution.py
@@ -58,9 +58,23 @@
     return lax.dot_general(dft, block, (((1,), (1,)), ((), ())), preferred_element_type=F32)
 
 
+def put_spectra(groups, folded, out, put, tmp_ref):
+    if not folded:
+        put[...] = out.astype(BF16)
+        return
+    for group in range(groups):
+        base = group * SUB * SUB
+        for high in range(SUB):
+            tmp_ref[pl.ds(base + high, SUB, stride=SUB), :] = out[
+                group * SUB : (group + 1) * SUB, high * LANES : (high + 1) * LANES
+            ]
+        put[group] = tmp_ref[base : base + 2 * FPD * SUB].astype(BF16)
+
+
 def prepare_kernel(
-    groups, plan_hbm, counts_hbm, wav_hbm, class_hbm, pattern_hbm, dft_ref, own_ref, wave_ref, shared_ref,
-    plan_ref, counts_ref, wav_ref, class_ref, bins_ref, sems,
+    groups, folded, plan_hbm, counts_hbm, wav_hbm, class_hbm, pattern_hbm, rec_hbm,
+    dft_ref, own_ref, wave_ref, shared_ref, early_ref, last_ref,
+    plan_ref, counts_ref, wav_ref, class_ref, bins_ref, rec_ref, tmp_ref, sems,
 ):
     nt = dft_ref.shape[1]
     depth, shots = class_hbm.shape[0], pattern_hbm.shape[0]
@@ -73,7 +87,11 @@
         pltpu.make_async_copy(counts_hbm, counts_ref, sems.at[1]),
         pltpu.make_async_copy(wav_hbm, wav_ref, sems.at[2]),
     ]
-    for copy in small + later:
+    early = [
+        pltpu.make_async_copy(rec_hbm.at[shot], rec_ref.at[shot], sems.at[5 + shot]) for shot in range(shots - 1)
+    ]
+    last = pltpu.make_async_copy(rec_hbm.at[shots - 1], last_ref, sems.at[4 + shots])
+    for copy in small + early + later + [last]:
         copy.start()
     for copy in small:
         copy.wait()
@@ -90,23 +108,18 @@
     for copy in later:
         copy.wait()
     shared_ref[:depth] = class_ref[...].astype(BF16)
-
-
-def send_kernel(groups, folded, dft_ref, rec_ref, out_ref, tmp_ref):
-    shots, cells, _ = rec_ref.shape
-    dft = dft_ref[...]
-    for shot in range(shots):
-        out = transform(dft, rec_ref[shot])
-        if not folded:
-            out_ref[shot] = out.astype(BF16)
-            continue
-        for group in range(groups):
-            base = (group * shots + shot) * SUB * SUB
-            for high in range(SUB):
-                tmp_ref[pl.ds(base + high, SUB, stride=SUB), :] = out[
-                    group * SUB : (group + 1) * SUB, high * LANES : (high + 1) * LANES
-                ]
-            out_ref[shot, group] = tmp_ref[base : base + 2 * FPD * SUB].astype(BF16)
+    for shot, copy in enumerate(early):
+        copy.wait()
+        put_spectra(groups, folded, transform(dft_ref[...], rec_ref[shot]), early_ref.at[shot], tmp_ref)
+    last.wait()
+
+
+def send_kernel(groups, folded, dft_ref, early_ref, last_ref, out_ref, tmp_ref):
+    early = early_ref.shape[0]
+    out = transform(dft_ref[...], last_ref[...])
+    for shot in range(early):
+        out_ref[shot] = early_ref[shot]
+    put_spectra(groups, folded, out, out_ref.at[early], tmp_ref)
 
 
 def make_bands(taps, nref, ny, picked_ref, band_ref):
@@ -156,14 +169,13 @@
 def run_steps(taps, depth, field_ref, band_ref, blend_ref, prepare, use):
     rows = field_ref.shape[1] - 2 * ROW_PAD
     order = [(step, plane) for step in range(depth) for plane in range(FPD)]
-    prepare(0)
+    for plane in range(FPD):
+        prepare(plane)
     left = shifted(taps, field_ref.at[0])
     for at, (step, plane) in enumerate(order):
         follow = None
         if at + 1 < len(order):
             after = order[at + 1][1]
-            if order[at + 1][0] == 0:
-                prepare(after)
             follow = shifted(taps, field_ref.at[after])
         new = advance(left, band_ref.at[plane], blend_ref[step])
         if step + 1 < depth:
@@ -309,38 +321,44 @@
     else:
         send_shape = (shots, groups * SUB, cells)
     table = filters.transpose(0, 2, 3, 1, 4)
-    dft, own, wave, shared = pl.pallas_call(
-        functools.partial(prepare_kernel, groups),
+    flat = records.reshape(shots, cells, nt)
+    tmp = pltpu.VMEM((groups * SUB * SUB + SUB, LANES), F32)
+    dft, own, wave, shared, early, last = pl.pallas_call(
+        functools.partial(prepare_kernel, groups, folded),
         out_shape=[
             jax.ShapeDtypeStruct((groups * SUB, nt), BF16),
             jax.ShapeDtypeStruct((SUB, LANES), jnp.int32),
             jax.ShapeDtypeStruct((SUB, LANES), F32),
             jax.ShapeDtypeStruct((depth + shots, rows, nx), BF16),
+            jax.ShapeDtypeStruct((shots - 1,) + send_shape[1:], BF16),
+            jax.ShapeDtypeStruct((cells, nt), BF16),
         ],
-        in_specs=[hbm()] * 5,
-        out_specs=[vmem()] * 4,
+        in_specs=[hbm()] * 6,
+        out_specs=[vmem()] * 6,
         scratch_shapes=[
             pltpu.SMEM(freq_plan.shape, jnp.int32),
             pltpu.SMEM(counts.shape, jnp.int32),
             pltpu.SMEM((2, nbin), F32),
             pltpu.VMEM(vel_index.shape, jnp.int32),
             bins,
-            pltpu.SemaphoreType.DMA((5,)),
+            pltpu.VMEM((shots - 1, cells, nt), BF16),
+            tmp,
+            pltpu.SemaphoreType.DMA((5 + shots,)),
         ],
         compiler_params=params,
         cost_estimate=pl.CostEstimate(flops=3 * 10**9, bytes_accessed=4 * 10**6, transcendentals=0),
         name="prepare",
-    )(*pinned(freq_plan, counts, wavelet.T, vel_index, source_pattern))
+    )(*pinned(freq_plan, counts, wavelet.T, vel_index, source_pattern, flat))
     others = from_halves(shared, halves)[1:]
     send = pl.pallas_call(
         functools.partial(send_kernel, groups, folded),
         out_shape=jax.ShapeDtypeStruct(send_shape, BF16),
-        in_specs=[vmem()] * 2,
+        in_specs=[vmem()] * 3,
         out_specs=vmem(),
-        scratch_shapes=[pltpu.VMEM((groups * shots * SUB * SUB + SUB, LANES), F32)],
+        scratch_shapes=[tmp],
         compiler_params=params,
         name="send_blocks",
-    )(dft, records.reshape(shots, cells, nt))
+    )(dft, early, last)
     if folded:
         send = send.reshape(groups * halves, items * SUB, LANES)
         recv = lax.all_to_all(send, ("half", "freq"), 0, 0, tiled=True)

time: 27.3 us -> 27.4 us (level)
  Pallas kernels: 5.86 us -> 6.24 us
  starting transfers between devices: 6.84 us -> 6.51 us
    pallas_call x1, Pallas kernels: 1.06 us -> 1.76 us  [body(): pl.pallas_call(functools.partial(prepare_kernel, groups, folded), out_sha...]
    all_to_all x1, starting transfers between devices: 6.32 us -> 5.99 us  [body(): recv = lax.all_to_all(send, ('half', 'freq'), 0, 0, tiled=True)]
    pallas_call x1, Pallas kernels: 1.38 us -> 1.06 us  [body(): pl.pallas_call(functools.partial(send_kernel, groups, folded), out_shape=...]
    unnamed x8 -> x6, local copies, waits for them, and re-layouts: 0.63 us -> 0.6 us
  transfers between devices with their start and end apart: 2 -> 2, of which waited for: 1 -> 1; matrix products, arithmetic and copies ran while one was open for 0% -> 0% of each run, Pallas kernels for 13% -> 12%
where the time goes in v10:
time: 27.4 us; the launch traced here: 27.1 us
  blocking collectives  9.35 us (34%)
  starting transfers between devices  6.51 us (24%)
  Pallas kernels  6.24 us (23%)
  waiting for transfers between devices  3.56 us (13%)
  local copies, waits for them, and re-layouts  0.73 us (3%)
  other arithmetic  0.62 us (2%)
    all_to_all x1, blocking collectives, body(): terms = lax.all_to_all(terms, ('freq', 'half', 'shot'), 0, 0, tiled=True)  9.35 us
    all_to_all x1, starting transfers between devices, body(): recv = lax.all_to_all(send, ('half', 'freq'), 0, 0, tiled=True)  5.99 us
    all_to_all x1, waiting for transfers between devices, body(): recv = lax.all_to_all(send, ('half', 'freq'), 0, 0, tiled=True)  3.56 us
    pallas_call x1, Pallas kernels, body(): pl.pallas_call(functools.partial(source_kernel, taps, nref, depth, halves...  2.15 us
    pallas_call x1, Pallas kernels, body(): pl.pallas_call(functools.partial(prepare_kernel, groups, folded), out_sha...  1.76 us
    pallas_call x1, Pallas kernels, body(): pl.pallas_call(functools.partial(migrate_kernel, (groups, halves, copies,...  1.27 us
    pallas_call x1, Pallas kernels, body(): pl.pallas_call(functools.partial(send_kernel, groups, folded), out_shape=...  1.06 us
    reduce_sum x1, other arithmetic, body(): return jnp.sum(terms.astype(F32), axis=0).reshape(1, share, depth, nx)  0.62 us
  transfers between devices with their start and end apart: 2, of which 1 were waited for; matrix products, arithmetic and copies ran while one was open for 0% of the time, Pallas kernels for 12%

profile of v10, /device:TPU:0, one launch (start us, length us, event | category | flops | bytes accessed | tf_op | source)
XLA Modules:
  0.0 27.1 jit_solution(16896090806637298325)
XLA Ops:
  0.0 0.0 copy-start.1
  0.0 0.0 copy-start
  0.0 1.8 %prepare.1 = (bf16[32,512]{1,0:T(8,128)(2,1)S(1)}, s32[8,128]{1,0:T(8,128)S(1)}, f32[8,128]{1,0:T(8,128)S(1)}, bf16[4,32,128]{2,1,0:T(8,128)(2,1)S(1)}, bf16[1,4...) custom-call(s32[4,6]{1,0:T(4,128)} %plan_hbm.1, s32[4]{0:T(128)} %counts_hbm.1, f32[2,256]{1,0:T(2,128)} %bitcast.8, ...), custom_call_target="tpu_custom_call" | custom-call | flops 3000000000 | bytes 4000000 | tf_op jit(solution)/shard_map/prepare/pallas_call | solution.py:326
  1.8 0.5 %collective-permute-start = (bf16[4,32,128]{2,1,0:T(8,128)(2,1)S(1)}, bf16[4,32,128]{2,1,0:T(8,128)(2,1)S(1)}, u32[]{:S(2)}, u32[]{:S(2)}) collective-permute-start(bf16[4,32,128]{2,1,0:T(8,128)(2,1)S(1)} %get-tuple-element.19), channel_id=1, source_target_pairs={{1,0},{0,1},{3,2},{2,3},{5,4},{4,5},{7,6},{6,7},{9,8},{8,9},{11,10... | collective-permute-start | bytes 98312 | tf_op jit(solution)/shard_map/ppermute | solution.py:298
  2.3 1.1 %send_blocks.1 = bf16[2,4,48,128]{3,2,1,0:T(8,128)(2,1)} custom-call(bf16[32,512]{1,0:T(8,128)(2,1)S(1)} %get-tuple-element.14.dft_ref, bf16[1,4,48,128]{3,2,1,0:T(8,128)(2,1)S(1)} %get-tuple-element.15.early_ref, bf16[1024,512]{1,0:T(8,128)(2,1)S(1)} %get-tuple-element.16.last_ref), custom_call_target="tpu_custom_call" | custom-call | tf_op jit(solution)/shard_map/send_blocks/pallas_call | solution.py:353
  3.4 6.0 %all-to-all-start = ((bf16[8,48,128]{2,1,0:T(8,128)(2,1)}), bf16[8,48,128]{2,1,0:T(8,128)(2,1)S(1)}, u32[]{:S(2)}, u32[]{:S(2)}) async-start(bf16[8,48,128]{2,1,0:T(8,128)(2,1)} %bitcast.2), calls=%async_computation | async-start | bytes 196608 | tf_op jit(solution)/shard_map/all_to_all | solution.py:364
  9.3 0.0 copy-done.1
  9.4 0.1 reshape.14.filt_ref
  9.5 0.0 collective-permute-done.refs_0_
  9.5 0.0 copy-start.2
  9.5 0.6 %copy-done.2 = bf16[4,32,128]{2,1,0:T(8,128)(2,1)} copy-done((bf16[4,32,128]{2,1,0:T(8,128)(2,1)}, bf16[4,32,128]{2,1,0:T(8,128)(2,1)S(1)}, u32[]{:S(2)}) %copy-start.2) | copy-done | bytes 32792
  10.1 0.0 copy-done
  10.1 2.1 %source_fields.1 = (bf16[3,1664,256]{2,1,0:T(8,128)(2,1)S(1)}, f32[2,128,128]{2,1,0:T(8,128)S(1)}, f32[2,3,128,128]{3,2,1,0:T(8,128)S(1)}) custom-call(s32[8,128]{1,0:T(8,128)S(1)} %get-tuple-element.17.own_ref, f32[8,128]{1,0:T(8,128)S(1)} %get-tuple-element.18.wave_ref, bf16[676,256]{1,0:T(8,128)(2,1)S(1)} %reshape.14.filt_ref, f32[1,64]{1,0:T(1,128)} %bitcast.9, ...), custom_call_target="tpu_custom_call" | custom-call | flops 4000000000 | bytes 10000000 | tf_op jit(solution)/shard_map/source_fields/pallas_call | solution.py:374
  12.3 3.6 %all-to-all-done.recv_ref = bf16[8,48,128]{2,1,0:T(8,128)(2,1)S(1)} async-done(((bf16[8,48,128]{2,1,0:T(8,128)(2,1)}), bf16[8,48,128]{2,1,0:T(8,128)(2,1)S(1)}, u32[]{:S(2)}, u32[]{:S(2)}) %all-to-all-start) | async-done | bytes 98336 | tf_op jit(solution)/shard_map/all_to_all | solution.py:364
  15.8 1.3 %migrate.1 = bf16[16,16,128]{2,1,0:T(8,128)(2,1)S(1)} custom-call(bf16[8,48,128]{2,1,0:T(8,128)(2,1)S(1)} %all-to-all-done.recv_ref, bf16[3,1664,256]{2,1,0:T(8,128)(2,1)S(1)} %get-tuple-element.20.band_ref, f32[2,128,128]{2,1,0:T(8,128)S(1)} %get-tuple-element.21.blend_ref, f32[2,3,128,128]{3,2,1,0:T(8,128)S(1)} %get-tuple-element.22.source_ref), custom_call_target="tpu_custom_call" | custom-call | tf_op jit(solution)/shard_map/migrate/pallas_call | solution.py:401
  17.1 9.3 %all_to_all.10 = bf16[16,16,128]{2,1,0:T(8,128)(2,1)S(1)} all-to-all(bf16[16,16,128]{2,1,0:T(8,128)(2,1)S(1)} %migrate.1), channel_id=1, replica_groups=mesh['group'=2,'freq'=4,'shot'=2,'half'=2] {'freq','half','shot'}, dimensions={0} | all-to-all | bytes 131072 | tf_op jit(solution)/shard_map/all_to_all | solution.py:414
  26.4 0.6 %convert_reduce_fusion = f32[16,128]{1,0:T(8,128)} fusion(bf16[16,16,128]{2,1,0:T(8,128)(2,1)S(1)} %all_to_all.10), kind=kLoop, calls=%fused_computation | loop fusion | flops 63488 | bytes 73728 | tf_op jit(solution)/shard_map/reduce_sum | solution.py:415
Async XLA Ops:
  0.0 9.3 %copy-start.1 = (bf16[2,2,13,13,256]{4,1,3,2,0:T(2,128)(2,1)S(1)}, bf16[2,2,13,13,256]{4,1,3,2,0:T(2,128)(2,1)}, u32[]{:S(2)}) copy-start(bf16[2,2,13,13,256]{4,1,3,2,0:T(2,128)(2,1)} %param.11) | copy-start | bytes 1038340
  0.0 10.1 %copy-start = (bf16[2,32,128]{2,1,0:T(8,128)(2,1)S(1)}, bf16[2,32,128]{2,1,0:T(8,128)(2,1)}, u32[]{:S(2)}) copy-start(bf16[2,32,128]{2,1,0:T(8,128)(2,1)} %pattern_hbm.3) | copy-start | bytes 49156
  1.8 7.7 %collective-permute-start = (bf16[4,32,128]{2,1,0:T(8,128)(2,1)S(1)}, bf16[4,32,128]{2,1,0:T(8,128)(2,1)S(1)}, u32[]{:S(2)}, u32[]{:S(2)}) collective-permute-start(bf16[4,32,128]{2,1,0:T(8,128)(2,1)S(1)} %get-tuple-element.19), channel_id=1, source_target_pairs={{1,0},{0,1},{3,2},{2,3},{5,4},{4,5},{7,6},{6,7},{9,8},{8,9},{11,10... | collective-permute-start | bytes 98312 | tf_op jit(solution)/shard_map/ppermute | solution.py:298
  3.4 12.5 %all-to-all-start = ((bf16[8,48,128]{2,1,0:T(8,128)(2,1)}), bf16[8,48,128]{2,1,0:T(8,128)(2,1)S(1)}, u32[]{:S(2)}, u32[]{:S(2)}) async-start(bf16[8,48,128]{2,1,0:T(8,128)(2,1)} %bitcast.2), calls=%async_computation | async-start | bytes 196608 | tf_op jit(solution)/shard_map/all_to_all | solution.py:364
  9.5 0.6 %copy-start.2 = (bf16[4,32,128]{2,1,0:T(8,128)(2,1)}, bf16[4,32,128]{2,1,0:T(8,128)(2,1)S(1)}, u32[]{:S(2)}) copy-start(bf16[4,32,128]{2,1,0:T(8,128)(2,1)S(1)} %collective-permute-done.refs_0_) | copy-start | bytes 98308

commit v11 on v8

--- a/solution.py
+++ b/solution.py
@@ -156,14 +156,13 @@
 def run_steps(taps, depth, field_ref, band_ref, blend_ref, prepare, use):
     rows = field_ref.shape[1] - 2 * ROW_PAD
     order = [(step, plane) for step in range(depth) for plane in range(FPD)]
-    prepare(0)
+    for plane in range(FPD):
+        prepare(plane)
     left = shifted(taps, field_ref.at[0])
     for at, (step, plane) in enumerate(order):
         follow = None
         if at + 1 < len(order):
             after = order[at + 1][1]
-            if order[at + 1][0] == 0:
-                prepare(after)
             follow = shifted(taps, field_ref.at[after])
         new = advance(left, band_ref.at[plane], blend_ref[step])
         if step + 1 < depth:

time: 27.3 us -> 27.3 us (level)
  no operation moved by 1% of the time
where the time goes in v11:
time: 27.3 us; the launch traced here: 27 us
  blocking collectives  9.35 us (34%)
  starting transfers between devices  6.84 us (25%)
  Pallas kernels  5.86 us (21%)
  waiting for transfers between devices  3.55 us (13%)
  local copies, waits for them, and re-layouts  0.76 us (3%)
  other arithmetic  0.62 us (2%)
    all_to_all x1, blocking collectives, body(): terms = lax.all_to_all(terms, ('freq', 'half', 'shot'), 0, 0, tiled=True)  9.35 us
    all_to_all x1, starting transfers between devices, body(): recv = lax.all_to_all(send, ('half', 'freq'), 0, 0, tiled=True)  6.32 us
    all_to_all x1, waiting for transfers between devices, body(): recv = lax.all_to_all(send, ('half', 'freq'), 0, 0, tiled=True)  3.54 us
    pallas_call x1, Pallas kernels, body(): pl.pallas_call(functools.partial(source_kernel, taps, nref, depth, halves...  2.15 us
    pallas_call x1, Pallas kernels, body(): pl.pallas_call(functools.partial(send_kernel, groups, folded), out_shape=...  1.38 us
    pallas_call x1, Pallas kernels, body(): pl.pallas_call(functools.partial(migrate_kernel, (groups, halves, copies,...  1.27 us
    pallas_call x1, Pallas kernels, body(): pl.pallas_call(functools.partial(prepare_kernel, groups), out_shape=[jax....  1.06 us
    unnamed x8, local copies, waits for them, and re-layouts  0.63 us
  transfers between devices with their start and end apart: 2, of which 1 were waited for; matrix products, arithmetic and copies ran while one was open for 0% of the time, Pallas kernels for 13%

profile of v11, /device:TPU:0, one launch (start us, length us, event | category | flops | bytes accessed | tf_op | source)
XLA Modules:
  0.0 27.0 jit_solution(13200723889488631838)
XLA Ops:
  0.0 0.0 copy-start
  0.0 1.1 %prepare.1 = (bf16[32,512]{1,0:T(8,128)(2,1)S(1)}, s32[8,128]{1,0:T(8,128)S(1)}, f32[8,128]{1,0:T(8,128)S(1)}, bf16[4,32,128]{2,1,0:T(8,128)(2,1)S(1)}) custom-call(s32[4,6]{1,0:T(4,128)} %plan_hbm.1, s32[4]{0:T(128)} %counts_hbm.1, f32[2,256]{1,0:T(2,128)} %bitcast.8, s32[2,32,128]{2,1,0:T(8,128)} %class_hbm.3, bf16[2,32,128]{2,1,0:T(8,128)(2,1)} %pattern_hbm.3), custom_call_target="tpu_custom_call" | custom-call | flops 3000000000 | bytes 4000000 | tf_op jit(solution)/shard_map/prepare/pallas_call | solution.py:311
  1.1 0.0 copy-start.2
  1.1 0.0 copy-start.1
  1.1 0.5 %collective-permute-start = (bf16[4,32,128]{2,1,0:T(8,128)(2,1)S(1)}, bf16[4,32,128]{2,1,0:T(8,128)(2,1)S(1)}, u32[]{:S(2)}, u32[]{:S(2)}) collective-permute-start(bf16[4,32,128]{2,1,0:T(8,128)(2,1)S(1)} %get-tuple-element.15), channel_id=1, source_target_pairs={{1,0},{0,1},{3,2},{2,3},{5,4},{4,5},{7,6},{6,7},{9,8},{8,9},{11,10... | collective-permute-start | bytes 98312 | tf_op jit(solution)/shard_map/ppermute | solution.py:285
  1.6 0.0 copy-done
  1.6 1.4 %send_blocks.1 = bf16[2,4,48,128]{3,2,1,0:T(8,128)(2,1)} custom-call(bf16[32,512]{1,0:T(8,128)(2,1)S(1)} %get-tuple-element.12.dft_ref, bf16[2,1024,512]{2,1,0:T(8,128)(2,1)S(1)} %bitcast.6), custom_call_target="tpu_custom_call" | custom-call | tf_op jit(solution)/shard_map/send_blocks/pallas_call | solution.py:334
  3.0 6.3 %all-to-all-start = ((bf16[8,48,128]{2,1,0:T(8,128)(2,1)}), bf16[8,48,128]{2,1,0:T(8,128)(2,1)S(1)}, u32[]{:S(2)}, u32[]{:S(2)}) async-start(bf16[8,48,128]{2,1,0:T(8,128)(2,1)} %bitcast.2), calls=%async_computation | async-start | bytes 196608 | tf_op jit(solution)/shard_map/all_to_all | solution.py:345
  9.3 0.0 copy-done.2
  9.3 0.1 reshape.14.filt_ref
  9.5 0.0 collective-permute-done.refs_0_
  9.5 0.0 copy-start.3
  9.5 0.6 %copy-done.3 = bf16[4,32,128]{2,1,0:T(8,128)(2,1)} copy-done((bf16[4,32,128]{2,1,0:T(8,128)(2,1)}, bf16[4,32,128]{2,1,0:T(8,128)(2,1)S(1)}, u32[]{:S(2)}) %copy-start.3) | copy-done | bytes 32792
  10.1 0.0 copy-done.1
  10.1 2.1 %source_fields.1 = (bf16[3,1664,256]{2,1,0:T(8,128)(2,1)S(1)}, f32[2,128,128]{2,1,0:T(8,128)S(1)}, f32[2,3,128,128]{3,2,1,0:T(8,128)S(1)}) custom-call(s32[8,128]{1,0:T(8,128)S(1)} %get-tuple-element.13.own_ref, f32[8,128]{1,0:T(8,128)S(1)} %get-tuple-element.14.wave_ref, bf16[676,256]{1,0:T(8,128)(2,1)S(1)} %reshape.14.filt_ref, f32[1,64]{1,0:T(1,128)} %bitcast.9, ...), custom_call_target="tpu_custom_call" | custom-call | flops 4000000000 | bytes 10000000 | tf_op jit(solution)/shard_map/source_fields/pallas_call | solution.py:355
  12.3 3.5 %all-to-all-done.recv_ref = bf16[8,48,128]{2,1,0:T(8,128)(2,1)S(1)} async-done(((bf16[8,48,128]{2,1,0:T(8,128)(2,1)}), bf16[8,48,128]{2,1,0:T(8,128)(2,1)S(1)}, u32[]{:S(2)}, u32[]{:S(2)}) %all-to-all-start) | async-done | bytes 98336 | tf_op jit(solution)/shard_map/all_to_all | solution.py:345
  15.8 1.3 %migrate.1 = bf16[16,16,128]{2,1,0:T(8,128)(2,1)S(1)} custom-call(bf16[8,48,128]{2,1,0:T(8,128)(2,1)S(1)} %all-to-all-done.recv_ref, bf16[3,1664,256]{2,1,0:T(8,128)(2,1)S(1)} %get-tuple-element.16.band_ref, f32[2,128,128]{2,1,0:T(8,128)S(1)} %get-tuple-element.17.blend_ref, f32[2,3,128,128]{3,2,1,0:T(8,128)S(1)} %get-tuple-element.18.source_ref), custom_call_target="tpu_custom_call" | custom-call | tf_op jit(solution)/shard_map/migrate/pallas_call | solution.py:382
  17.1 9.3 %all_to_all.10 = bf16[16,16,128]{2,1,0:T(8,128)(2,1)S(1)} all-to-all(bf16[16,16,128]{2,1,0:T(8,128)(2,1)S(1)} %migrate.1), channel_id=1, replica_groups=mesh['group'=2,'freq'=4,'shot'=2,'half'=2] {'freq','half','shot'}, dimensions={0} | all-to-all | bytes 131072 | tf_op jit(solution)/shard_map/all_to_all | solution.py:395
  26.4 0.6 %convert_reduce_fusion = f32[16,128]{1,0:T(8,128)} fusion(bf16[16,16,128]{2,1,0:T(8,128)(2,1)S(1)} %all_to_all.10), kind=kLoop, calls=%fused_computation | loop fusion | flops 63488 | bytes 73728 | tf_op jit(solution)/shard_map/reduce_sum | solution.py:396
Async XLA Ops:
  0.0 1.6 %copy-start = (bf16[2,32,32,512]{3,2,1,0:T(8,128)(2,1)S(1)}, bf16[2,32,32,512]{3,2,1,0:T(8,128)(2,1)}, u32[]{:S(2)}) copy-start(bf16[2,32,32,512]{3,2,1,0:T(8,128)(2,1)} %param.8) | copy-start | bytes 6291460
  1.1 8.3 %copy-start.2 = (bf16[2,2,13,13,256]{4,1,3,2,0:T(2,128)(2,1)S(1)}, bf16[2,2,13,13,256]{4,1,3,2,0:T(2,128)(2,1)}, u32[]{:S(2)}) copy-start(bf16[2,2,13,13,256]{4,1,3,2,0:T(2,128)(2,1)} %param.11) | copy-start | bytes 1038340
  1.1 9.0 %copy-start.1 = (bf16[2,32,128]{2,1,0:T(8,128)(2,1)S(1)}, bf16[2,32,128]{2,1,0:T(8,128)(2,1)}, u32[]{:S(2)}) copy-start(bf16[2,32,128]{2,1,0:T(8,128)(2,1)} %pattern_hbm.3) | copy-start | bytes 49156
  1.1 8.4 %collective-permute-start = (bf16[4,32,128]{2,1,0:T(8,128)(2,1)S(1)}, bf16[4,32,128]{2,1,0:T(8,128)(2,1)S(1)}, u32[]{:S(2)}, u32[]{:S(2)}) collective-permute-start(bf16[4,32,128]{2,1,0:T(8,128)(2,1)S(1)} %get-tuple-element.15), channel_id=1, source_target_pairs={{1,0},{0,1},{3,2},{2,3},{5,4},{4,5},{7,6},{6,7},{9,8},{8,9},{11,10... | collective-permute-start | bytes 98312 | tf_op jit(solution)/shard_map/ppermute | solution.py:285
  3.0 12.8 %all-to-all-start = ((bf16[8,48,128]{2,1,0:T(8,128)(2,1)}), bf16[8,48,128]{2,1,0:T(8,128)(2,1)S(1)}, u32[]{:S(2)}, u32[]{:S(2)}) async-start(bf16[8,48,128]{2,1,0:T(8,128)(2,1)} %bitcast.2), calls=%async_computation | async-start | bytes 196608 | tf_op jit(solution)/shard_map/all_to_all | solution.py:345
  9.5 0.6 %copy-start.3 = (bf16[4,32,128]{2,1,0:T(8,128)(2,1)}, bf16[4,32,128]{2,1,0:T(8,128)(2,1)S(1)}, u32[]{:S(2)}) copy-start(bf16[4,32,128]{2,1,0:T(8,128)(2,1)S(1)} %collective-permute-done.refs_0_) | copy-start | bytes 98308
